TPU v7x, 256 devices: a whole 4x4x8 slice. The times are simulated.
256 devices in a mesh: tm: 64 (over z, x, core), det: 4 (over y).
Axes of the slice: x: 4, y: 4, z: 8, core: 2. Of those that a mesh axis runs over, the one named last changes fastest.
Arguments:
- strain: float32 [4, 65536], P('det', 'tm'), may hold values from -6 to 6
- decay_rate: float32 [8192], replicated, may hold values from 7.6293945e-07 to 0.0333333333
- frequency: float32 [8192], replicated, may hold values from 0.03 to 1.5
- gain: float32 [2, 8192], replicated, may hold values from -0.06455711 to 0.06455711
- member: int32 [8192], replicated, may hold values from 0 to 8191, each once
- sky_delay: int32 [64, 4], replicated, may hold values from 0 to 127
- antenna: float32 [64, 2, 4], replicated, may hold values from -2.1 to 2.1
Outputs:
- peak: float32 [32, 65536], P('det', 'tm')
Inputs may be any that keep to these rules, and one draw needn't show every extreme that they name: `member`: a permutation of the 8192 pool filters.
All inputs are finite; a program needn't handle non-finite values.
Results may differ from a plain program's by a relative error of at most 0.0027.
Values sent between devices are 32-bit elements; how exact they have to be, the bound alone decides.
No kernel may reach another device: no remote copies, remote signals or barrier semaphores. Data moves between devices by JAX's collectives and lax.ppermute only.
A program may use at most 64 MiB of HBM per device.

v0:
```python
import jax
import jax.numpy as jnp
from jax import lax
from jax.sharding import PartitionSpec as P

FILT = 256
SKY = 64
DELAY = 128


HIGHEST = lax.Precision.HIGHEST


def passed_along(value, axis, steps):
    count = lax.axis_size(axis)
    initial, last = (max(0, -steps), min(count, count - steps))
    return lax.ppermute(value, axis, [(source, source + steps) for source in range(initial, last)])


def plain_powers(decay_rows, angle_rows, exponent_count):
    exponents = jnp.arange(exponent_count, dtype=jnp.float32)
    magnitude = jnp.exp(-decay_rows[..., None] * exponents)
    phase_angle = angle_rows[..., None] * exponents
    return (magnitude * jnp.cos(phase_angle), magnitude * jnp.sin(phase_angle))


def block_powers(step_real, step_imag, block_count):
    position = jnp.arange(block_count, dtype=jnp.int32)
    result_real = jnp.ones(step_real.shape + (block_count,), jnp.float32)
    result_imag = jnp.zeros(step_real.shape + (block_count,), jnp.float32)
    base_real = step_real[..., None]
    base_imag = step_imag[..., None]
    for bit_place in range((block_count - 1).bit_length()):
        chosen = position >> bit_place & 1 == 1
        updated_real = result_real * base_real - result_imag * base_imag
        updated_imag = result_real * base_imag + result_imag * base_real
        result_real = jnp.where(chosen, updated_real, result_real)
        result_imag = jnp.where(chosen, updated_imag, result_imag)
        base_real, base_imag = (
            base_real * base_real - base_imag * base_imag,
            2.0 * base_real * base_imag,
        )
    return (result_real, result_imag)


def local_filter(blocks, decay_rows, angle_rows, gain_real, gain_imag):
    block_width = blocks.shape[-1]
    power_real, power_imag = plain_powers(decay_rows, angle_rows, block_width + 1)
    scaled_real = gain_real[..., None] * power_real - gain_imag[..., None] * power_imag
    scaled_imag = gain_real[..., None] * power_imag + gain_imag[..., None] * power_real
    kernel_real = jnp.sum(scaled_real[..., :block_width], axis=1)
    kernel_imag = jnp.sum(scaled_imag[..., :block_width], axis=1)
    lag_matrix = jnp.arange(block_width)[:, None] - jnp.arange(block_width)[None, :]
    lag_index = jnp.clip(lag_matrix, 0, block_width - 1)
    causal = lag_matrix >= 0
    toeplitz_real = jnp.where(causal, kernel_real[:, lag_index], 0.0)
    toeplitz_imag = jnp.where(causal, kernel_imag[:, lag_index], 0.0)
    direct_real = jnp.einsum("gts,dms->gdmt", toeplitz_real, blocks, precision=HIGHEST)
    direct_imag = jnp.einsum("gts,dms->gdmt", toeplitz_imag, blocks, precision=HIGHEST)
    tail_real = scaled_real[..., block_width - 1 :: -1]
    tail_imag = scaled_imag[..., block_width - 1 :: -1]
    ends_real = jnp.einsum("gks,dms->gkdm", tail_real, blocks, precision=HIGHEST)
    ends_imag = jnp.einsum("gks,dms->gkdm", tail_imag, blocks, precision=HIGHEST)
    step_real = power_real[..., block_width]
    step_imag = power_imag[..., block_width]

    def advance(carried, element):
        state_real, state_imag = carried
        new_real = (
            step_real[..., None] * state_real - step_imag[..., None] * state_imag + element[0]
        )
        new_imag = (
            step_real[..., None] * state_imag + step_imag[..., None] * state_real + element[1]
        )
        return ((new_real, new_imag), (state_real, state_imag))

    empty_state = jnp.zeros(ends_real.shape[:-1], jnp.float32)
    final_state, start_state = lax.scan(
        advance,
        (empty_state, empty_state),
        (jnp.moveaxis(ends_real, -1, 0), jnp.moveaxis(ends_imag, -1, 0)),
    )
    lead_real = power_real[..., 1:]
    lead_imag = power_imag[..., 1:]
    output_real = (
        direct_real
        + jnp.einsum("gkt,mgkd->gdmt", lead_real, start_state[0], precision=HIGHEST)
        - jnp.einsum("gkt,mgkd->gdmt", lead_imag, start_state[1], precision=HIGHEST)
    )
    output_imag = (
        direct_imag
        + jnp.einsum("gkt,mgkd->gdmt", lead_real, start_state[1], precision=HIGHEST)
        + jnp.einsum("gkt,mgkd->gdmt", lead_imag, start_state[0], precision=HIGHEST)
    )
    shape_out = output_real.shape[:2] + (output_real.shape[2] * output_real.shape[3],)
    block_count = blocks.shape[1]
    span_real, span_imag = block_powers(step_real, step_imag, block_count)
    window_real = (
        span_real[..., block_count - 1] * step_real - span_imag[..., block_count - 1] * step_imag
    )
    window_imag = (
        span_real[..., block_count - 1] * step_imag + span_imag[..., block_count - 1] * step_real
    )
    return (
        output_real.reshape(shape_out),
        output_imag.reshape(shape_out),
        final_state[0],
        final_state[1],
        window_real,
        window_imag,
    )


def carry_terms(decay_rows, angle_rows, carry_real, carry_imag, block_width, block_count):
    power_real, power_imag = plain_powers(decay_rows, angle_rows, block_width + 1)
    span_real, span_imag = block_powers(
        power_real[..., block_width], power_imag[..., block_width], block_count
    )
    entry_real = (
        span_real[..., None, :] * carry_real[..., None]
        - span_imag[..., None, :] * carry_imag[..., None]
    )
    entry_imag = (
        span_real[..., None, :] * carry_imag[..., None]
        + span_imag[..., None, :] * carry_real[..., None]
    )
    lead_real = power_real[..., 1:]
    lead_imag = power_imag[..., 1:]
    correction_real = jnp.einsum(
        "gkt,gkdm->gdmt", lead_real, entry_real, precision=HIGHEST
    ) - jnp.einsum("gkt,gkdm->gdmt", lead_imag, entry_imag, precision=HIGHEST)
    correction_imag = jnp.einsum(
        "gkt,gkdm->gdmt", lead_real, entry_imag, precision=HIGHEST
    ) + jnp.einsum("gkt,gkdm->gdmt", lead_imag, entry_real, precision=HIGHEST)
    shape_out = correction_real.shape[:2] + (block_count * block_width,)
    return (correction_real.reshape(shape_out), correction_imag.reshape(shape_out))


def sky_peak(padded_real, padded_imag, sky_delay, antenna, length):
    detectors = padded_real.shape[1]

    def eight_skies(group_turn, running_max):
        for inner_sky in range(8):
            sky_index = group_turn * 8 + inner_sky
            totals = [jnp.zeros(running_max.shape, jnp.float32) for slot_index in range(4)]
            for detector in range(detectors):
                offset = sky_delay[sky_index, detector]
                piece_real = lax.dynamic_slice_in_dim(padded_real[:, detector], offset, length, 1)
                piece_imag = lax.dynamic_slice_in_dim(padded_imag[:, detector], offset, length, 1)
                for polarization in range(2):
                    weight = antenna[sky_index, polarization, detector]
                    totals[2 * polarization] = totals[2 * polarization] + weight * piece_real
                    totals[2 * polarization + 1] = (
                        totals[2 * polarization + 1] + weight * piece_imag
                    )
            energy = (
                totals[0] * totals[0]
                + totals[1] * totals[1]
                + totals[2] * totals[2]
                + totals[3] * totals[3]
            )
            running_max = jnp.maximum(running_max, energy)
        return running_max

    initial = jnp.zeros((padded_real.shape[0], length), jnp.float32)
    return lax.fori_loop(0, SKY // 8, eight_skies, initial)


def shards(strain, decay_rate, frequency, gain, member, sky_delay, antenna):
    length = strain.shape[1]
    block_width = min(128, length)
    block_count = length // block_width
    templates = member.shape[0] // FILT
    member_table = member.reshape(templates, FILT)
    row_count = member_table.shape[0]
    detector_count = strain.shape[0]
    blocks = strain.reshape(detector_count, block_count, block_width)
    grouped = member_table.reshape(row_count // 8, 8, FILT)
    decay_rows = decay_rate[grouped]
    angle_rows = frequency[grouped]
    gain_real = gain[0][grouped]
    gain_imag = gain[1][grouped]

    def first_pass(group_params):
        return local_filter(
            blocks, group_params[0], group_params[1], group_params[2], group_params[3]
        )

    output_real, output_imag, final_real, final_imag, window_real, window_imag = lax.map(
        first_pass, (decay_rows, angle_rows, gain_real, gain_imag)
    )

    def pass_once(step_number, carried):
        moved_real = (
            window_real[..., None] * carried[0] - window_imag[..., None] * carried[1] + final_real
        )
        moved_imag = (
            window_real[..., None] * carried[1] + window_imag[..., None] * carried[0] + final_imag
        )
        shifted = passed_along(jnp.stack((moved_real, moved_imag)), "tm", 1)
        return (shifted[0], shifted[1])

    no_state = jnp.zeros(final_real.shape, jnp.float32)
    carry_real, carry_imag = lax.fori_loop(
        0, lax.axis_size("tm") - 1, pass_once, (no_state, no_state)
    )

    def second_pass(group_params):
        return carry_terms(
            group_params[0],
            group_params[1],
            group_params[2],
            group_params[3],
            block_width,
            block_count,
        )

    correction_real, correction_imag = lax.map(
        second_pass, (decay_rows, angle_rows, carry_real, carry_imag)
    )
    snr_real = (output_real + correction_real).reshape(row_count, detector_count, length)
    snr_imag = (output_imag + correction_imag).reshape(row_count, detector_count, length)
    stacked = jnp.stack((snr_real, snr_imag), axis=2)
    regrouped = lax.all_to_all(stacked, "det", split_axis=0, concat_axis=1, tiled=True)
    ahead_rows = passed_along(regrouped[..., :DELAY], "tm", -1)
    extended = jnp.concatenate((regrouped, ahead_rows), axis=-1)
    return sky_peak(extended[:, :, 0], extended[:, :, 1], sky_delay, antenna, length)


def solution(mesh):
    in_specs = (P("det", "tm"), P(), P(), P(), P(), P(), P())
    out_specs = P("det", "tm")
    return jax.shard_map(shards, mesh=mesh, in_specs=in_specs, out_specs=out_specs, check_vma=False)
```

profile of v0, /device:TPU:103, one launch (start us, length us, event | category | flops | bytes accessed | tf_op | source)
XLA Modules:
  0.0 2333.4 jit_solution(17481677812566158196)
XLA Ops:
  1.8 45.5 %gather_fusion.2 = f32[8192]{0:T(1024)S(1)} fusion(f32[8192]{0:T(1024)S(1)} %bitcast.558, s32[8192]{0:T(1024)S(1)} %broadcast_clamp_fusion), kind=kCustom, calls=%fused_computation.2 | custom fusion | bytes 98304 | tf_op jit(solution)/shard_map/gather | solution.py:181
  47.4 45.5 %gather_fusion.5 = f32[8192]{0:T(1024)S(1)} fusion(f32[8192]{0:T(1024)S(1)} %bitcast.557, s32[8192]{0:T(1024)S(1)} %broadcast_clamp_fusion), kind=kCustom, calls=%fused_computation.5 | custom fusion | bytes 98304 | tf_op jit(solution)/shard_map/gather | solution.py:182
  93.0 45.5 %gather_fusion.3 = f32[8192]{0:T(1024)S(1)} fusion(f32[8192]{0:T(1024)S(1)} %copy-done, s32[8192]{0:T(1024)S(1)} %broadcast_clamp_fusion), kind=kCustom, calls=%fused_computation.3 | custom fusion | bytes 98304 | tf_op jit(solution)/shard_map/gather | solution.py:179
  139.3 45.5 %gather_fusion.4 = f32[8192]{0:T(1024)S(1)} fusion(f32[8192]{0:T(1024)S(1)} %copy-done.1, s32[8192]{0:T(1024)S(1)} %broadcast_clamp_fusion), kind=kCustom, calls=%fused_computation.4 | custom fusion | bytes 98304 | tf_op jit(solution)/shard_map/gather | solution.py:180
  186.2 672.7 %while.78 = (s32[]{:T(128)}, f32[4,8,1,1024]{3,1,2,0:T(8,128)}, f32[4,8,1,1024]{3,1,2,0:T(8,128)}, f32[4,8,256,1]{2,3,1,0:T(1,128)S(1)}, f32[4,8,256,1]{2,3,1,0:...) while((s32[]{:T(128)}, f32[4,8,1,1024]{3,1,2,0:T(8,128)}, ...), condition=%wide.region_5.6_spmd, body=%wide.region_0.5_spmd.sunk | while | flops 179982416 | bytes 28714056 | solution.py:189
  186.3 7.6 cosine_multiply_fusion.3
  224.6 54.4 %gather_fusion.1 = f32[16384,8]{1,0:T(8,128)} fusion(f32[8,128]{0,1:T(8,128)S(1)} %copy.78, s32[16384]{0:T(1024)S(1)} %fusion.118), kind=kCustom, calls=%fused_computation.clone.1 | custom fusion | bytes 1114112 | tf_op jit(solution)/shard_map/while/body/eval_jaxpr/gather | solution.py:56
  288.0 54.4 %gather_fusion = f32[16384,8]{1,0:T(8,128)} fusion(f32[8,128]{0,1:T(8,128)S(1)} %copy.74, s32[16384]{0:T(1024)S(1)} %fusion.118), kind=kCustom, calls=%fused_computation.1.clone.1 | custom fusion | bytes 1114112 | tf_op jit(solution)/shard_map/while/body/eval_jaxpr/gather | solution.py:57
  352.1 7.6 cosine_multiply_fusion.3
  390.4 54.4 %gather_fusion.1 = f32[16384,8]{1,0:T(8,128)} fusion(f32[8,128]{0,1:T(8,128)S(1)} %copy.78, s32[16384]{0:T(1024)S(1)} %fusion.118), kind=kCustom, calls=%fused_computation.clone.1 | custom fusion | bytes 1114112 | tf_op jit(solution)/shard_map/while/body/eval_jaxpr/gather | solution.py:56
  453.9 54.4 %gather_fusion = f32[16384,8]{1,0:T(8,128)} fusion(f32[8,128]{0,1:T(8,128)S(1)} %copy.74, s32[16384]{0:T(1024)S(1)} %fusion.118), kind=kCustom, calls=%fused_computation.1.clone.1 | custom fusion | bytes 1114112 | tf_op jit(solution)/shard_map/while/body/eval_jaxpr/gather | solution.py:57
  518.0 7.6 cosine_multiply_fusion.3
  556.3 54.4 %gather_fusion.1 = f32[16384,8]{1,0:T(8,128)} fusion(f32[8,128]{0,1:T(8,128)S(1)} %copy.78, s32[16384]{0:T(1024)S(1)} %fusion.118), kind=kCustom, calls=%fused_computation.clone.1 | custom fusion | bytes 1114112 | tf_op jit(solution)/shard_map/while/body/eval_jaxpr/gather | solution.py:56
  619.7 54.4 %gather_fusion = f32[16384,8]{1,0:T(8,128)} fusion(f32[8,128]{0,1:T(8,128)S(1)} %copy.74, s32[16384]{0:T(1024)S(1)} %fusion.118), kind=kCustom, calls=%fused_computation.1.clone.1 | custom fusion | bytes 1114112 | tf_op jit(solution)/shard_map/while/body/eval_jaxpr/gather | solution.py:57
  683.8 7.6 cosine_multiply_fusion.3
  722.1 54.4 %gather_fusion.1 = f32[16384,8]{1,0:T(8,128)} fusion(f32[8,128]{0,1:T(8,128)S(1)} %copy.78, s32[16384]{0:T(1024)S(1)} %fusion.118), kind=kCustom, calls=%fused_computation.clone.1 | custom fusion | bytes 1114112 | tf_op jit(solution)/shard_map/while/body/eval_jaxpr/gather | solution.py:56
  785.6 54.4 %gather_fusion = f32[16384,8]{1,0:T(8,128)} fusion(f32[8,128]{0,1:T(8,128)S(1)} %copy.74, s32[16384]{0:T(1024)S(1)} %fusion.118), kind=kCustom, calls=%fused_computation.1.clone.1 | custom fusion | bytes 1114112 | tf_op jit(solution)/shard_map/while/body/eval_jaxpr/gather | solution.py:57
  858.9 569.4 %while.79 = (s32[]{:T(128)}, f32[4,8,256,1]{2,3,1,0:T(1,128)S(1)}, f32[4,8,256,1]{2,3,1,0:T(1,128)S(1)}, f32[4,8,256]{2,1,0:T(8,128)S(1)}, f32[4,8,256]{2,1,0:T(...) while((s32[]{:T(128)}, f32[4,8,256,1]{2,3,1,0:T(1,128)S(1)}, ...), condition=%wide.region_7.8_spmd, body=%wide.region_6.7_spmd.sunk | while | flops 81922 | bytes 786557 | solution.py:204
  1428.3 58.6 %while.80 = (s32[]{:T(128)}, f32[4,8,1,1024]{3,1,2,0:T(8,128)S(1)}, f32[4,8,1,1024]{3,1,2,0:T(8,128)S(1)}, f32[4,8,256]{2,1,0:T(8,128)S(1)}, f32[4,8,256]{2,1,0:...) while((s32[]{:T(128)}, f32[4,8,1,1024]{3,1,2,0:T(8,128)S(1)}, ...), condition=%wide.region_9.10_spmd, body=%wide.region_8.9_spmd.sunk | while | flops 103143496 | bytes 11473585 | solution.py:218
  1428.4 7.6 sine_multiply_fusion.3
  1443.0 7.6 sine_multiply_fusion.3
  1487.6 9.5 all_to_all.18
  1499.2 8.7 collective-permute-done.1
  1507.9 824.6 %while.81 = (s32[]{:T(128)}, f32[8,1024]{1,0:T(8,128)S(1)}, f32[64,2,4]{0,2,1:T(4,128)S(1)}, f32[8,4,1152]{2,0,1:T(8,128)S(1)}, s32[64,4]{0,1:T(4,128)S(1)}, /*i...) while((s32[]{:T(128)}, f32[8,1024]{1,0:T(8,128)S(1)}, ...), condition=%wide.region_11.12_spmd.clone, body=%wide.region_10.11_spmd.clone.sunk | while | flops 2367619 | bytes 2755407 | solution.py:166
  1570.1 40.9 %bitcast_maximum_fusion.9 = f32[8,1024]{1,0:T(8,128)S(1)} fusion(f32[8,1024]{1,0:T(8,128)S(1)} %get-tuple-element.1454, f32[8,1,1152]{2,0,1:T(8,128)S(1)} %get-tuple-element.1183, s32[]{:T(128)S(6)} %select_n.985, f32[8,1,1152]{2,0,1:T(8,128)S(1)} %get-tuple-element.1185, s32[]{:T(128)S(6)} %select_n.986, f32[8,1,1152]{2,0,1:T(8,128)S(1)} %get-tuple-element.1187, ...), kind=kLoop, calls=%fused_computation.17.clone.1 | loop fusion | flops 2367488 | bytes 2163073 | tf_op jit(solution)/shard_map/while/body/eval_jaxpr/max | solution.py:162
  1673.2 40.9 %bitcast_maximum_fusion.9 = f32[8,1024]{1,0:T(8,128)S(1)} fusion(f32[8,1024]{1,0:T(8,128)S(1)} %get-tuple-element.1454, f32[8,1,1152]{2,0,1:T(8,128)S(1)} %get-tuple-element.1183, s32[]{:T(128)S(6)} %select_n.985, f32[8,1,1152]{2,0,1:T(8,128)S(1)} %get-tuple-element.1185, s32[]{:T(128)S(6)} %select_n.986, f32[8,1,1152]{2,0,1:T(8,128)S(1)} %get-tuple-element.1187, ...), kind=kLoop, calls=%fused_computation.17.clone.1 | loop fusion | flops 2367488 | bytes 2163073 | tf_op jit(solution)/shard_map/while/body/eval_jaxpr/max | solution.py:162
  1776.2 40.9 %bitcast_maximum_fusion.9 = f32[8,1024]{1,0:T(8,128)S(1)} fusion(f32[8,1024]{1,0:T(8,128)S(1)} %get-tuple-element.1454, f32[8,1,1152]{2,0,1:T(8,128)S(1)} %get-tuple-element.1183, s32[]{:T(128)S(6)} %select_n.985, f32[8,1,1152]{2,0,1:T(8,128)S(1)} %get-tuple-element.1185, s32[]{:T(128)S(6)} %select_n.986, f32[8,1,1152]{2,0,1:T(8,128)S(1)} %get-tuple-element.1187, ...), kind=kLoop, calls=%fused_computation.17.clone.1 | loop fusion | flops 2367488 | bytes 2163073 | tf_op jit(solution)/shard_map/while/body/eval_jaxpr/max | solution.py:162
  1879.3 40.9 %bitcast_maximum_fusion.9 = f32[8,1024]{1,0:T(8,128)S(1)} fusion(f32[8,1024]{1,0:T(8,128)S(1)} %get-tuple-element.1454, f32[8,1,1152]{2,0,1:T(8,128)S(1)} %get-tuple-element.1183, s32[]{:T(128)S(6)} %select_n.985, f32[8,1,1152]{2,0,1:T(8,128)S(1)} %get-tuple-element.1185, s32[]{:T(128)S(6)} %select_n.986, f32[8,1,1152]{2,0,1:T(8,128)S(1)} %get-tuple-element.1187, ...), kind=kLoop, calls=%fused_computation.17.clone.1 | loop fusion | flops 2367488 | bytes 2163073 | tf_op jit(solution)/shard_map/while/body/eval_jaxpr/max | solution.py:162
  1982.4 40.9 %bitcast_maximum_fusion.9 = f32[8,1024]{1,0:T(8,128)S(1)} fusion(f32[8,1024]{1,0:T(8,128)S(1)} %get-tuple-element.1454, f32[8,1,1152]{2,0,1:T(8,128)S(1)} %get-tuple-element.1183, s32[]{:T(128)S(6)} %select_n.985, f32[8,1,1152]{2,0,1:T(8,128)S(1)} %get-tuple-element.1185, s32[]{:T(128)S(6)} %select_n.986, f32[8,1,1152]{2,0,1:T(8,128)S(1)} %get-tuple-element.1187, ...), kind=kLoop, calls=%fused_computation.17.clone.1 | loop fusion | flops 2367488 | bytes 2163073 | tf_op jit(solution)/shard_map/while/body/eval_jaxpr/max | solution.py:162
  2085.5 40.9 %bitcast_maximum_fusion.9 = f32[8,1024]{1,0:T(8,128)S(1)} fusion(f32[8,1024]{1,0:T(8,128)S(1)} %get-tuple-element.1454, f32[8,1,1152]{2,0,1:T(8,128)S(1)} %get-tuple-element.1183, s32[]{:T(128)S(6)} %select_n.985, f32[8,1,1152]{2,0,1:T(8,128)S(1)} %get-tuple-element.1185, s32[]{:T(128)S(6)} %select_n.986, f32[8,1,1152]{2,0,1:T(8,128)S(1)} %get-tuple-element.1187, ...), kind=kLoop, calls=%fused_computation.17.clone.1 | loop fusion | flops 2367488 | bytes 2163073 | tf_op jit(solution)/shard_map/while/body/eval_jaxpr/max | solution.py:162
  2188.5 40.9 %bitcast_maximum_fusion.9 = f32[8,1024]{1,0:T(8,128)S(1)} fusion(f32[8,1024]{1,0:T(8,128)S(1)} %get-tuple-element.1454, f32[8,1,1152]{2,0,1:T(8,128)S(1)} %get-tuple-element.1183, s32[]{:T(128)S(6)} %select_n.985, f32[8,1,1152]{2,0,1:T(8,128)S(1)} %get-tuple-element.1185, s32[]{:T(128)S(6)} %select_n.986, f32[8,1,1152]{2,0,1:T(8,128)S(1)} %get-tuple-element.1187, ...), kind=kLoop, calls=%fused_computation.17.clone.1 | loop fusion | flops 2367488 | bytes 2163073 | tf_op jit(solution)/shard_map/while/body/eval_jaxpr/max | solution.py:162
  2291.6 40.9 %bitcast_maximum_fusion.9 = f32[8,1024]{1,0:T(8,128)S(1)} fusion(f32[8,1024]{1,0:T(8,128)S(1)} %get-tuple-element.1454, f32[8,1,1152]{2,0,1:T(8,128)S(1)} %get-tuple-element.1183, s32[]{:T(128)S(6)} %select_n.985, f32[8,1,1152]{2,0,1:T(8,128)S(1)} %get-tuple-element.1185, s32[]{:T(128)S(6)} %select_n.986, f32[8,1,1152]{2,0,1:T(8,128)S(1)} %get-tuple-element.1187, ...), kind=kLoop, calls=%fused_computation.17.clone.1 | loop fusion | flops 2367488 | bytes 2163073 | tf_op jit(solution)/shard_map/while/body/eval_jaxpr/max | solution.py:162
  (758 shorter events, 836.1 us)
Async XLA Ops:
  865.8 8.9 collective-permute-start
  874.9 8.9 collective-permute-start
  884.0 8.9 collective-permute-start
  893.0 8.9 collective-permute-start
  902.1 8.9 collective-permute-start
  911.2 8.9 collective-permute-start
  920.3 8.9 collective-permute-start
  929.3 8.9 collective-permute-start
  938.4 8.9 collective-permute-start
  947.5 8.9 collective-permute-start
  956.6 8.9 collective-permute-start
  965.6 8.9 collective-permute-start
  974.7 8.9 collective-permute-start
  983.8 8.9 collective-permute-start
  992.9 8.9 collective-permute-start
  1001.9 8.9 collective-permute-start
  1011.0 8.9 collective-permute-start
  1020.1 8.9 collective-permute-start
  1029.2 8.9 collective-permute-start
  1038.2 8.9 collective-permute-start
  1047.3 8.9 collective-permute-start
  1056.4 8.9 collective-permute-start
  1065.5 8.9 collective-permute-start
  1074.5 8.9 collective-permute-start
  1083.6 8.9 collective-permute-start
  1092.7 8.9 collective-permute-start
  1147.1 8.9 collective-permute-start
  1201.6 8.9 collective-permute-start
  1256.0 8.9 collective-permute-start
  1319.6 8.9 collective-permute-start
  1374.0 8.9 collective-permute-start
  1497.3 10.6 collective-permute-start.1
  (64 other events, 774.8 us)
where the time goes:
time: 2350 us; the launch traced here: 2330 us
  local copies, waits for them, and re-layouts  758 us (32%)
  loops' own time  495 us (21%)
  starting transfers between devices  478 us (20%)
  other arithmetic  444 us (19%)
  waiting for transfers between devices  91.2 us (4%)
  matrix products  57.9 us (2%)
    another operation x1, loops' own time, sky_peak(): return lax.fori_loop(0, SKY // 8, eight_skies, initial)  481 us
    ppermute x64, starting transfers between devices, passed_along(): lax.ppermute(value, axis, [(source, source + steps) for source in range(i...  478 us
    max x8, other arithmetic, eight_skies(): running_max = jnp.maximum(running_max, energy)  327 us
    gather x8, local copies, waits for them, and re-layouts, local_filter(): toeplitz_real = jnp.where(causal, kernel_real[:, lag_index], 0.0)  238 us
    gather x8, local copies, waits for them, and re-layouts, local_filter(): toeplitz_imag = jnp.where(causal, kernel_imag[:, lag_index], 0.0)  238 us
    ppermute x64, waiting for transfers between devices, passed_along(): lax.ppermute(value, axis, [(source, source + steps) for source in range(i...  91.2 us
    mul x8, other arithmetic, plain_powers(): return (magnitude * jnp.cos(phase_angle), magnitude * jnp.sin(phase_angle))  61.1 us
  transfers between devices with their start and end apart: 64, of which 64 were waited for; matrix products, arithmetic and copies ran while one was open for 0% of the time, Pallas kernels for 0%

commit v1 on v0

v1 whole, which is shorter than its diff:
```python
import math

import jax
import jax.numpy as jnp
import numpy as np
from jax import lax
from jax.experimental import pallas as pl
from jax.experimental.pallas import tpu as pltpu
from jax.sharding import Mesh, PartitionSpec as P

FILT = 256
SKY = 64
WIDE = 8 * FILT
F32, BF16 = jnp.float32, jnp.bfloat16

TURN = 1.0 / (2.0 * math.pi)
TURN_HEAD = math.floor(TURN * 2**14) / 2**14
TURN_TAIL = TURN - TURN_HEAD

ROW_128, ROW_256, ROW_1024, ROW_8192 = 7, 8, 10, 13
ROW_GAIN, ROW_LEAD, ROWS = 16, 17, 24

VMEM_LIMIT = 56 * 2**20


def taylor(first, start, count):
    return [
        first * (-1) ** k * math.pi ** (2 * k + start) / math.factorial(2 * k + start)
        for k in range(count)
    ]


SINE, COSINE = taylor(1.0, 1, 8), taylor(1.0, 0, 9)


def horner(coefficients, square):
    total = jnp.full(square.shape, coefficients[-1], F32)
    for c in coefficients[-2::-1]:
        total = total * square + c
    return total


def cmul(ar, ai, br, bi):
    return ar * br - ai * bi, ar * bi + ai * br


def halves(x):
    head = x.astype(BF16)
    return head, (x - head.astype(F32)).astype(BF16)


def dot(a, b, contract_b=0):
    return lax.dot_general(
        a, b, (((1,), (contract_b,)), ((), ())), preferred_element_type=F32
    )


def dot3(a_head, a_tail, b_head, b_tail, contract_b=0):
    rows = a_head.shape[0]
    both = dot(jnp.concatenate([a_head, a_tail], axis=0), b_head, contract_b)
    return both[:rows] + both[rows:] + dot(a_head, b_tail, contract_b)


def prepare_kernel(
    place, strain, decay, frequency, gain, member, flip,
    sent, pr_head, pr_tail, pi_head, pi_tail, row_re, row_im, wr, wi, vr, vi,
    par,
):
    zi, xc, det = place[0], place[1], place[2]

    x = strain[...]
    head = x.astype(BF16)
    rest = x - head.astype(F32)
    middle = rest.astype(BF16)
    tail = (rest - middle.astype(F32)).astype(BF16)
    turned = dot(head, flip[...]) + (dot(middle, flip[...]) + dot(tail, flip[...]))
    for r in range(8):
        for p in range(32):
            sent[p, r : r + 1, :] = turned[7 - r : 8 - r, :]

    for half in range(2):
        index = member[pl.ds(pl.multiple_of(16 * det + 8 * half, 8), 8), :]
        high, low = index >> 7, index & 127

        def one_row(r, carried):
            hit = high == r
            values = (
                decay[pl.ds(r, 1), :],
                frequency[pl.ds(r, 1), :],
                gain[0, pl.ds(r, 1), :],
                gain[1, pl.ds(r, 1), :],
            )
            return tuple(
                jnp.where(
                    hit,
                    jnp.take_along_axis(jnp.broadcast_to(v, (8, 128)), low, axis=1),
                    c,
                )
                for v, c in zip(values, carried)
            )

        nothing = jnp.zeros((8, 128), F32)
        found = lax.fori_loop(0, 64, one_row, (nothing,) * 4, unroll=8)
        for k in range(4):
            par[k, 8 * half : 8 * half + 8, :] = found[k]

    power = jnp.left_shift(1, lax.broadcasted_iota(jnp.int32, (16, 128), 0)).astype(F32)
    place8 = lax.broadcasted_iota(jnp.int32, (8, 128), 0)
    ahead_z = zi - 1 - place8
    ahead_x = (xc + 7 - place8) & 7

    def choose(exponent, rows, re, im):
        out_re = jnp.ones((8, 128), F32)
        out_im = jnp.zeros((8, 128), F32)
        for bit, row in enumerate(rows):
            new_re, new_im = cmul(out_re, out_im, re[row : row + 1], im[row : row + 1])
            on = (exponent >> bit) & 1 == 1
            out_re = jnp.where(on, new_re, out_re)
            out_im = jnp.where(on, new_im, out_im)
        return out_re, out_im

    def one_chunk(c, _):
        lanes = pl.ds(pl.multiple_of(c * 128, 128), 128)
        f = par[1, pl.ds(c, 1), :]
        f_head = jnp.floor(f * 2048.0) * (1.0 / 2048.0)
        f_tail = f - f_head
        first = power * (f_head * TURN_HEAD)
        second = power * (f_head * TURN_TAIL + f_tail * TURN)
        turn = (first - jnp.floor(first + 0.5)) + (second - jnp.floor(second + 0.5))
        turn = turn - jnp.floor(turn + 0.5)
        square = turn * turn
        sine = turn * horner(SINE, square)
        cosine = horner(COSINE, square)
        size = jnp.exp(-power * par[0, pl.ds(c, 1), :])
        re = size * (1.0 - 2.0 * sine * sine)
        im = size * (2.0 * sine * cosine)
        row_re[0:16, lanes] = re
        row_im[0:16, lanes] = im
        g_re, g_im = par[2, pl.ds(c, 1), :], par[3, pl.ds(c, 1), :]
        l_re, l_im = cmul(g_re, g_im, re[0:1], im[0:1])
        empty = jnp.zeros((6, 128), F32)
        row_re[16:24, lanes] = jnp.concatenate([g_re, l_re, empty], axis=0)
        row_im[16:24, lanes] = jnp.concatenate([g_im, l_im, empty], axis=0)
        w_re, w_im = choose(ahead_z, (13, 14, 15), re, im)
        wr[:, lanes] = jnp.where(ahead_z >= 0, w_re, 0.0)
        wi[:, lanes] = jnp.where(ahead_z >= 0, w_im, 0.0)
        vr[:, lanes], vi[:, lanes] = choose(ahead_x, (10, 11, 12), re, im)
        t_re, t_im = choose(place8, (0, 1, 2), re, im)
        for row in range(3, 8):
            n_re, n_im = cmul(t_re, t_im, re[row : row + 1], im[row : row + 1])
            t_re = jnp.concatenate([t_re, n_re], axis=0)
            t_im = jnp.concatenate([t_im, n_im], axis=0)
        pr_head[:, lanes], pr_tail[:, lanes] = halves(t_re)
        pi_head[:, lanes], pi_tail[:, lanes] = halves(t_im)
        return 0

    lax.fori_loop(0, WIDE // 128, one_chunk, 0)


def column_kernel(
    place, x, pr_head, pr_tail, pi_head, pi_tail, row_re, row_im, wr, wi,
    sent, lhs_head, lhs_tail,
):
    zi, xc = place[0], place[1]
    for q in range(4):
        rows = jnp.concatenate(
            [x[pl.ds(2 * q, 32, stride=8), :], x[pl.ds(2 * q + 1, 32, stride=8), :]],
            axis=1,
        )
        lhs_head[32 * q : 32 * q + 32, :], lhs_tail[32 * q : 32 * q + 32, :] = halves(rows)
    own = lax.broadcasted_iota(jnp.int32, (8, 256), 0) == zi

    def one_part(part, _):
        lanes = pl.ds(pl.multiple_of(part * 256, 256), 256)
        a_head, a_tail = lhs_head[...], lhs_tail[...]
        e_re = dot3(a_head, a_tail, pr_head[:, lanes], pr_tail[:, lanes])
        e_im = dot3(a_head, a_tail, pi_head[:, lanes], pi_tail[:, lanes])
        step_re = row_re[ROW_256 : ROW_256 + 1, lanes]
        step_im = row_im[ROW_256 : ROW_256 + 1, lanes]
        s_re, s_im = e_re[96:128], e_im[96:128]
        for q in (2, 1, 0):
            s_re, s_im = cmul(s_re, s_im, step_re, step_im)
            s_re = s_re + e_re[32 * q : 32 * q + 32]
            s_im = s_im + e_im[32 * q : 32 * q + 32]
        w_re, w_im = wr[:, lanes], wi[:, lanes]
        before_re, before_im, own_re, own_im = [], [], [], []
        for d in range(4):
            d_re, d_im = s_re[8 * d : 8 * d + 8], s_im[8 * d : 8 * d + 8]
            t_re, t_im = cmul(d_re, d_im, w_re, w_im)
            before_re.append(jnp.sum(t_re, axis=0, keepdims=True))
            before_im.append(jnp.sum(t_im, axis=0, keepdims=True))
            own_re.append(jnp.sum(jnp.where(own, d_re, 0.0), axis=0, keepdims=True))
            own_im.append(jnp.sum(jnp.where(own, d_im, 0.0), axis=0, keepdims=True))
        b_re, b_im, o_re, o_im = (
            jnp.concatenate(v, axis=0) for v in (before_re, before_im, own_re, own_im)
        )
        i_re, i_im = cmul(
            b_re, b_im,
            row_re[ROW_8192 : ROW_8192 + 1, lanes], row_im[ROW_8192 : ROW_8192 + 1, lanes],
        )
        without = jnp.concatenate([b_re, b_im], axis=0)
        within = jnp.concatenate([i_re + o_re, i_im + o_im], axis=0)
        for p in range(8):
            sent[p, :, lanes] = jnp.where(xc < p, within, without)
        return 0

    lax.fori_loop(0, WIDE // 256, one_part, 0)

    shard = jnp.where(xc == 0, zi + 1, zi)
    inside = shard < 8
    row = jnp.minimum(shard, 7) * 8 + 7
    halo = jnp.concatenate(
        [x[pl.ds(row + 64 * d, 1), :] for d in range(4)] + [jnp.zeros((4, 128), F32)],
        axis=0,
    )
    halo = jnp.where(inside, halo, 0.0)
    for p in range(8):
        sent[p, :, WIDE : WIDE + 128] = halo


def peak_kernel(
    place, delay, antenna, got, x, pr_head, pr_tail, pi_head, pi_tail, row_re, row_im, vr, vi, flip,
    out, blocks, e_re, e_im, s_re, s_im, snr, grouped, shifted,
):
    zi, xc = place[0], place[1]
    last = jnp.logical_and(zi == 7, xc == 7)

    for m in range(8):
        for d in range(4):
            blocks[4 * m + d : 4 * m + d + 1, :] = x[
                pl.ds(64 * d + 8 * zi + (7 - m), 1), :
            ]
    blocks[32:40, :] = got[(xc + 1) & 7, :, WIDE : WIDE + 128]
    x_head, x_tail = halves(blocks[...])
    n_head, n_tail = (dot(v, flip[...]).astype(BF16) for v in (x_head, x_tail))

    def one_part(part, _):
        lanes = pl.ds(pl.multiple_of(part * 256, 256), 256)
        a_head, a_tail = x_head[0:32], x_tail[0:32]
        l_re = dot3(a_head, a_tail, pr_head[0:128, lanes], pr_tail[0:128, lanes])
        l_im = dot3(a_head, a_tail, pi_head[0:128, lanes], pi_tail[0:128, lanes])
        q_re = jnp.zeros((4, 256), F32)
        q_im = jnp.zeros((4, 256), F32)
        for p in range(8):
            t_re, t_im = cmul(
                got[p, 0:4, lanes], got[p, 4:8, lanes],
                vr[p : p + 1, lanes], vi[p : p + 1, lanes],
            )
            q_re, q_im = q_re + t_re, q_im + t_im
        step_re = row_re[ROW_128 : ROW_128 + 1, lanes]
        step_im = row_im[ROW_128 : ROW_128 + 1, lanes]
        g_re = row_re[ROW_LEAD : ROW_LEAD + 1, lanes]
        g_im = row_im[ROW_LEAD : ROW_LEAD + 1, lanes]
        for m in range(9):
            t_re, t_im = cmul(q_re, q_im, g_re, g_im)
            if m == 8:
                t_re = jnp.where(last, 0.0, t_re)
                t_im = jnp.where(last, 0.0, t_im)
            s_re[4 * m : 4 * m + 4, lanes] = t_re
            s_im[4 * m : 4 * m + 4, lanes] = t_im
            if m < 8:
                q_re, q_im = cmul(q_re, q_im, step_re, step_im)
                q_re = q_re + l_re[4 * m : 4 * m + 4]
                q_im = q_im + l_im[4 * m : 4 * m + 4]
        s_re[36:40, lanes] = jnp.broadcast_to(row_re[ROW_GAIN : ROW_GAIN + 1, lanes], (4, 256))
        s_im[36:40, lanes] = jnp.broadcast_to(row_im[ROW_GAIN : ROW_GAIN + 1, lanes], (4, 256))

        both_head, both_tail = halves(jnp.concatenate([s_re[:, lanes], s_im[:, lanes]], axis=0))
        lead_head = jnp.concatenate([pr_head[0:128, lanes], pi_head[0:128, lanes]], axis=0)
        lead_tail = jnp.concatenate([pr_tail[0:128, lanes], pi_tail[0:128, lanes]], axis=0)
        full = dot3(both_head, both_tail, lead_head, lead_tail, 1)
        f_re = full[0:40, 0:128] - full[40:80, 128:256]
        f_im = full[0:40, 128:256] + full[40:80, 0:128]
        lag = lax.broadcasted_iota(jnp.int32, (128, 128), 1) - lax.broadcasted_iota(
            jnp.int32, (128, 128), 0
        )
        response = []
        for f in (f_re, f_im):
            spread = jnp.broadcast_to(f[36:37, :], (128, 128))
            rolled = pltpu.roll(spread, 0, 1, stride=1, stride_axis=0)
            response.append(jnp.where(lag >= 0, rolled, 0.0))
        r_head, r_tail = halves(jnp.concatenate(response, axis=1))
        direct = dot3(n_head, n_tail, r_head, r_tail)
        snr[0] = f_re + direct[:, 0:128]
        snr[1] = f_im + direct[:, 128:256]
        for c in range(2):
            for d in range(4):
                grouped[c, d, pl.ds(part, 9, stride=8), :] = snr[c, pl.ds(d, 9, stride=4), :]
        return 0

    grouped[:, :, 72:128, :] = jnp.zeros((2, 4, 56, 128), F32)
    lax.fori_loop(0, WIDE // 256, one_part, 0)

    early = lax.broadcasted_iota(jnp.int32, (64, 128), 1) < 64
    for c in range(2):
        for d in range(4):
            t = grouped[c, d].T
            top, low = t[0:64], t[64:128]
            ahead_top, ahead_low = pltpu.roll(top, 120, 1), pltpu.roll(low, 120, 1)
            shifted[c, d, 0:64, :] = jnp.where(early, top, pltpu.roll(low, 64, 1))
            shifted[c, d, 64:128, :] = jnp.where(early, low, pltpu.roll(top, 56, 1))
            shifted[c, d, 128:192, :] = jnp.where(early, ahead_top, pltpu.roll(low, 56, 1))

    def one_sky(s, best):
        total = [None] * 4
        for d in range(4):
            rows = pl.ds(delay[4 * s + d], 64)
            for c in range(2):
                piece = shifted[c, d, rows, :]
                for p in range(2):
                    term = antenna[8 * s + 4 * p + d] * piece
                    k = 2 * p + c
                    total[k] = term if total[k] is None else total[k] + term
        energy = (total[0] * total[0] + total[1] * total[1]) + (
            total[2] * total[2] + total[3] * total[3]
        )
        return jnp.maximum(best, energy)

    best = lax.fori_loop(0, SKY, one_sky, jnp.zeros((64, 128), F32), unroll=2)
    turned = best.T
    for m in range(8):
        out[:, 128 * m : 128 * m + 128] = jnp.concatenate(
            [turned[8 * m : 8 * m + 8], turned[64 + 8 * m : 72 + 8 * m]], axis=1
        )


def call(kernel, n_scalar, n_vector, shapes, scratch):
    scalar, vector = (pl.BlockSpec(memory_space=m) for m in (pltpu.SMEM, pltpu.VMEM))
    return pl.pallas_call(
        kernel,
        out_shape=[jax.ShapeDtypeStruct(*s) for s in shapes],
        in_specs=[scalar] * n_scalar + [vector] * n_vector,
        out_specs=[vector] * len(shapes),
        scratch_shapes=[pltpu.VMEM(*s) for s in scratch],
        compiler_params=pltpu.CompilerParams(vmem_limit_bytes=VMEM_LIMIT),
    )


def shards(strain, decay_rate, frequency, gain, member, sky_delay, antenna):
    plane = 2 * lax.axis_index("x") + lax.axis_index("core")
    place = jnp.stack([lax.axis_index("z"), plane, lax.axis_index("det")]).astype(jnp.int32)
    flip = jnp.asarray(np.eye(128, dtype=np.float32)[::-1], dtype=BF16)
    table = ((256, WIDE), BF16)
    rows = ((ROWS, WIDE), F32)
    eight = ((8, WIDE), F32)
    sent, prh, prt, pih, pit, rr, ri, wr, wi, vr, vi = call(
        prepare_kernel, 1, 6,
        [((32, 8, 128), F32), table, table, table, table, rows, rows, eight, eight, eight, eight],
        [((4, 16, 128), F32)],
    )(
        place, strain.reshape(8, 128), decay_rate.reshape(64, 128), frequency.reshape(64, 128),
        gain.reshape(2, 64, 128), member.reshape(64, 128), flip,
    )
    column = lax.all_to_all(sent, ("det", "z"), 0, 0, tiled=True).reshape(256, 128)
    (partial,) = call(
        column_kernel, 1, 9, [((8, 8, WIDE + 128), F32)], [((128, 256), BF16), ((128, 256), BF16)]
    )(place, column, prh, prt, pih, pit, rr, ri, wr, wi)
    got = lax.all_to_all(partial, ("x", "core"), 0, 0, tiled=True)
    (peak,) = call(
        peak_kernel, 3, 11, [((8, 1024), F32)],
        [
            ((40, 128), F32), ((32, WIDE), F32), ((32, WIDE), F32), ((40, WIDE), F32),
            ((40, WIDE), F32), ((2, 40, 128), F32), ((2, 4, 128, 128), F32),
            ((2, 4, 192, 128), F32),
        ],
    )(
        place, sky_delay.reshape(-1), antenna.reshape(-1),
        got, column, prh, prt, pih, pit, rr, ri, vr, vi, flip,
    )
    return peak


def solution(mesh):
    fine = Mesh(mesh.devices.reshape(8, 4, 2, 4), ("z", "x", "core", "det"))
    time = ("z", "x", "core")
    in_specs = (P("det", time), P(), P(), P(), P(), P(), P())
    return jax.shard_map(
        shards, mesh=fine, in_specs=in_specs, out_specs=P("det", time), check_vma=False
    )
```

time: 2350 us -> 65.6 us (0.03)
  the two profiles are of different devices: /device:TPU:103 before, /device:TPU:1 now
where the time goes in v1:
time: 65.6 us; the launch traced here: 65.2 us
  Pallas kernels  24.7 us (38%)
  blocking collectives  21.3 us (32%)
  waiting for transfers between devices  8.19 us (12%)
  starting transfers between devices  6.5 us (10%)
  local copies, waits for them, and re-layouts  3.9 us (6%)
  other arithmetic  0.66 us (1%)
    all_to_all x1, blocking collectives, shards(): lax.all_to_all(sent, ('det', 'z'), 0, 0, tiled=True).reshape(256, 128)  21.3 us
    pallas_call x1, Pallas kernels, shards(): call(peak_kernel, 3, 11, [((8, 1024), F32)], [((40, 128), F32), ((32, WID...  11.7 us
    all_to_all x1, waiting for transfers between devices, shards(): got = lax.all_to_all(partial, ('x', 'core'), 0, 0, tiled=True)  8.19 us
    pallas_call x1, Pallas kernels, shards(): call(prepare_kernel, 1, 6, [((32, 8, 128), F32), table, table, table, tab...  7.02 us
    all_to_all x1, starting transfers between devices, shards(): got = lax.all_to_all(partial, ('x', 'core'), 0, 0, tiled=True)  6.5 us
    pallas_call x1, Pallas kernels, shards(): call(column_kernel, 1, 9, [((8, 8, WIDE + 128), F32)], [((128, 256), BF16...  5.95 us
    unnamed x9, local copies, waits for them, and re-layouts  2.49 us
  transfers between devices with their start and end apart: 1, of which 1 were waited for; matrix products, arithmetic and copies ran while one was open for 2% of the time, Pallas kernels for 0%

profile of v1, /device:TPU:1, one launch (start us, length us, event | category | flops | bytes accessed | tf_op | source)
XLA Modules:
  0.0 65.2 jit_solution(2638316306088698157)
XLA Ops:
  0.0 1.5 %copy.13 = f32[1,2,64,128]{3,2,1,0:T(8,128)} copy(f32[1,2,64,128]{3,1,2,0:T(2,128)} %bitcast.15) | data formatting | bytes 131072
  1.5 0.7 %pad_add_fusion.place = s32[3]{0:T(128)} fusion(s32[1]{0:T(128)} %bitcast.2, s32[1]{0:T(128)} %bitcast.1, s32[1]{0:T(128)} %bitcast), kind=kLoop, calls=%fused_computation.1 | loop fusion | flops 6 | bytes 24 | tf_op jit(solution)/shard_map/stack | solution.py:341
  2.1 7.0 %shard_map.82 = (f32[32,8,128]{2,1,0:T(8,128)}, bf16[256,2048]{1,0:T(8,128)(2,1)}, bf16[256,2048]{1,0:T(8,128)(2,1)}, bf16[256,2048]{1,0:T(8,128)(2,1)}, bf16[25...) custom-call(s32[3]{0:T(128)} %pad_add_fusion.place, ...), custom_call_target="tpu_custom_call" | custom-call | tf_op jit(solution)/shard_map/pallas_call | solution.py:346
  9.2 21.3 %all_to_all.10 = f32[32,8,128]{2,1,0:T(8,128)} all-to-all(f32[32,8,128]{2,1,0:T(8,128)} %get-tuple-element.16), channel_id=1, replica_groups=mesh['z'=8,'x'=4,'core'=2,'det'=4] {'det','z'}, dimensions={0} | all-to-all | bytes 262144 | tf_op jit(solution)/shard_map/all_to_all | solution.py:354
  30.4 6.0 %shard_map.83 = f32[8,8,2176]{2,1,0:T(8,128)} custom-call(s32[3]{0:T(128)} %pad_add_fusion.place, f32[256,128]{1,0:T(8,128)} %bitcast.12, bf16[256,2048]{1,0:T(8,128)(2,1)} %get-tuple-element.17.pr_head, bf16[256,2048]{1,0:T(8,128)(2,1)} %get-tuple-element.18.pr_tail, bf16[256,2048]{1,0:T(8,128)(2,1)} %get-tuple-element.19.pi_head, ...), custom_call_target="tpu_custom_call" | custom-call | tf_op jit(solution)/shard_map/pallas_call | solution.py:355
  36.4 0.0 copy-start.1
  36.4 6.5 %all-to-all-start.1 = ((f32[8,8,2176]{2,1,0:T(8,128)}), f32[8,8,2176]{2,1,0:T(8,128)S(1)}, u32[]{:S(2)}, u32[]{:S(2)}) async-start(f32[8,8,2176]{2,1,0:T(8,128)} %shard_map.83), calls=%async_computation.1 | async-start | bytes 1114112 | tf_op jit(solution)/shard_map/all_to_all | solution.py:358
  42.9 0.0 copy-done.1
  42.9 0.1 copy.10
  43.0 0.0 copy-start.2
  43.0 0.7 %reshape.25.antenna = f32[512]{0:T(512)} reshape(f32[64,2,4]{2,1,0:T(2,128)S(1)} %copy.10) | data formatting | bytes 4096 | tf_op jit(solution)/shard_map/reshape | solution.py:367
  43.8 0.0 copy-done.2
  43.8 0.1 copy.9
  43.9 0.7 %reshape.24.delay = s32[256]{0:T(256)} reshape(s32[64,4]{1,0:T(8,128)S(1)} %copy.9) | data formatting | bytes 2048 | tf_op jit(solution)/shard_map/reshape | solution.py:367
  44.5 8.2 %all-to-all-done.1.got = f32[8,8,2176]{2,1,0:T(8,128)S(1)} async-done(((f32[8,8,2176]{2,1,0:T(8,128)}), f32[8,8,2176]{2,1,0:T(8,128)S(1)}, u32[]{:S(2)}, u32[]{:S(2)}) %all-to-all-start.1) | async-done | bytes 557088 | tf_op jit(solution)/shard_map/all_to_all | solution.py:358
  52.7 0.0 copy-start
  52.7 0.8 %copy-done = f32[8,8,2176]{2,1,0:T(8,128)} copy-done((f32[8,8,2176]{2,1,0:T(8,128)}, f32[8,8,2176]{2,1,0:T(8,128)S(1)}, u32[]{:S(2)}) %copy-start) | copy-done | bytes 557080
  53.5 11.7 %shard_map.84 = f32[8,1024]{1,0:T(8,128)} custom-call(s32[3]{0:T(128)} %pad_add_fusion.place, s32[256]{0:T(256)} %reshape.24.delay, f32[512]{0:T(512)} %reshape.25.antenna, f32[8,8,2176]{2,1,0:T(8,128)} %copy-done, f32[256,128]{1,0:T(8,128)} %bitcast.13, bf16[256,2048]{1,0:T(8,128)(2,1)} %get-tuple-element.17.pr_head, ...), custom_call_target="tpu_custom_call" | custom-call | tf_op jit(solution)/shard_map/pallas_call | solution.py:359
Async XLA Ops:
  36.4 6.5 %copy-start.1 = (f32[64,2,4]{0,2,1:T(4,128)S(1)}, f32[64,2,4]{0,2,1:T(4,128)}, u32[]{:S(2)}) copy-start(f32[64,2,4]{0,2,1:T(4,128)} %param.14) | copy-start | bytes 6148
  36.4 16.3 %all-to-all-start.1 = ((f32[8,8,2176]{2,1,0:T(8,128)}), f32[8,8,2176]{2,1,0:T(8,128)S(1)}, u32[]{:S(2)}, u32[]{:S(2)}) async-start(f32[8,8,2176]{2,1,0:T(8,128)} %shard_map.83), calls=%async_computation.1 | async-start | bytes 1114112 | tf_op jit(solution)/shard_map/all_to_all | solution.py:358
  43.0 0.7 %copy-start.2 = (s32[64,4]{0,1:T(4,128)S(1)}, s32[64,4]{0,1:T(4,128)}, u32[]{:S(2)}) copy-start(s32[64,4]{0,1:T(4,128)} %param.13) | copy-start | bytes 3076
  52.7 0.8 %copy-start = (f32[8,8,2176]{2,1,0:T(8,128)}, f32[8,8,2176]{2,1,0:T(8,128)S(1)}, u32[]{:S(2)}) copy-start(f32[8,8,2176]{2,1,0:T(8,128)S(1)} %all-to-all-done.1.got) | copy-start | bytes 1671172

commit v2 on v1

v2 whole, which is shorter than its diff:
```python
import math

import jax
import jax.numpy as jnp
import numpy as np
from jax import lax
from jax.experimental import pallas as pl
from jax.experimental.pallas import tpu as pltpu
from jax.sharding import Mesh, PartitionSpec as P

FILT = 256
SKY = 64
WIDE = 8 * FILT
F32, BF16 = jnp.float32, jnp.bfloat16

TURN = 1.0 / (2.0 * math.pi)
TURN_HEAD = math.floor(TURN * 2**14) / 2**14
TURN_TAIL = TURN - TURN_HEAD

ROW_128, ROW_8192, ROW_GAIN, ROW_LEAD = 0, 1, 2, 3

VMEM_LIMIT = 16 * 2**20
UNROLL = True


def taylor(first, start, count):
    return [
        first * (-1) ** k * math.pi ** (2 * k + start) / math.factorial(2 * k + start)
        for k in range(count)
    ]


SINE, COSINE = taylor(1.0, 1, 8), taylor(1.0, 0, 9)


def horner(coefficients, square):
    total = jnp.full(square.shape, coefficients[-1], F32)
    for c in coefficients[-2::-1]:
        total = total * square + c
    return total


def cmul(ar, ai, br, bi):
    return ar * br - ai * bi, ar * bi + ai * br


def halves(x):
    head = x.astype(BF16)
    return head, (x - head.astype(F32)).astype(BF16)


def dot(a, b, contract_b=0):
    return lax.dot_general(
        a, b, (((1,), (contract_b,)), ((), ())), preferred_element_type=F32
    )


def dot3(a_head, a_tail, b_head, b_tail, contract_b=0):
    rows = a_head.shape[0]
    both = dot(jnp.concatenate([a_head, a_tail], axis=0), b_head, contract_b)
    return both[:rows] + both[rows:] + dot(a_head, b_tail, contract_b)


def lead_tables(lanes, pr_head, pr_tail, pi_head, pi_tail):
    return (
        jnp.concatenate([pr_head[:, lanes], pi_head[:, lanes]], axis=0),
        jnp.concatenate([pr_tail[:, lanes], pi_tail[:, lanes]], axis=0),
    )


def prepare_kernel(
    place, decay, frequency, gain, member,
    pr_head, pr_tail, pi_head, pi_tail, row_re, row_im, wr, wi, vr, vi, response,
    par,
):
    zi, xc, det = place[0], place[1], place[2]

    index = [
        member[pl.ds(pl.multiple_of(16 * det + 8 * half, 8), 8), :] for half in range(2)
    ]
    high, low = [v >> 7 for v in index], [v & 127 for v in index]

    def one_row(r, carried):
        lanes = pl.ds(pl.multiple_of(r * 128, 128), 128)
        values = (
            decay[pl.ds(r, 1), :],
            frequency[pl.ds(r, 1), :],
            gain[0:1, lanes],
            gain[1:2, lanes],
        )
        spread = [jnp.broadcast_to(v, (8, 128)) for v in values]
        return tuple(
            jnp.where(
                high[h] == r,
                jnp.take_along_axis(spread[k], low[h], axis=1),
                carried[4 * h + k],
            )
            for h in range(2)
            for k in range(4)
        )

    nothing = jnp.zeros((8, 128), F32)
    found = lax.fori_loop(0, 64, one_row, (nothing,) * 8, unroll=8)
    for h in range(2):
        for k in range(4):
            par[k, 8 * h : 8 * h + 8, :] = found[4 * h + k]

    power = jnp.left_shift(1, lax.broadcasted_iota(jnp.int32, (16, 128), 0)).astype(F32)
    place8 = lax.broadcasted_iota(jnp.int32, (8, 128), 0)
    ahead_z = zi - 1 - place8
    ahead_x = (place8 + 7 - xc) & 7

    def choose(exponent, rows, re, im):
        out_re = jnp.ones((8, 128), F32)
        out_im = jnp.zeros((8, 128), F32)
        for bit, row in enumerate(rows):
            new_re, new_im = cmul(out_re, out_im, re[row : row + 1], im[row : row + 1])
            on = (exponent >> bit) & 1 == 1
            out_re = jnp.where(on, new_re, out_re)
            out_im = jnp.where(on, new_im, out_im)
        return out_re, out_im

    def one_chunk(c, _):
        lanes = pl.ds(pl.multiple_of(c * 128, 128), 128)
        f = par[1, pl.ds(c, 1), :]
        f_head = jnp.floor(f * 2048.0) * (1.0 / 2048.0)
        f_tail = f - f_head
        first = power * (f_head * TURN_HEAD)
        second = power * (f_head * TURN_TAIL + f_tail * TURN)
        turn = (first - jnp.floor(first + 0.5)) + (second - jnp.floor(second + 0.5))
        turn = turn - jnp.floor(turn + 0.5)
        square = turn * turn
        sine = turn * horner(SINE, square)
        cosine = horner(COSINE, square)
        size = jnp.exp(-power * par[0, pl.ds(c, 1), :])
        re = size * (1.0 - 2.0 * sine * sine)
        im = size * (2.0 * sine * cosine)
        g_re, g_im = par[2, pl.ds(c, 1), :], par[3, pl.ds(c, 1), :]
        l_re, l_im = cmul(g_re, g_im, re[0:1], im[0:1])
        empty = jnp.zeros((4, 128), F32)
        row_re[:, lanes] = jnp.concatenate([re[7:8], re[13:14], g_re, l_re, empty], axis=0)
        row_im[:, lanes] = jnp.concatenate([im[7:8], im[13:14], g_im, l_im, empty], axis=0)
        w_re, w_im = choose(ahead_z, (13, 14, 15), re, im)
        wr[:, lanes] = jnp.where(ahead_z >= 0, w_re, 0.0)
        wi[:, lanes] = jnp.where(ahead_z >= 0, w_im, 0.0)
        vr[:, lanes], vi[:, lanes] = choose(ahead_x, (10, 11, 12), re, im)
        t_re, t_im = choose(place8, (0, 1, 2), re, im)
        for row in range(3, 7):
            n_re, n_im = cmul(t_re, t_im, re[row : row + 1], im[row : row + 1])
            t_re = jnp.concatenate([t_re, n_re], axis=0)
            t_im = jnp.concatenate([t_im, n_im], axis=0)
        pr_head[:, lanes], pr_tail[:, lanes] = halves(t_re)
        pi_head[:, lanes], pi_tail[:, lanes] = halves(t_im)
        return 0

    lax.fori_loop(0, WIDE // 128, one_chunk, 0)

    for j in range(WIDE // FILT):
        lanes = slice(FILT * j, FILT * j + FILT)
        both_head, both_tail = halves(jnp.concatenate([row_re[:, lanes], row_im[:, lanes]], axis=0))
        full = dot3(both_head, both_tail, *lead_tables(lanes, pr_head, pr_tail, pi_head, pi_tail), 1)
        full_re = full[0:8, 0:128] - full[8:16, 128:256]
        full_im = full[0:8, 128:256] + full[8:16, 0:128]
        response[j : j + 1, :] = full_re[ROW_GAIN : ROW_GAIN + 1]
        response[8 + j : 9 + j, :] = full_im[ROW_GAIN : ROW_GAIN + 1]


def delayed(row):
    lag = lax.broadcasted_iota(jnp.int32, (128, 128), 1) - lax.broadcasted_iota(
        jnp.int32, (128, 128), 0
    )
    rolled = pltpu.roll(jnp.broadcast_to(row, (128, 128)), 0, 1, stride=1, stride_axis=0)
    return jnp.where(lag >= 0, rolled, 0.0)


def column_kernel(
    place, x, flip, pr_head, pr_tail, pi_head, pi_tail, row_re, row_im, wr, wi, vr, vi,
    sent, turned, lhs,
):
    zi, xc = place[0], place[1]
    turned[...] = dot(jnp.concatenate(halves(x[...]), axis=0), flip[...])
    for q in range(8):
        rows = [turned[pl.ds(256 * h + 7 - q, 32, stride=8), :].astype(BF16) for h in (0, 1, 0)]
        lhs[32 * q : 32 * q + 32, :] = jnp.concatenate(rows, axis=1)
    own = lax.broadcasted_iota(jnp.int32, (8, 256), 0) == zi

    def one_part(part, _):
        lanes = pl.ds(pl.multiple_of(part * 256, 256), 256)
        e_re, e_im = (
            dot(lhs[...], jnp.concatenate([head[:, lanes], head[:, lanes], tail[:, lanes]], axis=0))
            for head, tail in ((pr_head, pr_tail), (pi_head, pi_tail))
        )
        step_re = row_re[ROW_128 : ROW_128 + 1, lanes]
        step_im = row_im[ROW_128 : ROW_128 + 1, lanes]
        s_re, s_im = e_re[224:256], e_im[224:256]
        for q in range(6, -1, -1):
            s_re, s_im = cmul(s_re, s_im, step_re, step_im)
            s_re = s_re + e_re[32 * q : 32 * q + 32]
            s_im = s_im + e_im[32 * q : 32 * q + 32]
        w_re, w_im = wr[:, lanes], wi[:, lanes]
        before_re, before_im, own_re, own_im = [], [], [], []
        for d in range(4):
            d_re, d_im = s_re[8 * d : 8 * d + 8], s_im[8 * d : 8 * d + 8]
            t_re, t_im = cmul(d_re, d_im, w_re, w_im)
            before_re.append(jnp.sum(t_re, axis=0, keepdims=True))
            before_im.append(jnp.sum(t_im, axis=0, keepdims=True))
            own_re.append(jnp.sum(jnp.where(own, d_re, 0.0), axis=0, keepdims=True))
            own_im.append(jnp.sum(jnp.where(own, d_im, 0.0), axis=0, keepdims=True))
        b_re, b_im, o_re, o_im = (
            jnp.concatenate(v, axis=0) for v in (before_re, before_im, own_re, own_im)
        )
        i_re, i_im = cmul(
            b_re, b_im,
            row_re[ROW_8192 : ROW_8192 + 1, lanes], row_im[ROW_8192 : ROW_8192 + 1, lanes],
        )
        i_re, i_im = i_re + o_re, i_im + o_im
        for p in range(8):
            t_re, t_im = cmul(
                jnp.where(xc < p, i_re, b_re), jnp.where(xc < p, i_im, b_im),
                vr[p : p + 1, lanes], vi[p : p + 1, lanes],
            )
            sent[p, :, lanes] = jnp.concatenate([t_re, t_im], axis=0)
        return 0

    lax.fori_loop(0, WIDE // 256, one_part, 0, unroll=UNROLL)

    shard = jnp.where(xc == 0, zi + 1, zi)
    inside = shard < 8
    row = jnp.minimum(shard, 7) * 8
    halo = jnp.concatenate(
        [x[pl.ds(row + 64 * d, 1), :] for d in range(4)] + [jnp.zeros((4, 128), F32)],
        axis=0,
    )
    halo = jnp.where(inside, halo, 0.0)
    for p in range(8):
        sent[p, :, WIDE : WIDE + 128] = halo


def local_kernel(
    place, x, flip, pr_head, pr_tail, pi_head, pi_tail, response,
    e_re, e_im, direct, blocks,
):
    zi = place[0]
    for m in range(8):
        for d in range(4):
            row = 4 * m + d
            blocks[row : row + 1, :] = x[pl.ds(64 * d + 8 * zi + m, 1), :]
    n_head, n_tail = halves(blocks[...])
    x_head, x_tail = (dot(v, flip[...]).astype(BF16) for v in (n_head, n_tail))
    for j in range(WIDE // FILT):
        lanes = slice(FILT * j, FILT * j + FILT)
        e_re[:, lanes] = dot3(x_head, x_tail, pr_head[:, lanes], pr_tail[:, lanes])
        e_im[:, lanes] = dot3(x_head, x_tail, pi_head[:, lanes], pi_tail[:, lanes])
        matrices = [delayed(response[row : row + 1, :]) for row in (j, 8 + j)]
        direct[j] = dot3(n_head, n_tail, *halves(jnp.concatenate(matrices, axis=1)))


def peak_kernel(
    place, delay, antenna, got, e_re, e_im, direct, response,
    pr_head, pr_tail, pi_head, pi_tail, row_re, row_im,
    out, s_re, s_im, snr, grouped, shifted,
):
    zi, xc = place[0], place[1]
    last = jnp.logical_and(zi == 7, xc == 7)
    halo = got[(xc + 1) & 7, :, WIDE : WIDE + 128]
    h_head, h_tail = halves(response[...])

    def one_part(part, _):
        lanes = pl.ds(pl.multiple_of(part * FILT, FILT), FILT)
        l_re, l_im = e_re[:, lanes], e_im[:, lanes]
        q = got[0, :, lanes]
        for p in range(1, 8):
            q = q + got[p, :, lanes]
        q_re, q_im = q[0:4], q[4:8]
        step_re = row_re[ROW_128 : ROW_128 + 1, lanes]
        step_im = row_im[ROW_128 : ROW_128 + 1, lanes]
        g_re = row_re[ROW_LEAD : ROW_LEAD + 1, lanes]
        g_im = row_im[ROW_LEAD : ROW_LEAD + 1, lanes]
        for m in range(9):
            t_re, t_im = cmul(q_re, q_im, g_re, g_im)
            if m == 8:
                t_re = jnp.where(last, 0.0, t_re)
                t_im = jnp.where(last, 0.0, t_im)
            s_re[4 * m : 4 * m + 4, lanes] = t_re
            s_im[4 * m : 4 * m + 4, lanes] = t_im
            if m < 8:
                q_re, q_im = cmul(q_re, q_im, step_re, step_im)
                q_re = q_re + l_re[4 * m : 4 * m + 4]
                q_im = q_im + l_im[4 * m : 4 * m + 4]
        both_head, both_tail = halves(jnp.concatenate([s_re[:, lanes], s_im[:, lanes]], axis=0))
        full = dot3(both_head, both_tail, *lead_tables(lanes, pr_head, pr_tail, pi_head, pi_tail), 1)
        own = direct[part]
        f_re = full[0:40, 0:128] - full[40:80, 128:256]
        f_im = full[0:40, 128:256] + full[40:80, 0:128]
        snr[0, 0:32, :], snr[0, 32:40, :] = f_re[0:32] + own[:, 0:128], f_re[32:40]
        snr[1, 0:32, :], snr[1, 32:40, :] = f_im[0:32] + own[:, 128:256], f_im[32:40]
        for c in range(2):
            for d in range(4):
                grouped[c, d, pl.ds(part, 9, stride=8), :] = snr[c, pl.ds(d, 9, stride=4), :]
        return 0

    grouped[:, :, 72:128, :] = jnp.zeros((2, 4, 56, 128), F32)
    s_re[36:40, :] = jnp.zeros((4, WIDE), F32)
    s_im[36:40, :] = jnp.zeros((4, WIDE), F32)
    lax.fori_loop(0, WIDE // 256, one_part, 0, unroll=UNROLL)

    for d in range(4):
        ahead = dot3(h_head, h_tail, *halves(delayed(halo[d : d + 1])))
        for c in range(2):
            grouped[c, d, 64:72, :] = grouped[c, d, 64:72, :] + ahead[8 * c : 8 * c + 8]

    early = lax.broadcasted_iota(jnp.int32, (64, 128), 1) < 64
    for c in range(2):
        for d in range(4):
            t = grouped[c, d].T
            top, low = t[0:64], t[64:128]
            ahead_top, ahead_low = pltpu.roll(top, 120, 1), pltpu.roll(low, 120, 1)
            shifted[c, d, 0:64, :] = jnp.where(early, top, pltpu.roll(low, 64, 1))
            shifted[c, d, 64:128, :] = jnp.where(early, low, pltpu.roll(top, 56, 1))
            shifted[c, d, 128:192, :] = jnp.where(early, ahead_top, pltpu.roll(low, 56, 1))

    def one_sky(s, best):
        total = [None] * 4
        for d in range(4):
            rows = pl.ds(delay[4 * s + d], 64)
            for c in range(2):
                piece = shifted[c, d, rows, :]
                for p in range(2):
                    term = antenna[8 * s + 4 * p + d] * piece
                    k = 2 * p + c
                    total[k] = term if total[k] is None else total[k] + term
        energy = (total[0] * total[0] + total[1] * total[1]) + (
            total[2] * total[2] + total[3] * total[3]
        )
        return jnp.maximum(best, energy)

    best = lax.fori_loop(0, SKY, one_sky, jnp.zeros((64, 128), F32), unroll=2)
    turned = best.T
    for m in range(8):
        out[:, 128 * m : 128 * m + 128] = jnp.concatenate(
            [turned[8 * m : 8 * m + 8], turned[64 + 8 * m : 72 + 8 * m]], axis=1
        )


def call(kernel, n_scalar, n_vector, shapes, scratch):
    scalar, vector = (pl.BlockSpec(memory_space=m) for m in (pltpu.SMEM, pltpu.VMEM))
    return pl.pallas_call(
        kernel,
        out_shape=[jax.ShapeDtypeStruct(*s) for s in shapes],
        in_specs=[scalar] * n_scalar + [vector] * n_vector,
        out_specs=[vector] * len(shapes),
        scratch_shapes=[pltpu.VMEM(*s) for s in scratch],
        compiler_params=pltpu.CompilerParams(vmem_limit_bytes=VMEM_LIMIT),
    )


TABLE, EIGHT = ((128, WIDE), BF16), ((8, WIDE), F32)
PREPARED = [TABLE] * 4 + [EIGHT] * 6 + [((16, 128), F32)]
LOCAL = [((32, WIDE), F32), ((32, WIDE), F32), ((8, 32, 256), F32)]


def prepare(*args):
    return call(prepare_kernel, 1, 4, PREPARED, [((4, 16, 128), F32)])(*args)


def of_column(*args):
    scratch = [((512, 128), F32), ((256, 384), BF16)]
    return call(column_kernel, 1, 12, [((8, 8, WIDE + 128), F32)], scratch)(*args)[0]


def of_device(*args):
    return call(local_kernel, 1, 7, LOCAL, [((32, 128), F32)])(*args)


def to_peak(*args):
    scratch = [
        ((40, WIDE), F32), ((40, WIDE), F32), ((2, 40, 128), F32), ((2, 4, 128, 128), F32),
        ((2, 4, 192, 128), F32),
    ]
    return call(peak_kernel, 3, 11, [((8, 1024), F32)], scratch)(*args)[0]


def shards(strain, decay_rate, frequency, gain, member, sky_delay, antenna):
    sent = jnp.broadcast_to(strain.reshape(1, 8, 128), (32, 8, 128))
    column = lax.all_to_all(sent, ("det", "z"), 0, 0, tiled=True).reshape(256, 128)
    plane = 2 * lax.axis_index("x") + lax.axis_index("core")
    place = jnp.stack([lax.axis_index("z"), plane, lax.axis_index("det")]).astype(jnp.int32)
    flip = jnp.asarray(np.eye(128, dtype=np.float32)[::-1], dtype=BF16)
    prh, prt, pih, pit, rr, ri, wr, wi, vr, vi, response = prepare(
        place, decay_rate.reshape(64, 128), frequency.reshape(64, 128), gain, member.reshape(64, 128)
    )
    partial = of_column(place, column, flip, prh, prt, pih, pit, rr, ri, wr, wi, vr, vi)
    got = lax.all_to_all(partial, ("x", "core"), 0, 0, tiled=True)
    e_re, e_im, direct = of_device(place, column, flip, prh, prt, pih, pit, response)
    return to_peak(
        place, sky_delay.reshape(-1), antenna.reshape(-1),
        got, e_re, e_im, direct, response, prh, prt, pih, pit, rr, ri,
    )


def solution(mesh):
    fine = Mesh(mesh.devices.reshape(8, 4, 2, 4), ("z", "x", "core", "det"))
    time = ("z", "x", "core")
    in_specs = (P("det", time), P(), P(), P(), P(), P(), P())
    return jax.shard_map(
        shards, mesh=fine, in_specs=in_specs, out_specs=P("det", time), check_vma=False
    )
```

time: 65.6 us -> 48.9 us (0.75)
  blocking collectives: 21.3 us -> 0 us
  starting transfers between devices: 6.5 us -> 18.7 us
  Pallas kernels: 24.7 us -> 14 us
  waiting for transfers between devices: 8.19 us -> 10.9 us
  local copies, waits for them, and re-layouts: 3.9 us -> 4.72 us
    all_to_all x1 -> x0, blocking collectives: 21.3 us -> none  [shards(): lax.all_to_all(sent, ('det', 'z'), 0, 0, tiled=True).reshape(256, 128)]
    all_to_all x0 -> x1, starting transfers between devices: none -> 12.2 us  [shards(): lax.all_to_all(sent, ('det', 'z'), 0, 0, tiled=True).reshape(256, 128)]
    pallas_call x3 -> x4, Pallas kernels: 24.7 us -> 14 us  [the longest x1 5.49 us: to_peak(): return call(peak_kernel, 3, 11, [((8, 1024), F32)], scratch)(*args)[0]]
    all_to_all x0 -> x1, waiting for transfers between devices: none -> 4.13 us  [shards(): lax.all_to_all(sent, ('det', 'z'), 0, 0, tiled=True).reshape(256, 128)]
    all_to_all x1, waiting for transfers between devices: 8.19 us -> 6.79 us  [shards(): got = lax.all_to_all(partial, ('x', 'core'), 0, 0, tiled=True)]
    broadcast_in_dim x0 -> x1, local copies, waits for them, and re-layouts: none -> 1.34 us  [shards(): sent = jnp.broadcast_to(strain.reshape(1, 8, 128), (32, 8, 128))]
    unnamed x9 -> x20, local copies, waits for them, and re-layouts: 2.49 us -> 3.14 us
  transfers between devices with their start and end apart: 1 -> 2, of which waited for: 1 -> 2; matrix products, arithmetic and copies ran while one was open for 2% -> 1% of each run, Pallas kernels for 0% -> 11%
where the time goes in v2:
time: 48.9 us; the launch traced here: 48.4 us
  starting transfers between devices  18.7 us (38%)
  Pallas kernels  14 us (29%)
  waiting for transfers between devices  10.9 us (22%)
  local copies, waits for them, and re-layouts  4.72 us (10%)
    all_to_all x1, starting transfers between devices, shards(): lax.all_to_all(sent, ('det', 'z'), 0, 0, tiled=True).reshape(256, 128)  12.2 us
    all_to_all x1, waiting for transfers between devices, shards(): got = lax.all_to_all(partial, ('x', 'core'), 0, 0, tiled=True)  6.79 us
    all_to_all x1, starting transfers between devices, shards(): got = lax.all_to_all(partial, ('x', 'core'), 0, 0, tiled=True)  6.5 us
    pallas_call x1, Pallas kernels, to_peak(): return call(peak_kernel, 3, 11, [((8, 1024), F32)], scratch)(*args)[0]  5.49 us
    pallas_call x1, Pallas kernels, prepare(): return call(prepare_kernel, 1, 4, PREPARED, [((4, 16, 128), F32)])(*args)  4.26 us
    all_to_all x1, waiting for transfers between devices, shards(): lax.all_to_all(sent, ('det', 'z'), 0, 0, tiled=True).reshape(256, 128)  4.13 us
    unnamed x20, local copies, waits for them, and re-layouts  3.14 us
    pallas_call x1, Pallas kernels, of_column(): call(column_kernel, 1, 12, [((8, 8, WIDE + 128), F32)], scratch)(*args)[0]  2.98 us
  transfers between devices with their start and end apart: 2, of which 2 were waited for; matrix products, arithmetic and copies ran while one was open for 1% of the time, Pallas kernels for 11%

profile of v2, /device:TPU:1, one launch (start us, length us, event | category | flops | bytes accessed | tf_op | source)
XLA Modules:
  0.0 48.4 jit_solution(12271226213513786501)
XLA Ops:
  0.0 1.3 %broadcast_in_dim.8 = f32[32,8,128]{2,1,0:T(8,128)} broadcast(f32[8,128]{1,0:T(8,128)} %bitcast.13), dimensions={1,2} | broadcast | bytes 135168 | tf_op jit(solution)/shard_map/broadcast_in_dim | solution.py:384
  1.3 0.0 copy-start.3
  1.3 0.0 copy-start.5
  1.3 0.0 copy-start.6
  1.4 12.2 %all-to-all-start = ((f32[32,8,128]{2,1,0:T(8,128)}), f32[32,8,128]{2,1,0:T(8,128)S(1)}, u32[]{:S(2)}, u32[]{:S(2)}) async-start(f32[32,8,128]{2,1,0:T(8,128)} %broadcast_in_dim.8), calls=%async_computation | async-start | bytes 262144 | tf_op jit(solution)/shard_map/all_to_all | solution.py:385
  13.5 0.0 copy-start.4
  13.5 0.1 pad_add_fusion.place
  13.6 0.0 copy-done.3
  13.6 0.0 copy-done.5
  13.6 0.0 copy-done.6
  13.6 0.7 %copy-done.4 = f32[8192]{0:T(1024)S(1)} copy-done((f32[8192]{0:T(1024)S(1)}, f32[8192]{0:T(1024)}, u32[]{:S(2)}) %copy-start.4) | copy-done | bytes 32792
  14.3 0.0 copy-start.2
  14.3 4.3 %shard_map.82 = (bf16[128,2048]{1,0:T(8,128)(2,1)S(1)}, bf16[128,2048]{1,0:T(8,128)(2,1)S(1)}, bf16[128,2048]{1,0:T(8,128)(2,1)S(1)}, bf16[128,2048]{1,0:T(8,128...) custom-call(s32[3]{0:T(128)S(1)} %pad_add_fusion.place, ...), custom_call_target="tpu_custom_call" | custom-call | tf_op jit(solution)/shard_map/pallas_call | solution.py:363
  18.6 4.1 %all-to-all-done = f32[32,8,128]{2,1,0:T(8,128)S(1)} async-done(((f32[32,8,128]{2,1,0:T(8,128)}), f32[32,8,128]{2,1,0:T(8,128)S(1)}, u32[]{:S(2)}, u32[]{:S(2)}) %all-to-all-start) | async-done | bytes 131104 | tf_op jit(solution)/shard_map/all_to_all | solution.py:385
  22.7 0.0 copy-done.2
  22.7 3.0 %shard_map.83 = f32[8,8,2176]{2,1,0:T(8,128)} custom-call(s32[3]{0:T(128)S(1)} %pad_add_fusion.place, f32[256,128]{1,0:T(8,128)S(1)} %bitcast.8, bf16[128,128]{1,0:T(8,128)(2,1)S(1)} %copy-done.2, bf16[128,2048]{1,0:T(8,128)(2,1)S(1)} %get-tuple-element.19.pr_head, bf16[128,2048]{1,0:T(8,128)(2,1)S(1)} %get-tuple-element.20.pr_tail, ...), custom_call_target="tpu_custom_call" | custom-call | tf_op jit(solution)/shard_map/pallas_call | solution.py:368
  25.7 0.0 copy-start.8
  25.7 6.5 %all-to-all-start.1 = ((f32[8,8,2176]{2,1,0:T(8,128)}), f32[8,8,2176]{2,1,0:T(8,128)S(1)}, u32[]{:S(2)}, u32[]{:S(2)}) async-start(f32[8,8,2176]{2,1,0:T(8,128)} %shard_map.83), calls=%async_computation.1 | async-start | bytes 1114112 | tf_op jit(solution)/shard_map/all_to_all | solution.py:393
  32.2 0.0 copy-done.8
  32.2 0.1 copy.9
  32.3 0.0 copy-start.7
  32.3 0.1 reshape.20.delay
  32.4 0.6 %copy-done.7 = f32[64,2,4]{0,2,1:T(4,128)S(1)} copy-done((f32[64,2,4]{0,2,1:T(4,128)S(1)}, f32[64,2,4]{0,2,1:T(4,128)}, u32[]{:S(2)}) %copy-start.7) | copy-done | bytes 2072
  33.0 0.1 copy.10
  33.1 0.1 reshape.21.antenna
  33.2 1.3 %shard_map.84 = (f32[32,2048]{1,0:T(8,128)S(1)}, f32[32,2048]{1,0:T(8,128)S(1)}, f32[8,32,256]{2,1,0:T(8,128)S(1)}) custom-call(s32[3]{0:T(128)S(1)} %pad_add_fusion.place, f32[256,128]{1,0:T(8,128)S(1)} %bitcast.9, bf16[128,128]{1,0:T(8,128)(2,1)S(1)} %copy-done.2, bf16[128,2048]{1,0:T(8,128)(2,1)S(1)} %get-tuple-element.19.pr_head, ...), custom_call_target="tpu_custom_call" | custom-call | tf_op jit(solution)/shard_map/pallas_call | solution.py:372
  34.5 0.0 copy-start
  34.5 0.7 %copy-done = f32[8,32,256]{2,1,0:T(8,128)} copy-done((f32[8,32,256]{2,1,0:T(8,128)}, f32[8,32,256]{2,1,0:T(8,128)S(1)}, u32[]{:S(2)}) %copy-start) | copy-done | bytes 262168
  35.2 6.8 %all-to-all-done.1.got = f32[8,8,2176]{2,1,0:T(8,128)S(1)} async-done(((f32[8,8,2176]{2,1,0:T(8,128)}), f32[8,8,2176]{2,1,0:T(8,128)S(1)}, u32[]{:S(2)}, u32[]{:S(2)}) %all-to-all-start.1) | async-done | bytes 557088 | tf_op jit(solution)/shard_map/all_to_all | solution.py:393
  42.0 0.0 copy-start.1
  42.0 0.9 %copy-done.1 = f32[8,32,256]{2,1,0:T(8,128)S(1)} copy-done((f32[8,32,256]{2,1,0:T(8,128)S(1)}, f32[8,32,256]{2,1,0:T(8,128)}, u32[]{:S(2)}) %copy-start.1) | copy-done | bytes 262168
  43.0 5.5 %shard_map.85 = f32[8,1024]{1,0:T(8,128)} custom-call(s32[3]{0:T(128)S(1)} %pad_add_fusion.place, s32[256]{0:T(256)S(1)} %reshape.20.delay, f32[512]{0:T(512)S(1)} %reshape.21.antenna, f32[8,8,2176]{2,1,0:T(8,128)S(1)} %all-to-all-done.1.got, f32[32,2048]{1,0:T(8,128)S(1)} %get-tuple-element.30.e_re, f32[32,2048]{1,0:T(8,128)S(1)} %get-tuple-element.31.e_im, ...), custom_call_target="tpu_custom_call" | custom-call | tf_op jit(solution)/shard_map/pallas_call | solution.py:380
Async XLA Ops:
  1.3 12.3 %copy-start.3 = (f32[2,8192]{1,0:T(2,128)S(1)}, f32[2,8192]{1,0:T(2,128)}, u32[]{:S(2)}) copy-start(f32[2,8192]{1,0:T(2,128)} %gain.1) | copy-start | bytes 196612
  1.3 12.3 %copy-start.5 = (f32[8192]{0:T(1024)S(1)}, f32[8192]{0:T(1024)}, u32[]{:S(2)}) copy-start(f32[8192]{0:T(1024)} %param.10) | copy-start | bytes 98308
  1.3 12.3 %copy-start.6 = (s32[8192]{0:T(1024)S(1)}, s32[8192]{0:T(1024)}, u32[]{:S(2)}) copy-start(s32[8192]{0:T(1024)} %param.12) | copy-start | bytes 98308
  1.4 21.3 %all-to-all-start = ((f32[32,8,128]{2,1,0:T(8,128)}), f32[32,8,128]{2,1,0:T(8,128)S(1)}, u32[]{:S(2)}, u32[]{:S(2)}) async-start(f32[32,8,128]{2,1,0:T(8,128)} %broadcast_in_dim.8), calls=%async_computation | async-start | bytes 262144 | tf_op jit(solution)/shard_map/all_to_all | solution.py:385
  13.5 0.8 %copy-start.4 = (f32[8192]{0:T(1024)S(1)}, f32[8192]{0:T(1024)}, u32[]{:S(2)}) copy-start(f32[8192]{0:T(1024)} %param.9) | copy-start | bytes 98308
  14.3 8.4 %copy-start.2 = (bf16[128,128]{1,0:T(8,128)(2,1)S(1)}, bf16[128,128]{1,0:T(8,128)(2,1)}, u32[]{:S(2)}) copy-start(bf16[128,128]{1,0:T(8,128)(2,1)} %constant.21.clone.flip) | copy-start | bytes 98308
  25.7 6.5 %copy-start.8 = (s32[64,4]{0,1:T(4,128)S(1)}, s32[64,4]{0,1:T(4,128)}, u32[]{:S(2)}) copy-start(s32[64,4]{0,1:T(4,128)} %param.13) | copy-start | bytes 3076
  25.7 16.3 %all-to-all-start.1 = ((f32[8,8,2176]{2,1,0:T(8,128)}), f32[8,8,2176]{2,1,0:T(8,128)S(1)}, u32[]{:S(2)}, u32[]{:S(2)}) async-start(f32[8,8,2176]{2,1,0:T(8,128)} %shard_map.83), calls=%async_computation.1 | async-start | bytes 1114112 | tf_op jit(solution)/shard_map/all_to_all | solution.py:393
  32.3 0.7 %copy-start.7 = (f32[64,2,4]{0,2,1:T(4,128)S(1)}, f32[64,2,4]{0,2,1:T(4,128)}, u32[]{:S(2)}) copy-start(f32[64,2,4]{0,2,1:T(4,128)} %param.14) | copy-start | bytes 6148
  34.5 0.7 %copy-start = (f32[8,32,256]{2,1,0:T(8,128)}, f32[8,32,256]{2,1,0:T(8,128)S(1)}, u32[]{:S(2)}) copy-start(f32[8,32,256]{2,1,0:T(8,128)S(1)} %get-tuple-element.32.direct) | copy-start | bytes 786436
  42.0 1.0 %copy-start.1 = (f32[8,32,256]{2,1,0:T(8,128)S(1)}, f32[8,32,256]{2,1,0:T(8,128)}, u32[]{:S(2)}) copy-start(f32[8,32,256]{2,1,0:T(8,128)} %copy-done) | copy-start | bytes 786436

commit v3 on v2

--- a/solution.py
+++ b/solution.py
@@ -108,7 +108,7 @@
     power = jnp.left_shift(1, lax.broadcasted_iota(jnp.int32, (16, 128), 0)).astype(F32)
     place8 = lax.broadcasted_iota(jnp.int32, (8, 128), 0)
     ahead_z = zi - 1 - place8
-    ahead_x = (place8 + 7 - xc) & 7
+    ahead_x = jnp.where(place8 < 4, 2 * place8 - 1, 2 * place8 + 2 * (xc & 1) - 10) & 7
 
     def choose(exponent, rows, re, im):
         out_re = jnp.ones((8, 128), F32)
@@ -174,8 +174,8 @@
 
 
 def column_kernel(
-    place, x, flip, pr_head, pr_tail, pi_head, pi_tail, row_re, row_im, wr, wi, vr, vi,
-    sent, turned, lhs,
+    place, x, flip, pr_head, pr_tail, pi_head, pi_tail, row_re, row_im, wr, wi,
+    states, turned, lhs,
 ):
     zi, xc = place[0], place[1]
     turned[...] = dot(jnp.concatenate(halves(x[...]), axis=0), flip[...])
@@ -213,13 +213,8 @@
             b_re, b_im,
             row_re[ROW_8192 : ROW_8192 + 1, lanes], row_im[ROW_8192 : ROW_8192 + 1, lanes],
         )
-        i_re, i_im = i_re + o_re, i_im + o_im
-        for p in range(8):
-            t_re, t_im = cmul(
-                jnp.where(xc < p, i_re, b_re), jnp.where(xc < p, i_im, b_im),
-                vr[p : p + 1, lanes], vi[p : p + 1, lanes],
-            )
-            sent[p, :, lanes] = jnp.concatenate([t_re, t_im], axis=0)
+        states[0, :, lanes] = jnp.concatenate([b_re, b_im], axis=0)
+        states[1, :, lanes] = jnp.concatenate([i_re + o_re, i_im + o_im], axis=0)
         return 0
 
     lax.fori_loop(0, WIDE // 256, one_part, 0, unroll=UNROLL)
@@ -232,13 +227,30 @@
         axis=0,
     )
     halo = jnp.where(inside, halo, 0.0)
-    for p in range(8):
-        sent[p, :, WIDE : WIDE + 128] = halo
+    for p in range(2):
+        states[p, :, WIDE : WIDE + 128] = halo
+
+
+def chip_kernel(place, mine, other, vr, vi, *sent):
+    x, core = place[1] >> 1, place[1] & 1
+    for k in range(4):
+        target = 2 * ((x + k) & 3) + core
+        for part in range(WIDE // 256):
+            lanes = slice(256 * part, 256 * part + 256)
+            total = None
+            for states, column, row in ((mine, 2 * x + core, k), (other, 2 * x + 1 - core, 4 + k)):
+                state = states[jnp.where(column < target, 1, 0), :, lanes]
+                term = cmul(
+                    state[0:4], state[4:8], vr[row : row + 1, lanes], vi[row : row + 1, lanes]
+                )
+                total = term if total is None else (total[0] + term[0], total[1] + term[1])
+            sent[k][:, lanes] = jnp.concatenate(total, axis=0)
+        sent[k][:, WIDE : WIDE + 128] = other[0, :, WIDE : WIDE + 128]
 
 
 def local_kernel(
-    place, x, flip, pr_head, pr_tail, pi_head, pi_tail, response,
-    e_re, e_im, direct, blocks,
+    place, x, flip, pr_head, pr_tail, pi_head, pi_tail, row_re, row_im, response,
+    local, blocks, s_all,
 ):
     zi = place[0]
     for m in range(8):
@@ -247,62 +259,67 @@
             blocks[row : row + 1, :] = x[pl.ds(64 * d + 8 * zi + m, 1), :]
     n_head, n_tail = halves(blocks[...])
     x_head, x_tail = (dot(v, flip[...]).astype(BF16) for v in (n_head, n_tail))
+    s_all[...] = jnp.zeros((80, WIDE), F32)
     for j in range(WIDE // FILT):
         lanes = slice(FILT * j, FILT * j + FILT)
-        e_re[:, lanes] = dot3(x_head, x_tail, pr_head[:, lanes], pr_tail[:, lanes])
-        e_im[:, lanes] = dot3(x_head, x_tail, pi_head[:, lanes], pi_tail[:, lanes])
-        matrices = [delayed(response[row : row + 1, :]) for row in (j, 8 + j)]
-        direct[j] = dot3(n_head, n_tail, *halves(jnp.concatenate(matrices, axis=1)))
-
-
-def peak_kernel(
-    place, delay, antenna, got, e_re, e_im, direct, response,
-    pr_head, pr_tail, pi_head, pi_tail, row_re, row_im,
-    out, s_re, s_im, snr, grouped, shifted,
-):
-    zi, xc = place[0], place[1]
-    last = jnp.logical_and(zi == 7, xc == 7)
-    halo = got[(xc + 1) & 7, :, WIDE : WIDE + 128]
-    h_head, h_tail = halves(response[...])
-
-    def one_part(part, _):
-        lanes = pl.ds(pl.multiple_of(part * FILT, FILT), FILT)
-        l_re, l_im = e_re[:, lanes], e_im[:, lanes]
-        q = got[0, :, lanes]
-        for p in range(1, 8):
-            q = q + got[p, :, lanes]
-        q_re, q_im = q[0:4], q[4:8]
-        step_re = row_re[ROW_128 : ROW_128 + 1, lanes]
-        step_im = row_im[ROW_128 : ROW_128 + 1, lanes]
-        g_re = row_re[ROW_LEAD : ROW_LEAD + 1, lanes]
-        g_im = row_im[ROW_LEAD : ROW_LEAD + 1, lanes]
-        for m in range(9):
-            t_re, t_im = cmul(q_re, q_im, g_re, g_im)
-            if m == 8:
-                t_re = jnp.where(last, 0.0, t_re)
-                t_im = jnp.where(last, 0.0, t_im)
-            s_re[4 * m : 4 * m + 4, lanes] = t_re
-            s_im[4 * m : 4 * m + 4, lanes] = t_im
+        l_re = dot3(x_head, x_tail, pr_head[:, lanes], pr_tail[:, lanes])
+        l_im = dot3(x_head, x_tail, pi_head[:, lanes], pi_tail[:, lanes])
+        g_re, g_im, step_re, step_im = (
+            v[row : row + 1, lanes] for row in (ROW_LEAD, ROW_128) for v in (row_re, row_im)
+        )
+        q_re, q_im = l_re[0:4], l_im[0:4]
+        for m in range(1, 9):
+            s_all[4 * m : 4 * m + 4, lanes], s_all[40 + 4 * m : 44 + 4 * m, lanes] = cmul(
+                q_re, q_im, g_re, g_im
+            )
             if m < 8:
                 q_re, q_im = cmul(q_re, q_im, step_re, step_im)
                 q_re = q_re + l_re[4 * m : 4 * m + 4]
                 q_im = q_im + l_im[4 * m : 4 * m + 4]
-        both_head, both_tail = halves(jnp.concatenate([s_re[:, lanes], s_im[:, lanes]], axis=0))
-        full = dot3(both_head, both_tail, *lead_tables(lanes, pr_head, pr_tail, pi_head, pi_tail), 1)
-        own = direct[part]
+        full = dot3(
+            *halves(s_all[:, lanes]), *lead_tables(lanes, pr_head, pr_tail, pi_head, pi_tail), 1
+        )
+        matrices = [delayed(response[row : row + 1, :]) for row in (j, 8 + j)]
+        own = dot3(n_head, n_tail, *halves(jnp.concatenate(matrices, axis=1)))
         f_re = full[0:40, 0:128] - full[40:80, 128:256]
         f_im = full[0:40, 128:256] + full[40:80, 0:128]
-        snr[0, 0:32, :], snr[0, 32:40, :] = f_re[0:32] + own[:, 0:128], f_re[32:40]
-        snr[1, 0:32, :], snr[1, 32:40, :] = f_im[0:32] + own[:, 128:256], f_im[32:40]
-        for c in range(2):
+        local[j, 0, 0:32, :], local[j, 0, 32:40, :] = f_re[0:32] + own[:, 0:128], f_re[32:40]
+        local[j, 1, 0:32, :], local[j, 1, 32:40, :] = f_im[0:32] + own[:, 128:256], f_im[32:40]
+
+
+def peak_kernel(
+    place, delay, antenna, got0, got1, got2, got3, local, response,
+    pr_head, pr_tail, pi_head, pi_tail, row_re, row_im,
+    out, s_all, snr, grouped, shifted,
+):
+    zi, xc = place[0], place[1]
+    keep = jnp.where(jnp.logical_and(zi == 7, xc == 7), 0.0, 1.0)
+    ahead_lanes = slice(WIDE, WIDE + 128)
+    halo = jnp.where((xc & 1) == 0, got0[:, ahead_lanes], got3[:, ahead_lanes])
+    h_head, h_tail = halves(response[...])
+    s_all[...] = jnp.zeros((80, WIDE), F32)
+    grouped[:, :, 72:128, :] = jnp.zeros((2, 4, 56, 128), F32)
+
+    for j in range(WIDE // FILT):
+        lanes = slice(FILT * j, FILT * j + FILT)
+        q = (got0[:, lanes] + got1[:, lanes]) + (got2[:, lanes] + got3[:, lanes])
+        g_re, g_im, step_re, step_im = (
+            v[row : row + 1, lanes] for row in (ROW_LEAD, ROW_128) for v in (row_re, row_im)
+        )
+        q_re, q_im = cmul(q[0:4], q[4:8], g_re, g_im)
+        for m in range(9):
+            s_all[4 * m : 4 * m + 4, lanes] = q_re
+            s_all[40 + 4 * m : 44 + 4 * m, lanes] = q_im
+            q_re, q_im = cmul(q_re, q_im, step_re, step_im)
+        full = dot3(
+            *halves(s_all[:, lanes]), *lead_tables(lanes, pr_head, pr_tail, pi_head, pi_tail), 1
+        )
+        f_re = full[0:40, 0:128] - full[40:80, 128:256] + local[j, 0]
+        f_im = full[0:40, 128:256] + full[40:80, 0:128] + local[j, 1]
+        for c, f in enumerate((f_re, f_im)):
+            snr[c, 0:32, :], snr[c, 32:40, :] = f[0:32], f[32:40] * keep
             for d in range(4):
-                grouped[c, d, pl.ds(part, 9, stride=8), :] = snr[c, pl.ds(d, 9, stride=4), :]
-        return 0
-
-    grouped[:, :, 72:128, :] = jnp.zeros((2, 4, 56, 128), F32)
-    s_re[36:40, :] = jnp.zeros((4, WIDE), F32)
-    s_im[36:40, :] = jnp.zeros((4, WIDE), F32)
-    lax.fori_loop(0, WIDE // 256, one_part, 0, unroll=UNROLL)
+                grouped[c, d, pl.ds(j, 9, stride=8), :] = snr[c, pl.ds(d, 9, stride=4), :]
 
     for d in range(4):
         ahead = dot3(h_head, h_tail, *halves(delayed(halo[d : d + 1])))
@@ -356,7 +373,7 @@
 
 TABLE, EIGHT = ((128, WIDE), BF16), ((8, WIDE), F32)
 PREPARED = [TABLE] * 4 + [EIGHT] * 6 + [((16, 128), F32)]
-LOCAL = [((32, WIDE), F32), ((32, WIDE), F32), ((8, 32, 256), F32)]
+STATE = ((8, WIDE + 128), F32)
 
 
 def prepare(*args):
@@ -365,19 +382,23 @@
 
 def of_column(*args):
     scratch = [((512, 128), F32), ((256, 384), BF16)]
-    return call(column_kernel, 1, 12, [((8, 8, WIDE + 128), F32)], scratch)(*args)[0]
+    return call(column_kernel, 1, 10, [((2, 8, WIDE + 128), F32)], scratch)(*args)[0]
+
+
+def of_chip(*args):
+    return call(chip_kernel, 1, 4, [STATE] * 4, [])(*args)
 
 
 def of_device(*args):
-    return call(local_kernel, 1, 7, LOCAL, [((32, 128), F32)])(*args)
+    scratch = [((32, 128), F32), ((80, WIDE), F32)]
+    return call(local_kernel, 1, 9, [((8, 2, 40, 128), F32)], scratch)(*args)[0]
 
 
 def to_peak(*args):
     scratch = [
-        ((40, WIDE), F32), ((40, WIDE), F32), ((2, 40, 128), F32), ((2, 4, 128, 128), F32),
-        ((2, 4, 192, 128), F32),
+        ((80, WIDE), F32), ((2, 40, 128), F32), ((2, 4, 128, 128), F32), ((2, 4, 192, 128), F32),
     ]
-    return call(peak_kernel, 3, 11, [((8, 1024), F32)], scratch)(*args)[0]
+    return call(peak_kernel, 3, 12, [((8, 1024), F32)], scratch)(*args)[0]
 
 
 def shards(strain, decay_rate, frequency, gain, member, sky_delay, antenna):
@@ -386,15 +407,19 @@
     plane = 2 * lax.axis_index("x") + lax.axis_index("core")
     place = jnp.stack([lax.axis_index("z"), plane, lax.axis_index("det")]).astype(jnp.int32)
     flip = jnp.asarray(np.eye(128, dtype=np.float32)[::-1], dtype=BF16)
-    prh, prt, pih, pit, rr, ri, wr, wi, vr, vi, response = prepare(
+    *tables, rr, ri, wr, wi, vr, vi, response = prepare(
         place, decay_rate.reshape(64, 128), frequency.reshape(64, 128), gain, member.reshape(64, 128)
     )
-    partial = of_column(place, column, flip, prh, prt, pih, pit, rr, ri, wr, wi, vr, vi)
-    got = lax.all_to_all(partial, ("x", "core"), 0, 0, tiled=True)
-    e_re, e_im, direct = of_device(place, column, flip, prh, prt, pih, pit, response)
+    mine = of_column(place, column, flip, *tables, rr, ri, wr, wi)
+    other = lax.ppermute(mine, "core", [(0, 1), (1, 0)])
+    first, *rest = of_chip(place, mine, other, vr, vi)
+    got = [
+        lax.ppermute(v, "x", [(x, (x + k) % 4) for x in range(4)]) for k, v in enumerate(rest, 1)
+    ]
+    local = of_device(place, column, flip, *tables, rr, ri, response)
     return to_peak(
         place, sky_delay.reshape(-1), antenna.reshape(-1),
-        got, e_re, e_im, direct, response, prh, prt, pih, pit, rr, ri,
+        first, *got, local, response, *tables, rr, ri,
     )
 
 

time: 48.9 us -> 42.6 us (0.87)
  waiting for transfers between devices: 10.9 us -> 5.13 us
  local copies, waits for them, and re-layouts: 4.72 us -> 3.05 us
  Pallas kernels: 14 us -> 14.8 us
  starting transfers between devices: 18.7 us -> 19.2 us
    ppermute x0 -> x4, starting transfers between devices: none -> 7.05 us  [the longest x3 4.88 us: shards(): lax.ppermute(v, 'x', [(x, (x + k) % 4) for x in range(4)])]
    all_to_all x1 -> x0, waiting for transfers between devices: 6.79 us -> none  [shards(): got = lax.all_to_all(partial, ('x', 'core'), 0, 0, tiled=True)]
    all_to_all x1 -> x0, starting transfers between devices: 6.5 us -> none  [shards(): got = lax.all_to_all(partial, ('x', 'core'), 0, 0, tiled=True)]
    unnamed x20 -> x16, local copies, waits for them, and re-layouts: 3.14 us -> 1.47 us
    ppermute x0 -> x4, waiting for transfers between devices: none -> 1 us  [the longest x1 1 us: shards(): other = lax.ppermute(mine, 'core', [(0, 1), (1, 0)])]
    pallas_call x3 -> x4, Pallas kernels: 9.76 us -> 10.5 us  [the longest x1 5.48 us: to_peak(): return call(peak_kernel, 3, 12, [((8, 1024), F32)], scratch)(*args)[0]]
  transfers between devices with their start and end apart: 2 -> 5, of which waited for: 2 -> 2; matrix products, arithmetic and copies ran while one was open for 1% -> 1% of each run, Pallas kernels for 11% -> 15%
where the time goes in v3:
time: 42.6 us; the launch traced here: 42.3 us
  starting transfers between devices  19.2 us (45%)
  Pallas kernels  14.8 us (35%)
  waiting for transfers between devices  5.13 us (12%)
  local copies, waits for them, and re-layouts  3.05 us (7%)
    all_to_all x1, starting transfers between devices, shards(): lax.all_to_all(sent, ('det', 'z'), 0, 0, tiled=True).reshape(256, 128)  12.2 us
    pallas_call x1, Pallas kernels, to_peak(): return call(peak_kernel, 3, 12, [((8, 1024), F32)], scratch)(*args)[0]  5.48 us
    ppermute x3, starting transfers between devices, shards(): lax.ppermute(v, 'x', [(x, (x + k) % 4) for x in range(4)])  4.88 us
    pallas_call x1, Pallas kernels, prepare(): return call(prepare_kernel, 1, 4, PREPARED, [((4, 16, 128), F32)])(*args)  4.26 us
    all_to_all x1, waiting for transfers between devices, shards(): lax.all_to_all(sent, ('det', 'z'), 0, 0, tiled=True).reshape(256, 128)  4.13 us
    pallas_call x1, Pallas kernels, of_device(): return call(local_kernel, 1, 9, [((8, 2, 40, 128), F32)], scratch)(*args)[0]  2.23 us
    ppermute x1, starting transfers between devices, shards(): other = lax.ppermute(mine, 'core', [(0, 1), (1, 0)])  2.16 us
    pallas_call x1, Pallas kernels, of_column(): call(column_kernel, 1, 10, [((2, 8, WIDE + 128), F32)], scratch)(*args)[0]  2.09 us
  transfers between devices with their start and end apart: 5, of which 2 were waited for; matrix products, arithmetic and copies ran while one was open for 1% of the time, Pallas kernels for 15%

profile of v3, /device:TPU:1, one launch (start us, length us, event | category | flops | bytes accessed | tf_op | source)
XLA Modules:
  0.0 42.3 jit_solution(9804449309753718681)
XLA Ops:
  0.0 1.3 %broadcast_in_dim.8 = f32[32,8,128]{2,1,0:T(8,128)} broadcast(f32[8,128]{1,0:T(8,128)} %bitcast.13), dimensions={1,2} | broadcast | bytes 135168 | tf_op jit(solution)/shard_map/broadcast_in_dim | solution.py:405
  1.3 0.0 copy-start.1
  1.3 0.0 copy-start.3
  1.4 12.2 %all-to-all-start = ((f32[32,8,128]{2,1,0:T(8,128)}), f32[32,8,128]{2,1,0:T(8,128)S(1)}, u32[]{:S(2)}, u32[]{:S(2)}) async-start(f32[32,8,128]{2,1,0:T(8,128)} %broadcast_in_dim.8), calls=%async_computation | async-start | bytes 262144 | tf_op jit(solution)/shard_map/all_to_all | solution.py:406
  13.5 0.0 copy-start.2
  13.5 0.1 pad_add_fusion.place
  13.6 0.0 copy-done.1
  13.6 0.0 copy-done.3
  13.6 0.0 copy-done.4
  13.6 0.7 %copy-done.2 = f32[8192]{0:T(1024)S(1)} copy-done((f32[8192]{0:T(1024)S(1)}, f32[8192]{0:T(1024)}, u32[]{:S(2)}) %copy-start.2) | copy-done | bytes 32792
  14.3 4.3 %shard_map.82 = (bf16[128,2048]{1,0:T(8,128)(2,1)S(1)}, bf16[128,2048]{1,0:T(8,128)(2,1)S(1)}, bf16[128,2048]{1,0:T(8,128)(2,1)S(1)}, bf16[128,2048]{1,0:T(8,128...) custom-call(s32[3]{0:T(128)S(1)} %pad_add_fusion.place, ...), custom_call_target="tpu_custom_call" | custom-call | tf_op jit(solution)/shard_map/pallas_call | solution.py:380
  18.6 4.1 %all-to-all-done = f32[32,8,128]{2,1,0:T(8,128)S(1)} async-done(((f32[32,8,128]{2,1,0:T(8,128)}), f32[32,8,128]{2,1,0:T(8,128)S(1)}, u32[]{:S(2)}, u32[]{:S(2)}) %all-to-all-start) | async-done | bytes 131104 | tf_op jit(solution)/shard_map/all_to_all | solution.py:406
  22.7 0.0 copy-done
  22.7 2.1 %shard_map.83.mine = f32[2,8,2176]{2,1,0:T(8,128)S(1)} custom-call(s32[3]{0:T(128)S(1)} %pad_add_fusion.place, f32[256,128]{1,0:T(8,128)S(1)} %bitcast.8, bf16[128,128]{1,0:T(8,128)(2,1)S(1)} %copy-done, bf16[128,2048]{1,0:T(8,128)(2,1)S(1)} %get-tuple-element.20.pr_head, bf16[128,2048]{1,0:T(8,128)(2,1)S(1)} %get-tuple-element.21.pr_tail, ...), custom_call_target="tpu_custom_call" | custom-call | tf_op jit(solution)/shard_map/pallas_call | solution.py:385
  24.8 2.2 %collective-permute-start = (f32[2,8,2176]{2,1,0:T(8,128)S(1)}, f32[2,8,2176]{2,1,0:T(8,128)S(1)}, u32[]{:S(2)}, u32[]{:S(2)}) collective-permute-start(f32[2,8,2176]{2,1,0:T(8,128)S(1)} %shard_map.83.mine), channel_id=1, source_target_pairs={{0,4},{4,0},{1,5},{5,1},{2,6},{6,2},{3,7},{7,3},{8,12},{12,8},{9,1... | collective-permute-start | bytes 417800 | tf_op jit(solution)/shard_map/ppermute | solution.py:414
  26.9 1.0 %collective-permute-done.other = f32[2,8,2176]{2,1,0:T(8,128)S(1)} collective-permute-done((f32[2,8,2176]{2,1,0:T(8,128)S(1)}, f32[2,8,2176]{2,1,0:T(8,128)S(1)}, u32[]{:S(2)}, u32[]{:S(2)}) %collective-permute-start) | collective-permute-done | bytes 139296 | tf_op jit(solution)/shard_map/ppermute | solution.py:414
  27.9 0.7 %shard_map.84 = (f32[8,2176]{1,0:T(8,128)S(1)}, f32[8,2176]{1,0:T(8,128)S(1)}, f32[8,2176]{1,0:T(8,128)S(1)}, f32[8,2176]{1,0:T(8,128)S(1)}) custom-call(s32[3]{0:T(128)S(1)} %pad_add_fusion.place, f32[2,8,2176]{2,1,0:T(8,128)S(1)} %shard_map.83.mine, f32[2,8,2176]{2,1,0:T(8,128)S(1)} %collective-permute-done.other, f32[8,2048]{1,0:T(8,128)S(1)} %get-tuple-element.28.vr, ...), custom_call_target="tpu_custom_call" | custom-call | tf_op jit(solution)/shard_map/pallas_call | solution.py:389
  28.6 0.0 copy-start.6
  28.7 1.3 %collective-permute-start.1 = (f32[8,2176]{1,0:T(8,128)S(1)}, f32[8,2176]{1,0:T(8,128)S(1)}, u32[]{:S(2)}, u32[]{:S(2)}) collective-permute-start(f32[8,2176]{1,0:T(8,128)S(1)} %get-tuple-element.31), channel_id=1, source_target_pairs={{0,8},{8,16},{16,24},{24,0},{1,9},{9,17},{17,25},{25,1},{2,10},{10... | collective-permute-start | bytes 208904 | tf_op jit(solution)/shard_map/ppermute | solution.py:417
  29.9 2.4 %collective-permute-start.2 = (f32[8,2176]{1,0:T(8,128)S(1)}, f32[8,2176]{1,0:T(8,128)S(1)}, u32[]{:S(2)}, u32[]{:S(2)}) collective-permute-start(f32[8,2176]{1,0:T(8,128)S(1)} %get-tuple-element.32), channel_id=1, source_target_pairs={{0,16},{8,24},{16,0},{24,8},{1,17},{9,25},{17,1},{25,9},{2,18},{10... | collective-permute-start | bytes 208904 | tf_op jit(solution)/shard_map/ppermute | solution.py:417
  32.4 1.2 %collective-permute-start.3 = (f32[8,2176]{1,0:T(8,128)S(1)}, f32[8,2176]{1,0:T(8,128)S(1)}, u32[]{:S(2)}, u32[]{:S(2)}) collective-permute-start(f32[8,2176]{1,0:T(8,128)S(1)} %get-tuple-element.33), channel_id=1, source_target_pairs={{0,24},{8,0},{16,8},{24,16},{1,25},{9,1},{17,9},{25,17},{2,26},{10... | collective-permute-start | bytes 208904 | tf_op jit(solution)/shard_map/ppermute | solution.py:417
  33.5 0.0 copy-done.6
  33.5 0.1 copy.9
  33.6 0.1 reshape.20.delay
  33.7 0.6 %copy-done.5 = f32[64,2,4]{0,2,1:T(4,128)S(1)} copy-done((f32[64,2,4]{0,2,1:T(4,128)S(1)}, f32[64,2,4]{0,2,1:T(4,128)}, u32[]{:S(2)}) %copy-start.5) | copy-done | bytes 2072
  34.3 0.1 copy.10
  34.4 0.1 reshape.21.antenna
  34.6 2.2 %shard_map.85.local = f32[8,2,40,128]{3,2,1,0:T(8,128)S(1)} custom-call(s32[3]{0:T(128)S(1)} %pad_add_fusion.place, f32[256,128]{1,0:T(8,128)S(1)} %bitcast.9, bf16[128,128]{1,0:T(8,128)(2,1)S(1)} %copy-done, bf16[128,2048]{1,0:T(8,128)(2,1)S(1)} %get-tuple-element.20.pr_head, bf16[128,2048]{1,0:T(8,128)(2,1)S(1)} %get-tuple-element.21.pr_tail, ...), custom_call_target="tpu_custom_call" | custom-call | tf_op jit(solution)/shard_map/pallas_call | solution.py:394
  36.8 0.0 collective-permute-done.1.got1
  36.8 0.0 collective-permute-done.2.got2
  36.8 0.0 collective-permute-done.3.got3
  36.8 5.5 %shard_map.86 = f32[8,1024]{1,0:T(8,128)} custom-call(s32[3]{0:T(128)S(1)} %pad_add_fusion.place, s32[256]{0:T(256)S(1)} %reshape.20.delay, f32[512]{0:T(512)S(1)} %reshape.21.antenna, f32[8,2176]{1,0:T(8,128)S(1)} %get-tuple-element.30.got0, f32[8,2176]{1,0:T(8,128)S(1)} %collective-permute-done.1.got1, f32[8,2176]{1,0:T(8,128)S(1)} %collective-permute-done.2.got2, ...), custom_call_target="tpu_custom_call" | custom-call | tf_op jit(solution)/shard_map/pallas_call | solution.py:401
  (3 shorter events, 0.0 us)
Async XLA Ops:
  1.3 12.3 %copy-start.1 = (f32[2,8192]{1,0:T(2,128)S(1)}, f32[2,8192]{1,0:T(2,128)}, u32[]{:S(2)}) copy-start(f32[2,8192]{1,0:T(2,128)} %gain.1) | copy-start | bytes 196612
  1.3 12.3 %copy-start.3 = (f32[8192]{0:T(1024)S(1)}, f32[8192]{0:T(1024)}, u32[]{:S(2)}) copy-start(f32[8192]{0:T(1024)} %param.10) | copy-start | bytes 98308
  1.3 12.3 %copy-start.4 = (s32[8192]{0:T(1024)S(1)}, s32[8192]{0:T(1024)}, u32[]{:S(2)}) copy-start(s32[8192]{0:T(1024)} %param.12) | copy-start | bytes 98308
  1.4 21.3 %all-to-all-start = ((f32[32,8,128]{2,1,0:T(8,128)}), f32[32,8,128]{2,1,0:T(8,128)S(1)}, u32[]{:S(2)}, u32[]{:S(2)}) async-start(f32[32,8,128]{2,1,0:T(8,128)} %broadcast_in_dim.8), calls=%async_computation | async-start | bytes 262144 | tf_op jit(solution)/shard_map/all_to_all | solution.py:406
  13.5 0.8 %copy-start.2 = (f32[8192]{0:T(1024)S(1)}, f32[8192]{0:T(1024)}, u32[]{:S(2)}) copy-start(f32[8192]{0:T(1024)} %param.9) | copy-start | bytes 98308
  14.3 8.4 %copy-start = (bf16[128,128]{1,0:T(8,128)(2,1)S(1)}, bf16[128,128]{1,0:T(8,128)(2,1)}, u32[]{:S(2)}) copy-start(bf16[128,128]{1,0:T(8,128)(2,1)} %constant.21.clone.flip) | copy-start | bytes 98308
  24.8 3.2 %collective-permute-start = (f32[2,8,2176]{2,1,0:T(8,128)S(1)}, f32[2,8,2176]{2,1,0:T(8,128)S(1)}, u32[]{:S(2)}, u32[]{:S(2)}) collective-permute-start(f32[2,8,2176]{2,1,0:T(8,128)S(1)} %shard_map.83.mine), channel_id=1, source_target_pairs={{0,4},{4,0},{1,5},{5,1},{2,6},{6,2},{3,7},{7,3},{8,12},{12,8},{9,1... | collective-permute-start | bytes 417800 | tf_op jit(solution)/shard_map/ppermute | solution.py:414
  28.6 4.9 %copy-start.6 = (s32[64,4]{0,1:T(4,128)S(1)}, s32[64,4]{0,1:T(4,128)}, u32[]{:S(2)}) copy-start(s32[64,4]{0,1:T(4,128)} %param.13) | copy-start | bytes 3076
  28.7 8.2 %collective-permute-start.1 = (f32[8,2176]{1,0:T(8,128)S(1)}, f32[8,2176]{1,0:T(8,128)S(1)}, u32[]{:S(2)}, u32[]{:S(2)}) collective-permute-start(f32[8,2176]{1,0:T(8,128)S(1)} %get-tuple-element.31), channel_id=1, source_target_pairs={{0,8},{8,16},{16,24},{24,0},{1,9},{9,17},{17,25},{25,1},{2,10},{10... | collective-permute-start | bytes 208904 | tf_op jit(solution)/shard_map/ppermute | solution.py:417
  29.9 6.9 %collective-permute-start.2 = (f32[8,2176]{1,0:T(8,128)S(1)}, f32[8,2176]{1,0:T(8,128)S(1)}, u32[]{:S(2)}, u32[]{:S(2)}) collective-permute-start(f32[8,2176]{1,0:T(8,128)S(1)} %get-tuple-element.32), channel_id=1, source_target_pairs={{0,16},{8,24},{16,0},{24,8},{1,17},{9,25},{17,1},{25,9},{2,18},{10... | collective-permute-start | bytes 208904 | tf_op jit(solution)/shard_map/ppermute | solution.py:417
  32.4 4.5 %collective-permute-start.3 = (f32[8,2176]{1,0:T(8,128)S(1)}, f32[8,2176]{1,0:T(8,128)S(1)}, u32[]{:S(2)}, u32[]{:S(2)}) collective-permute-start(f32[8,2176]{1,0:T(8,128)S(1)} %get-tuple-element.33), channel_id=1, source_target_pairs={{0,24},{8,0},{16,8},{24,16},{1,25},{9,1},{17,9},{25,17},{2,26},{10... | collective-permute-start | bytes 208904 | tf_op jit(solution)/shard_map/ppermute | solution.py:417
  33.6 0.7 %copy-start.5 = (f32[64,2,4]{0,2,1:T(4,128)S(1)}, f32[64,2,4]{0,2,1:T(4,128)}, u32[]{:S(2)}) copy-start(f32[64,2,4]{0,2,1:T(4,128)} %param.14) | copy-start | bytes 6148

commit v4 on v3

v4 whole, which is shorter than its diff:
```python
import functools
import math

import jax
import jax.numpy as jnp
import numpy as np
from jax import lax
from jax.experimental import pallas as pl
from jax.experimental.pallas import tpu as pltpu
from jax.sharding import Mesh, PartitionSpec as P

FILT = 256
SKY = 64
WIDE = 8 * FILT
F32, BF16 = jnp.float32, jnp.bfloat16

TURN = 1.0 / (2.0 * math.pi)
TURN_HEAD = math.floor(TURN * 2**14) / 2**14
TURN_TAIL = TURN - TURN_HEAD

ROW_128, ROW_1024, ROW_8192, ROW_GAIN, ROW_LEAD = 0, 1, 2, 3, 4

VMEM_LIMIT = 16 * 2**20
UNROLL = True
EARLY = 3


def taylor(first, start, count):
    return [
        first * (-1) ** k * math.pi ** (2 * k + start) / math.factorial(2 * k + start)
        for k in range(count)
    ]


SINE, COSINE = taylor(1.0, 1, 8), taylor(1.0, 0, 9)


def horner(coefficients, square):
    total = jnp.full(square.shape, coefficients[-1], F32)
    for c in coefficients[-2::-1]:
        total = total * square + c
    return total


def cmul(ar, ai, br, bi):
    return ar * br - ai * bi, ar * bi + ai * br


def halves(x):
    head = x.astype(BF16)
    return head, (x - head.astype(F32)).astype(BF16)


def dot(a, b, contract_b=0):
    return lax.dot_general(
        a, b, (((1,), (contract_b,)), ((), ())), preferred_element_type=F32
    )


def dot3(a_head, a_tail, b_head, b_tail, contract_b=0):
    rows = a_head.shape[0]
    both = dot(jnp.concatenate([a_head, a_tail], axis=0), b_head, contract_b)
    return both[:rows] + both[rows:] + dot(a_head, b_tail, contract_b)


def lead_tables(lanes, pr_head, pr_tail, pi_head, pi_tail):
    return (
        jnp.concatenate([pr_head[:, lanes], pi_head[:, lanes]], axis=0),
        jnp.concatenate([pr_tail[:, lanes], pi_tail[:, lanes]], axis=0),
    )


def prepare_kernel(
    place, decay, frequency, gain, member, antenna, sky_delay,
    pr_head, pr_tail, pi_head, pi_tail, row_re, row_im, block_re, block_im, wr, wi, vr, vi, response,
    weight, delay, par,
):
    zi, xc, det = place[0], place[1], place[2]

    delay[...] = sky_delay[...]
    one, two = antenna[0:4, :], antenna[4:8, :]
    scale = jnp.maximum(jnp.abs(one[0:1]), jnp.abs(two[0:1]))
    divisor = jnp.where(scale > 0.0, scale, 1.0)
    a, b = jnp.where(scale > 0.0, one[0:1] / divisor, 1.0), two[0:1] / divisor
    size = jnp.sqrt(a * a + b * b)
    cosine, sine = a / size, b / size
    weight[...] = jnp.concatenate([cosine * one + sine * two, cosine * two - sine * one], axis=0)

    index = [
        member[pl.ds(pl.multiple_of(16 * det + 8 * half, 8), 8), :] for half in range(2)
    ]
    high, low = [v >> 7 for v in index], [v & 127 for v in index]

    def one_row(r, carried):
        lanes = pl.ds(pl.multiple_of(r * 128, 128), 128)
        values = (
            decay[pl.ds(r, 1), :],
            frequency[pl.ds(r, 1), :],
            gain[0:1, lanes],
            gain[1:2, lanes],
        )
        spread = [jnp.broadcast_to(v, (8, 128)) for v in values]
        return tuple(
            jnp.where(
                high[h] == r,
                jnp.take_along_axis(spread[k], low[h], axis=1),
                carried[4 * h + k],
            )
            for h in range(2)
            for k in range(4)
        )

    nothing = jnp.zeros((8, 128), F32)
    found = lax.fori_loop(0, 64, one_row, (nothing,) * 8, unroll=8)
    for h in range(2):
        for k in range(4):
            par[k, 8 * h : 8 * h + 8, :] = found[4 * h + k]

    power = jnp.left_shift(1, lax.broadcasted_iota(jnp.int32, (16, 128), 0)).astype(F32)
    place8 = lax.broadcasted_iota(jnp.int32, (8, 128), 0)
    ahead_z = zi - 1 - (lax.broadcasted_iota(jnp.int32, (32, 128), 0) >> 2)
    ahead_x = jnp.where(place8 < 4, 2 * place8 - 1, 2 * place8 + 2 * (xc & 1) - 10) & 7

    def choose(exponent, rows, re, im):
        out_re = jnp.ones(exponent.shape, F32)
        out_im = jnp.zeros(exponent.shape, F32)
        for bit, row in enumerate(rows):
            new_re, new_im = cmul(out_re, out_im, re[row : row + 1], im[row : row + 1])
            on = (exponent >> bit) & 1 == 1
            out_re = jnp.where(on, new_re, out_re)
            out_im = jnp.where(on, new_im, out_im)
        return out_re, out_im

    def one_chunk(c, _):
        lanes = pl.ds(pl.multiple_of(c * 128, 128), 128)
        f = par[1, pl.ds(c, 1), :]
        f_head = jnp.floor(f * 2048.0) * (1.0 / 2048.0)
        f_tail = f - f_head
        first = power * (f_head * TURN_HEAD)
        second = power * (f_head * TURN_TAIL + f_tail * TURN)
        turn = (first - jnp.floor(first + 0.5)) + (second - jnp.floor(second + 0.5))
        turn = turn - jnp.floor(turn + 0.5)
        square = turn * turn
        sine = turn * horner(SINE, square)
        cosine = horner(COSINE, square)
        size = jnp.exp(-power * par[0, pl.ds(c, 1), :])
        re = size * (1.0 - 2.0 * sine * sine)
        im = size * (2.0 * sine * cosine)
        g_re, g_im = par[2, pl.ds(c, 1), :], par[3, pl.ds(c, 1), :]
        l_re, l_im = cmul(g_re, g_im, re[0:1], im[0:1])
        empty = jnp.zeros((3, 128), F32)
        for single, v, g, lead in ((row_re, re, g_re, l_re), (row_im, im, g_im, l_im)):
            single[:, lanes] = jnp.concatenate(
                [v[7:8], v[10:11], v[13:14], g, lead, empty], axis=0
            )
        block_re[:, lanes], block_im[:, lanes] = choose(place8, (7, 8, 9), re, im)
        w_re, w_im = choose(ahead_z, (13, 14, 15), re, im)
        wr[:, lanes] = jnp.where(ahead_z >= 0, w_re, 0.0)
        wi[:, lanes] = jnp.where(ahead_z >= 0, w_im, 0.0)
        vr[:, lanes], vi[:, lanes] = choose(ahead_x, (10, 11, 12), re, im)
        t_re, t_im = choose(place8, (0, 1, 2), re, im)
        for row in range(3, 7):
            n_re, n_im = cmul(t_re, t_im, re[row : row + 1], im[row : row + 1])
            t_re = jnp.concatenate([t_re, n_re], axis=0)
            t_im = jnp.concatenate([t_im, n_im], axis=0)
        pr_head[:, lanes], pr_tail[:, lanes] = halves(t_re)
        pi_head[:, lanes], pi_tail[:, lanes] = halves(t_im)
        return 0

    lax.fori_loop(0, WIDE // 128, one_chunk, 0)

    for j in range(WIDE // FILT):
        lanes = slice(FILT * j, FILT * j + FILT)
        both_head, both_tail = halves(jnp.concatenate([row_re[:, lanes], row_im[:, lanes]], axis=0))
        full = dot3(both_head, both_tail, *lead_tables(lanes, pr_head, pr_tail, pi_head, pi_tail), 1)
        full_re = full[0:8, 0:128] - full[8:16, 128:256]
        full_im = full[0:8, 128:256] + full[8:16, 0:128]
        response[j : j + 1, :] = full_re[ROW_GAIN : ROW_GAIN + 1]
        response[8 + j : 9 + j, :] = full_im[ROW_GAIN : ROW_GAIN + 1]


def delayed(row):
    lag = lax.broadcasted_iota(jnp.int32, (128, 128), 1) - lax.broadcasted_iota(
        jnp.int32, (128, 128), 0
    )
    rolled = pltpu.roll(jnp.broadcast_to(row, (128, 128)), 0, 1, stride=1, stride_axis=0)
    return jnp.where(lag >= 0, rolled, 0.0)


def column_kernel(
    place, x, flip, pr_head, pr_tail, pi_head, pi_tail, row_re, row_im, wr, wi,
    states, turned, lhs,
):
    zi, xc = place[0], place[1]
    turned[...] = dot(jnp.concatenate(halves(x[...]), axis=0), flip[...])
    for q in range(8):
        rows = [turned[pl.ds(256 * h + 7 - q, 32, stride=8), :].astype(BF16) for h in (0, 1, 0)]
        lhs[32 * q : 32 * q + 32, :] = jnp.concatenate(rows, axis=1)
    own = (lax.broadcasted_iota(jnp.int32, (32, 256), 0) >> 2) == zi
    upper = lax.broadcasted_iota(jnp.int32, (8, 256), 0) < 4

    def over_shards(v):
        total = (v[0:8] + v[8:16]) + (v[16:24] + v[24:32])
        return total + pltpu.roll(total, 4, 0)

    def one_part(part, _):
        lanes = pl.ds(pl.multiple_of(part * 256, 256), 256)
        e_re, e_im = (
            dot(lhs[...], jnp.concatenate([head[:, lanes], head[:, lanes], tail[:, lanes]], axis=0))
            for head, tail in ((pr_head, pr_tail), (pi_head, pi_tail))
        )
        step_re = row_re[ROW_128 : ROW_128 + 1, lanes]
        step_im = row_im[ROW_128 : ROW_128 + 1, lanes]
        s_re, s_im = e_re[224:256], e_im[224:256]
        for q in range(6, -1, -1):
            s_re, s_im = cmul(s_re, s_im, step_re, step_im)
            s_re = s_re + e_re[32 * q : 32 * q + 32]
            s_im = s_im + e_im[32 * q : 32 * q + 32]
        b_re, b_im = (over_shards(v) for v in cmul(s_re, s_im, wr[:, lanes], wi[:, lanes]))
        o_re, o_im = (over_shards(jnp.where(own, v, 0.0)) for v in (s_re, s_im))
        i_re, i_im = cmul(
            b_re, b_im,
            row_re[ROW_8192 : ROW_8192 + 1, lanes], row_im[ROW_8192 : ROW_8192 + 1, lanes],
        )
        states[0, :, lanes] = jnp.where(upper, b_re, b_im)
        states[1, :, lanes] = jnp.where(upper, i_re + o_re, i_im + o_im)
        return 0

    lax.fori_loop(0, WIDE // 256, one_part, 0, unroll=UNROLL)

    shard = jnp.where(xc == 0, zi + 1, zi)
    inside = shard < 8
    row = jnp.minimum(shard, 7) * 32
    halo = jnp.concatenate(
        [x[pl.ds(row + 8 * d, 1), :] for d in range(4)] + [jnp.zeros((4, 128), F32)],
        axis=0,
    )
    halo = jnp.where(inside, halo, 0.0)
    for p in range(2):
        states[p, :, WIDE : WIDE + 128] = halo


def chip_kernel(place, mine, other, vr, vi, beside, *sent):
    del beside
    upper = lax.broadcasted_iota(jnp.int32, (8, 256), 0) < 4
    x, core = place[1] >> 1, place[1] & 1
    for k in range(4):
        target = 2 * ((x + k) & 3) + core
        for part in range(WIDE // 256):
            lanes = slice(256 * part, 256 * part + 256)
            total = None
            for states, column, row in ((mine, 2 * x + core, k), (other, 2 * x + 1 - core, 4 + k)):
                state = states[jnp.where(column < target, 1, 0), :, lanes]
                turn = vi[row : row + 1, lanes]
                term = state * vr[row : row + 1, lanes] + pltpu.roll(state, 4, 0) * jnp.where(
                    upper, -turn, turn
                )
                total = term if total is None else total + term
            sent[k][:, lanes] = total
        sent[k][:, WIDE : WIDE + 128] = other[0, :, WIDE : WIDE + 128]


def local_kernel(
    place, x, flip, pr_head, pr_tail, pi_head, pi_tail, row_re, row_im, block_re, block_im, response,
    local, *, first,
):
    zi = place[0]
    n_head, n_tail = halves(x[pl.ds(pl.multiple_of(32 * zi, 32), 32), :])
    x_head, x_tail = (dot(v, flip[...]).astype(BF16) for v in (n_head, n_tail))
    row8 = lax.broadcasted_iota(jnp.int32, (8, FILT), 0)
    for k in range(local.shape[0]):
        j = first + k
        lanes = slice(FILT * j, FILT * j + FILT)
        l_re = dot3(x_head, x_tail, pr_head[:, lanes], pr_tail[:, lanes])
        l_im = dot3(x_head, x_tail, pi_head[:, lanes], pi_tail[:, lanes])
        g_re, g_im = (v[ROW_LEAD : ROW_LEAD + 1, lanes] for v in (row_re, row_im))
        s_re, s_im, end_re, end_im = [], [], [], []
        for d in range(4):
            q_re, q_im = cmul(l_re[8 * d : 8 * d + 8], l_im[8 * d : 8 * d + 8], g_re, g_im)
            for step in (1, 2, 4):
                t_re, t_im = cmul(
                    pltpu.roll(q_re, step, 0), pltpu.roll(q_im, step, 0),
                    block_re[step : step + 1, lanes], block_im[step : step + 1, lanes],
                )
                q_re = q_re + jnp.where(row8 >= step, t_re, 0.0)
                q_im = q_im + jnp.where(row8 >= step, t_im, 0.0)
            s_re.append(jnp.where(row8 >= 1, pltpu.roll(q_re, 1, 0), 0.0))
            s_im.append(jnp.where(row8 >= 1, pltpu.roll(q_im, 1, 0), 0.0))
            end_re.append(q_re[7:8])
            end_im.append(q_im[7:8])
        none = [jnp.zeros((4, FILT), F32)]
        full = dot3(
            *halves(jnp.concatenate(s_re + end_re + none + s_im + end_im + none, axis=0)),
            *lead_tables(lanes, pr_head, pr_tail, pi_head, pi_tail), 1,
        )
        matrices = [delayed(response[row : row + 1, :]) for row in (j, 8 + j)]
        own = dot3(n_head, n_tail, *halves(jnp.concatenate(matrices, axis=1)))
        f_re = full[0:40, 0:128] - full[40:80, 128:256]
        f_im = full[0:40, 128:256] + full[40:80, 0:128]
        local[k, 0, 0:32, :], local[k, 0, 32:40, :] = f_re[0:32] + own[:, 0:128], f_re[32:40]
        local[k, 1, 0:32, :], local[k, 1, 32:40, :] = f_im[0:32] + own[:, 128:256], f_im[32:40]


def peak_kernel(
    place, delay, antenna, got0, got1, got2, got3, local0, local1, response,
    pr_head, pr_tail, pi_head, pi_tail, row_re, row_im, block_re, block_im,
    out, grouped, shifted,
):
    zi, xc = place[0], place[1]
    keep = jnp.where(jnp.logical_and(zi == 7, xc == 7), 0.0, 1.0)
    ahead_lanes = slice(WIDE, WIDE + 128)
    halo = jnp.where((xc & 1) == 0, got0[:, ahead_lanes], got3[:, ahead_lanes])
    h_head, h_tail = halves(response[...])
    bottom = lax.broadcasted_iota(jnp.int32, (8, 128), 0) == 7

    for j in range(WIDE // FILT):
        lanes = slice(FILT * j, FILT * j + FILT)
        q = (got0[:, lanes] + got1[:, lanes]) + (got2[:, lanes] + got3[:, lanes])
        single = [
            v[row : row + 1, lanes] for row in (ROW_LEAD, ROW_1024) for v in (row_re, row_im)
        ]
        q_re, q_im = cmul(q, pltpu.roll(q, 4, 0), *single[:2])
        states = [
            cmul(
                jnp.broadcast_to(q_re[d : d + 1], (8, FILT)),
                jnp.broadcast_to(q_im[d : d + 1], (8, FILT)),
                block_re[:, lanes], block_im[:, lanes],
            )
            for d in range(4)
        ]
        s_re, s_im = zip(*states, cmul(q_re, q_im, *single[2:]))
        full = dot3(
            *halves(jnp.concatenate(s_re + s_im, axis=0)),
            *lead_tables(lanes, pr_head, pr_tail, pi_head, pi_tail), 1,
        )
        local, k = (local0, j) if j < EARLY else (local1, j - EARLY)
        f_re = full[0:40, 0:128] - full[40:80, 128:256] + local[k, 0]
        f_im = full[0:40, 128:256] + full[40:80, 0:128] + local[k, 1]
        for c, f in enumerate((f_re, f_im)):
            after = f[32:40] * keep
            for d in range(4):
                own = f[8 * d : 8 * d + 8]
                grouped[c, d, 8 * j : 8 * j + 8, :] = own
                grouped[c, d, 64 + 8 * j : 72 + 8 * j, :] = jnp.where(
                    bottom, after[d : d + 1], pltpu.roll(own, 7, 0)
                )

    for d in range(4):
        ahead = dot3(h_head, h_tail, *halves(delayed(halo[d : d + 1])))
        for c in range(2):
            rows = pl.ds(71, 8, stride=8)
            grouped[c, d, rows, :] = grouped[c, d, rows, :] + ahead[8 * c : 8 * c + 8]

    early = lax.broadcasted_iota(jnp.int32, (64, 128), 1) < 64
    for c in range(2):
        for d in range(4):
            t = grouped[c, d].T
            top, low = t[0:64], t[64:128]
            shifted[c, d, 0:64, :] = jnp.where(early, top, pltpu.roll(low, 64, 1))
            shifted[c, d, 64:128, :] = jnp.where(early, low, top)
            shifted[c, d, 128:192, :] = jnp.where(early, pltpu.roll(top, 64, 1), low)

    def one_sky(s, best):
        total = [None] * 4
        for d in range(4):
            rows = pl.ds(delay[d, s], 64)
            for c in range(2):
                piece = shifted[c, d, rows, :]
                for p in range(2 if d else 1):
                    term = antenna[4 * p + d, s] * piece
                    k = 2 * p + c
                    total[k] = term if total[k] is None else total[k] + term
        energy = (total[0] * total[0] + total[1] * total[1]) + (
            total[2] * total[2] + total[3] * total[3]
        )
        return jnp.maximum(best, energy)

    best = lax.fori_loop(0, SKY, one_sky, jnp.zeros((64, 128), F32), unroll=4)
    turned = best.T
    for j in range(8):
        for m in range(8):
            row = 8 * j + m
            out[j : j + 1, 128 * m : 128 * m + 128] = jnp.concatenate(
                [turned[row : row + 1], turned[64 + row : 65 + row]], axis=1
            )


def call(kernel, n_scalar, n_vector, shapes, scratch, n_unread=0):
    scalar, vector, unread = (
        pl.BlockSpec(memory_space=m) for m in (pltpu.SMEM, pltpu.VMEM, pl.ANY)
    )
    return pl.pallas_call(
        kernel,
        out_shape=[jax.ShapeDtypeStruct(*s) for s in shapes],
        in_specs=[scalar] * n_scalar + [vector] * n_vector + [unread] * n_unread,
        out_specs=[vector] * len(shapes),
        scratch_shapes=[pltpu.VMEM(*s) for s in scratch],
        compiler_params=pltpu.CompilerParams(vmem_limit_bytes=VMEM_LIMIT),
    )


TABLE, EIGHT = ((128, WIDE), BF16), ((8, WIDE), F32)
PREPARED = [TABLE] * 4 + [EIGHT] * 4 + [((32, WIDE), F32)] * 2 + [EIGHT] * 2
PREPARED += [((16, 128), F32), ((8, SKY), F32), ((4, SKY), jnp.int32)]
STATE = ((8, WIDE + 128), F32)


def prepare(*args):
    return call(prepare_kernel, 1, 6, PREPARED, [((4, 16, 128), F32)])(*args)


def of_column(*args):
    scratch = [((512, 128), F32), ((256, 384), BF16)]
    return call(column_kernel, 1, 10, [((2, 8, WIDE + 128), F32)], scratch)(*args)[0]


def of_chip(*args):
    return call(chip_kernel, 1, 4, [STATE] * 4, [], 1)(*args)


def of_device(first, count, *args):
    kernel = functools.partial(local_kernel, first=first)
    return call(kernel, 1, 11, [((count, 2, 40, 128), F32)], [])(*args)[0]


def to_peak(*args):
    scratch = [((2, 4, 128, 128), F32), ((2, 4, 192, 128), F32)]
    return call(peak_kernel, 3, 15, [((8, 1024), F32)], scratch)(*args)[0]


def shards(strain, decay_rate, frequency, gain, member, sky_delay, antenna):
    sent = jnp.broadcast_to(strain.reshape(1, 8, 128), (32, 8, 128))
    column = lax.all_to_all(sent, ("z", "det"), 0, 0, tiled=True).reshape(256, 128)
    plane = 2 * lax.axis_index("x") + lax.axis_index("core")
    place = jnp.stack([lax.axis_index("z"), plane, lax.axis_index("det")]).astype(jnp.int32)
    flip = jnp.asarray(np.eye(128, dtype=np.float32)[::-1], dtype=BF16)
    *tables, rr, ri, br, bi, wr, wi, vr, vi, response, weight, delay = prepare(
        place, decay_rate.reshape(64, 128), frequency.reshape(64, 128), gain, member.reshape(64, 128),
        jnp.transpose(antenna, (1, 2, 0)).reshape(8, SKY), sky_delay.T,
    )
    mine = of_column(place, column, flip, *tables, rr, ri, wr, wi)
    other = lax.ppermute(mine, "core", [(0, 1), (1, 0)])
    of = (place, column, flip, *tables, rr, ri, br, bi, response)
    local0 = of_device(0, EARLY, *of)
    first, *rest = of_chip(place, mine, other, vr, vi, local0)
    got = [
        lax.ppermute(v, "x", [(x, (x + k) % 4) for x in range(4)]) for k, v in enumerate(rest, 1)
    ]
    local1 = of_device(EARLY, 8 - EARLY, *of)
    return to_peak(
        place, delay, weight, first, *got, local0, local1, response, *tables, rr, ri, br, bi
    )


def solution(mesh):
    fine = Mesh(mesh.devices.reshape(8, 4, 2, 4), ("z", "x", "core", "det"))
    time = ("z", "x", "core")
    in_specs = (P("det", time), P(), P(), P(), P(), P(), P())
    return jax.shard_map(
        shards, mesh=fine, in_specs=in_specs, out_specs=P("det", time), check_vma=False
    )
```

time: 42.6 us -> 42.2 us (level)
  local copies, waits for them, and re-layouts: 3.05 us -> 2.04 us
  Pallas kernels: 14.8 us -> 15.6 us
    ppermute x1, waiting for transfers between devices: 1 us -> 0.01 us  [shards(): other = lax.ppermute(mine, 'core', [(0, 1), (1, 0)])]
    pallas_call x4 -> x5, Pallas kernels: 12.7 us -> 13.5 us  [the longest x1 5.07 us: to_peak(): return call(peak_kernel, 3, 15, [((8, 1024), F32)], scratch)(*args)[0]]
    ppermute x3, waiting for transfers between devices: 0.01 us -> 0.82 us  [shards(): lax.ppermute(v, 'x', [(x, (x + k) % 4) for x in range(4)])]
    unnamed x16 -> x14, local copies, waits for them, and re-layouts: 1.47 us -> 0.7 us
  transfers between devices with their start and end apart: 5 -> 5, of which waited for: 2 -> 2; matrix products, arithmetic and copies ran while one was open for 1% -> 0% of each run, Pallas kernels for 15% -> 19%
where the time goes in v4:
time: 42.2 us; the launch traced here: 41.9 us
  starting transfers between devices  19.2 us (45%)
  Pallas kernels  15.6 us (37%)
  waiting for transfers between devices  4.91 us (12%)
  local copies, waits for them, and re-layouts  2.04 us (5%)
    all_to_all x1, starting transfers between devices, shards(): lax.all_to_all(sent, ('z', 'det'), 0, 0, tiled=True).reshape(256, 128)  12.2 us
    pallas_call x1, Pallas kernels, to_peak(): return call(peak_kernel, 3, 15, [((8, 1024), F32)], scratch)(*args)[0]  5.07 us
    ppermute x3, starting transfers between devices, shards(): lax.ppermute(v, 'x', [(x, (x + k) % 4) for x in range(4)])  4.9 us
    pallas_call x1, Pallas kernels, prepare(): return call(prepare_kernel, 1, 6, PREPARED, [((4, 16, 128), F32)])(*args)  4.46 us
    all_to_all x1, waiting for transfers between devices, shards(): lax.all_to_all(sent, ('z', 'det'), 0, 0, tiled=True).reshape(256, 128)  4.09 us
    pallas_call x2, Pallas kernels, of_device(): return call(kernel, 1, 11, [((count, 2, 40, 128), F32)], [])(*args)[0]  3.32 us
    ppermute x1, starting transfers between devices, shards(): other = lax.ppermute(mine, 'core', [(0, 1), (1, 0)])  2.15 us
    pallas_call x1, Pallas kernels, of_column(): call(column_kernel, 1, 10, [((2, 8, WIDE + 128), F32)], scratch)(*args)[0]  2.05 us
  transfers between devices with their start and end apart: 5, of which 2 were waited for; matrix products, arithmetic and copies ran while one was open for 0% of the time, Pallas kernels for 19%

profile of v4, /device:TPU:1, one launch (start us, length us, event | category | flops | bytes accessed | tf_op | source)
XLA Modules:
  0.0 41.9 jit_solution(17652066842368992817)
XLA Ops:
  0.0 1.3 %broadcast_in_dim.8 = f32[32,8,128]{2,1,0:T(8,128)} broadcast(f32[8,128]{1,0:T(8,128)} %bitcast.20), dimensions={1,2} | broadcast | bytes 135168 | tf_op jit(solution)/shard_map/broadcast_in_dim | solution.py:432
  1.3 0.0 copy-start.1
  1.3 0.0 copy-start.3
  1.3 0.0 copy-start.4
  1.4 12.2 %all-to-all-start = ((f32[32,8,128]{2,1,0:T(8,128)}), f32[32,8,128]{2,1,0:T(8,128)S(1)}, u32[]{:S(2)}, u32[]{:S(2)}) async-start(f32[32,8,128]{2,1,0:T(8,128)} %broadcast_in_dim.8), calls=%async_computation | async-start | bytes 262144 | tf_op jit(solution)/shard_map/all_to_all | solution.py:433
  13.5 0.0 copy-start.2
  13.5 0.1 pad_add_fusion.place
  13.6 0.0 copy-start.5
  13.6 0.0 copy-start.6
  13.6 0.0 copy-done.1
  13.6 0.0 copy-done.3
  13.6 0.0 copy-done.4
  13.6 0.6 %copy-done.2 = f32[8192]{0:T(1024)S(1)} copy-done((f32[8192]{0:T(1024)S(1)}, f32[8192]{0:T(1024)}, u32[]{:S(2)}) %copy-start.2) | copy-done | bytes 32792
  14.3 0.0 copy-done.5
  14.3 0.0 copy-done.6
  14.3 0.0 copy-start
  14.3 4.5 %shard_map.82 = (bf16[128,2048]{1,0:T(8,128)(2,1)S(1)}, bf16[128,2048]{1,0:T(8,128)(2,1)S(1)}, bf16[128,2048]{1,0:T(8,128)(2,1)S(1)}, bf16[128,2048]{1,0:T(8,128...) custom-call(s32[3]{0:T(128)S(1)} %pad_add_fusion.place, ...), custom_call_target="tpu_custom_call" | custom-call | tf_op jit(solution)/shard_map/pallas_call | solution.py:409
  18.8 4.1 %all-to-all-done = f32[32,8,128]{2,1,0:T(8,128)S(1)} async-done(((f32[32,8,128]{2,1,0:T(8,128)}), f32[32,8,128]{2,1,0:T(8,128)S(1)}, u32[]{:S(2)}, u32[]{:S(2)}) %all-to-all-start) | async-done | bytes 131104 | tf_op jit(solution)/shard_map/all_to_all | solution.py:433
  22.9 0.0 copy-done
  22.9 2.0 %shard_map.83.mine = f32[2,8,2176]{2,1,0:T(8,128)S(1)} custom-call(s32[3]{0:T(128)S(1)} %pad_add_fusion.place, f32[256,128]{1,0:T(8,128)S(1)} %bitcast.12, bf16[128,128]{1,0:T(8,128)(2,1)S(1)} %copy-done, bf16[128,2048]{1,0:T(8,128)(2,1)S(1)} %get-tuple-element.26.pr_head, bf16[128,2048]{1,0:T(8,128)(2,1)S(1)} %get-tuple-element.27.pr_tail, ...), custom_call_target="tpu_custom_call" | custom-call | tf_op jit(solution)/shard_map/pallas_call | solution.py:414
  24.9 2.1 %collective-permute-start = (f32[2,8,2176]{2,1,0:T(8,128)S(1)}, f32[2,8,2176]{2,1,0:T(8,128)S(1)}, u32[]{:S(2)}, u32[]{:S(2)}) collective-permute-start(f32[2,8,2176]{2,1,0:T(8,128)S(1)} %shard_map.83.mine), channel_id=1, source_target_pairs={{0,4},{4,0},{1,5},{5,1},{2,6},{6,2},{3,7},{7,3},{8,12},{12,8},{9,1... | collective-permute-start | bytes 417800 | tf_op jit(solution)/shard_map/ppermute | solution.py:442
  27.1 1.5 %shard_map.84.beside.local0 = f32[3,2,40,128]{3,2,1,0:T(8,128)S(1)} custom-call(s32[3]{0:T(128)S(1)} %pad_add_fusion.place, f32[256,128]{1,0:T(8,128)S(1)} %bitcast.13, bf16[128,128]{1,0:T(8,128)(2,1)S(1)} %copy-done, bf16[128,2048]{1,0:T(8,128)(2,1)S(1)} %get-tuple-element.26.pr_head, bf16[128,2048]{1,0:T(8,128)(2,1)S(1)} %get-tuple-element.27.pr_tail, ...), custom_call_target="tpu_custom_call" | custom-call | tf_op jit(solution)/shard_map/pallas_call | solution.py:423
  28.6 0.0 collective-permute-done.other
  28.6 0.7 %shard_map.85 = (f32[8,2176]{1,0:T(8,128)S(1)}, f32[8,2176]{1,0:T(8,128)S(1)}, f32[8,2176]{1,0:T(8,128)S(1)}, f32[8,2176]{1,0:T(8,128)S(1)}) custom-call(s32[3]{0:T(128)S(1)} %pad_add_fusion.place, f32[2,8,2176]{2,1,0:T(8,128)S(1)} %shard_map.83.mine, f32[2,8,2176]{2,1,0:T(8,128)S(1)} %collective-permute-done.other, f32[8,2048]{1,0:T(8,128)S(1)} %get-tuple-element.34.vr, ...), custom_call_target="tpu_custom_call" | custom-call | tf_op jit(solution)/shard_map/pallas_call | solution.py:418
  29.3 1.3 %collective-permute-start.1 = (f32[8,2176]{1,0:T(8,128)S(1)}, f32[8,2176]{1,0:T(8,128)S(1)}, u32[]{:S(2)}, u32[]{:S(2)}) collective-permute-start(f32[8,2176]{1,0:T(8,128)S(1)} %get-tuple-element.40), channel_id=1, source_target_pairs={{0,8},{8,16},{16,24},{24,0},{1,9},{9,17},{17,25},{25,1},{2,10},{10... | collective-permute-start | bytes 208904 | tf_op jit(solution)/shard_map/ppermute | solution.py:447
  30.6 2.5 %collective-permute-start.2 = (f32[8,2176]{1,0:T(8,128)S(1)}, f32[8,2176]{1,0:T(8,128)S(1)}, u32[]{:S(2)}, u32[]{:S(2)}) collective-permute-start(f32[8,2176]{1,0:T(8,128)S(1)} %get-tuple-element.41), channel_id=1, source_target_pairs={{0,16},{8,24},{16,0},{24,8},{1,17},{9,25},{17,1},{25,9},{2,18},{10... | collective-permute-start | bytes 208904 | tf_op jit(solution)/shard_map/ppermute | solution.py:447
  33.0 1.2 %collective-permute-start.3 = (f32[8,2176]{1,0:T(8,128)S(1)}, f32[8,2176]{1,0:T(8,128)S(1)}, u32[]{:S(2)}, u32[]{:S(2)}) collective-permute-start(f32[8,2176]{1,0:T(8,128)S(1)} %get-tuple-element.42), channel_id=1, source_target_pairs={{0,24},{8,0},{16,8},{24,16},{1,25},{9,1},{17,9},{25,17},{2,26},{10... | collective-permute-start | bytes 208904 | tf_op jit(solution)/shard_map/ppermute | solution.py:447
  34.2 1.8 %shard_map.86.local1 = f32[5,2,40,128]{3,2,1,0:T(8,128)S(1)} custom-call(s32[3]{0:T(128)S(1)} %pad_add_fusion.place, f32[256,128]{1,0:T(8,128)S(1)} %bitcast.14, bf16[128,128]{1,0:T(8,128)(2,1)S(1)} %copy-done, bf16[128,2048]{1,0:T(8,128)(2,1)S(1)} %get-tuple-element.26.pr_head, bf16[128,2048]{1,0:T(8,128)(2,1)S(1)} %get-tuple-element.27.pr_tail, ...), custom_call_target="tpu_custom_call" | custom-call | tf_op jit(solution)/shard_map/pallas_call | solution.py:423
  36.0 0.0 collective-permute-done.1.got1
  36.0 0.8 %collective-permute-done.2.got2 = f32[8,2176]{1,0:T(8,128)S(1)} collective-permute-done((f32[8,2176]{1,0:T(8,128)S(1)}, f32[8,2176]{1,0:T(8,128)S(1)}, u32[]{:S(2)}, u32[]{:S(2)}) %collective-permute-start.2) | collective-permute-done | bytes 69664 | tf_op jit(solution)/shard_map/ppermute | solution.py:447
  36.8 0.0 collective-permute-done.3.got3
  36.8 5.1 %shard_map.87 = f32[8,1024]{1,0:T(8,128)} custom-call(s32[3]{0:T(128)S(1)} %pad_add_fusion.place, s32[4,64]{1,0:T(4,128)S(1)} %get-tuple-element.24.delay, f32[8,64]{1,0:T(8,128)S(1)} %get-tuple-element.25.antenna, f32[8,2176]{1,0:T(8,128)S(1)} %get-tuple-element.39.got0, f32[8,2176]{1,0:T(8,128)S(1)} %collective-permute-done.1.got1, ...), custom_call_target="tpu_custom_call" | custom-call | tf_op jit(solution)/shard_map/pallas_call | solution.py:428
Async XLA Ops:
  1.3 12.3 %copy-start.1 = (f32[2,8192]{1,0:T(2,128)S(1)}, f32[2,8192]{1,0:T(2,128)}, u32[]{:S(2)}) copy-start(f32[2,8192]{1,0:T(2,128)} %gain.1) | copy-start | bytes 196612
  1.3 12.3 %copy-start.3 = (f32[8192]{0:T(1024)S(1)}, f32[8192]{0:T(1024)}, u32[]{:S(2)}) copy-start(f32[8192]{0:T(1024)} %param.10) | copy-start | bytes 98308
  1.3 12.3 %copy-start.4 = (s32[8192]{0:T(1024)S(1)}, s32[8192]{0:T(1024)}, u32[]{:S(2)}) copy-start(s32[8192]{0:T(1024)} %param.12) | copy-start | bytes 98308
  1.4 21.5 %all-to-all-start = ((f32[32,8,128]{2,1,0:T(8,128)}), f32[32,8,128]{2,1,0:T(8,128)S(1)}, u32[]{:S(2)}, u32[]{:S(2)}) async-start(f32[32,8,128]{2,1,0:T(8,128)} %broadcast_in_dim.8), calls=%async_computation | async-start | bytes 262144 | tf_op jit(solution)/shard_map/all_to_all | solution.py:433
  13.5 0.8 %copy-start.2 = (f32[8192]{0:T(1024)S(1)}, f32[8192]{0:T(1024)}, u32[]{:S(2)}) copy-start(f32[8192]{0:T(1024)} %param.9) | copy-start | bytes 98308
  13.6 0.7 %copy-start.5 = (f32[64,2,4]{0,2,1:T(4,128)S(1)}, f32[64,2,4]{0,2,1:T(4,128)}, u32[]{:S(2)}) copy-start(f32[64,2,4]{0,2,1:T(4,128)} %param.14) | copy-start | bytes 6148
  13.6 0.7 %copy-start.6 = (s32[64,4]{0,1:T(4,128)S(1)}, s32[64,4]{0,1:T(4,128)}, u32[]{:S(2)}) copy-start(s32[64,4]{0,1:T(4,128)} %param.13) | copy-start | bytes 3076
  14.3 8.5 %copy-start = (bf16[128,128]{1,0:T(8,128)(2,1)S(1)}, bf16[128,128]{1,0:T(8,128)(2,1)}, u32[]{:S(2)}) copy-start(bf16[128,128]{1,0:T(8,128)(2,1)} %constant.21.clone.flip) | copy-start | bytes 98308
  24.9 3.7 %collective-permute-start = (f32[2,8,2176]{2,1,0:T(8,128)S(1)}, f32[2,8,2176]{2,1,0:T(8,128)S(1)}, u32[]{:S(2)}, u32[]{:S(2)}) collective-permute-start(f32[2,8,2176]{2,1,0:T(8,128)S(1)} %shard_map.83.mine), channel_id=1, source_target_pairs={{0,4},{4,0},{1,5},{5,1},{2,6},{6,2},{3,7},{7,3},{8,12},{12,8},{9,1... | collective-permute-start | bytes 417800 | tf_op jit(solution)/shard_map/ppermute | solution.py:442
  29.3 6.7 %collective-permute-start.1 = (f32[8,2176]{1,0:T(8,128)S(1)}, f32[8,2176]{1,0:T(8,128)S(1)}, u32[]{:S(2)}, u32[]{:S(2)}) collective-permute-start(f32[8,2176]{1,0:T(8,128)S(1)} %get-tuple-element.40), channel_id=1, source_target_pairs={{0,8},{8,16},{16,24},{24,0},{1,9},{9,17},{17,25},{25,1},{2,10},{10... | collective-permute-start | bytes 208904 | tf_op jit(solution)/shard_map/ppermute | solution.py:447
  30.6 6.3 %collective-permute-start.2 = (f32[8,2176]{1,0:T(8,128)S(1)}, f32[8,2176]{1,0:T(8,128)S(1)}, u32[]{:S(2)}, u32[]{:S(2)}) collective-permute-start(f32[8,2176]{1,0:T(8,128)S(1)} %get-tuple-element.41), channel_id=1, source_target_pairs={{0,16},{8,24},{16,0},{24,8},{1,17},{9,25},{17,1},{25,9},{2,18},{10... | collective-permute-start | bytes 208904 | tf_op jit(solution)/shard_map/ppermute | solution.py:447
  33.0 3.8 %collective-permute-start.3 = (f32[8,2176]{1,0:T(8,128)S(1)}, f32[8,2176]{1,0:T(8,128)S(1)}, u32[]{:S(2)}, u32[]{:S(2)}) collective-permute-start(f32[8,2176]{1,0:T(8,128)S(1)} %get-tuple-element.42), channel_id=1, source_target_pairs={{0,24},{8,0},{16,8},{24,16},{1,25},{9,1},{17,9},{25,17},{2,26},{10... | collective-permute-start | bytes 208904 | tf_op jit(solution)/shard_map/ppermute | solution.py:447

commit v5 on v4

--- a/solution.py
+++ b/solution.py
@@ -1,4 +1,3 @@
-import functools
 import math
 
 import jax
@@ -22,7 +21,6 @@
 
 VMEM_LIMIT = 16 * 2**20
 UNROLL = True
-EARLY = 3
 
 
 def taylor(first, start, count):
@@ -119,7 +117,8 @@
     power = jnp.left_shift(1, lax.broadcasted_iota(jnp.int32, (16, 128), 0)).astype(F32)
     place8 = lax.broadcasted_iota(jnp.int32, (8, 128), 0)
     ahead_z = zi - 1 - (lax.broadcasted_iota(jnp.int32, (32, 128), 0) >> 2)
-    ahead_x = jnp.where(place8 < 4, 2 * place8 - 1, 2 * place8 + 2 * (xc & 1) - 10) & 7
+    core = xc & 1
+    ahead_x = jnp.where(place8 == 4, 6 * core, jnp.where(place8 == 0, 7, (2 * place8 - 1 - core) & 7))
 
     def choose(exponent, rows, re, im):
         out_re = jnp.ones(exponent.shape, F32)
@@ -188,8 +187,8 @@
 
 
 def column_kernel(
-    place, x, flip, pr_head, pr_tail, pi_head, pi_tail, row_re, row_im, wr, wi,
-    states, turned, lhs,
+    place, x, flip, pr_head, pr_tail, pi_head, pi_tail, row_re, row_im, wr, wi, vr, vi,
+    own_core, other_core, next1, next2, next3, turned, lhs,
 ):
     zi, xc = place[0], place[1]
     turned[...] = dot(jnp.concatenate(halves(x[...]), axis=0), flip[...])
@@ -222,8 +221,20 @@
             b_re, b_im,
             row_re[ROW_8192 : ROW_8192 + 1, lanes], row_im[ROW_8192 : ROW_8192 + 1, lanes],
         )
-        states[0, :, lanes] = jnp.where(upper, b_re, b_im)
-        states[1, :, lanes] = jnp.where(upper, i_re + o_re, i_im + o_im)
+        before = jnp.where(upper, b_re, b_im)
+        through = jnp.where(upper, i_re + o_re, i_im + o_im)
+        x_at, core = xc >> 1, xc & 1
+        for row, sent in enumerate((own_core, next1, next2, next3, other_core)):
+            if row == 0:
+                state = before
+            elif row == 4:
+                state = jnp.where(core == 0, through, before)
+            else:
+                state = jnp.where(x_at + row < 4, through, before)
+            turn = vi[row : row + 1, lanes]
+            sent[:, lanes] = state * vr[row : row + 1, lanes] + pltpu.roll(
+                state, 4, 0
+            ) * jnp.where(upper, -turn, turn)
         return 0
 
     lax.fori_loop(0, WIDE // 256, one_part, 0, unroll=UNROLL)
@@ -236,40 +247,20 @@
         axis=0,
     )
     halo = jnp.where(inside, halo, 0.0)
-    for p in range(2):
-        states[p, :, WIDE : WIDE + 128] = halo
-
-
-def chip_kernel(place, mine, other, vr, vi, beside, *sent):
-    del beside
-    upper = lax.broadcasted_iota(jnp.int32, (8, 256), 0) < 4
-    x, core = place[1] >> 1, place[1] & 1
-    for k in range(4):
-        target = 2 * ((x + k) & 3) + core
-        for part in range(WIDE // 256):
-            lanes = slice(256 * part, 256 * part + 256)
-            total = None
-            for states, column, row in ((mine, 2 * x + core, k), (other, 2 * x + 1 - core, 4 + k)):
-                state = states[jnp.where(column < target, 1, 0), :, lanes]
-                turn = vi[row : row + 1, lanes]
-                term = state * vr[row : row + 1, lanes] + pltpu.roll(state, 4, 0) * jnp.where(
-                    upper, -turn, turn
-                )
-                total = term if total is None else total + term
-            sent[k][:, lanes] = total
-        sent[k][:, WIDE : WIDE + 128] = other[0, :, WIDE : WIDE + 128]
+    nothing = jnp.zeros((8, 128), F32)
+    for sent, v in ((own_core, nothing), (next1, nothing), (next2, nothing), (next3, halo), (other_core, halo)):
+        sent[:, WIDE : WIDE + 128] = v
 
 
 def local_kernel(
     place, x, flip, pr_head, pr_tail, pi_head, pi_tail, row_re, row_im, block_re, block_im, response,
-    local, *, first,
+    local,
 ):
     zi = place[0]
     n_head, n_tail = halves(x[pl.ds(pl.multiple_of(32 * zi, 32), 32), :])
     x_head, x_tail = (dot(v, flip[...]).astype(BF16) for v in (n_head, n_tail))
     row8 = lax.broadcasted_iota(jnp.int32, (8, FILT), 0)
-    for k in range(local.shape[0]):
-        j = first + k
+    for j in range(WIDE // FILT):
         lanes = slice(FILT * j, FILT * j + FILT)
         l_re = dot3(x_head, x_tail, pr_head[:, lanes], pr_tail[:, lanes])
         l_im = dot3(x_head, x_tail, pi_head[:, lanes], pi_tail[:, lanes])
@@ -297,29 +288,35 @@
         own = dot3(n_head, n_tail, *halves(jnp.concatenate(matrices, axis=1)))
         f_re = full[0:40, 0:128] - full[40:80, 128:256]
         f_im = full[0:40, 128:256] + full[40:80, 0:128]
-        local[k, 0, 0:32, :], local[k, 0, 32:40, :] = f_re[0:32] + own[:, 0:128], f_re[32:40]
-        local[k, 1, 0:32, :], local[k, 1, 32:40, :] = f_im[0:32] + own[:, 128:256], f_im[32:40]
+        local[j, 0, 0:32, :], local[j, 0, 32:40, :] = f_re[0:32] + own[:, 0:128], f_re[32:40]
+        local[j, 1, 0:32, :], local[j, 1, 32:40, :] = f_im[0:32] + own[:, 128:256], f_im[32:40]
 
 
 def peak_kernel(
-    place, delay, antenna, got0, got1, got2, got3, local0, local1, response,
+    place, delay, antenna, own_core, other_core, own_sum, other_sum, local, response,
     pr_head, pr_tail, pi_head, pi_tail, row_re, row_im, block_re, block_im,
     out, grouped, shifted,
 ):
     zi, xc = place[0], place[1]
     keep = jnp.where(jnp.logical_and(zi == 7, xc == 7), 0.0, 1.0)
     ahead_lanes = slice(WIDE, WIDE + 128)
-    halo = jnp.where((xc & 1) == 0, got0[:, ahead_lanes], got3[:, ahead_lanes])
+    second = (xc & 1) == 1
+    halo = jnp.where(second, other_sum[:, ahead_lanes], other_core[:, ahead_lanes])
     h_head, h_tail = halves(response[...])
     bottom = lax.broadcasted_iota(jnp.int32, (8, 128), 0) == 7
 
     for j in range(WIDE // FILT):
         lanes = slice(FILT * j, FILT * j + FILT)
-        q = (got0[:, lanes] + got1[:, lanes]) + (got2[:, lanes] + got3[:, lanes])
         single = [
             v[row : row + 1, lanes] for row in (ROW_LEAD, ROW_1024) for v in (row_re, row_im)
         ]
-        q_re, q_im = cmul(q, pltpu.roll(q, 4, 0), *single[:2])
+        q = own_sum[:, lanes] + other_sum[:, lanes]
+        q_re, q_im = cmul(
+            q, pltpu.roll(q, 4, 0),
+            jnp.where(second, single[2], 1.0), jnp.where(second, single[3], 0.0),
+        )
+        q = own_core[:, lanes] + other_core[:, lanes]
+        q_re, q_im = cmul(q_re + q, q_im + pltpu.roll(q, 4, 0), *single[:2])
         states = [
             cmul(
                 jnp.broadcast_to(q_re[d : d + 1], (8, FILT)),
@@ -333,9 +330,8 @@
             *halves(jnp.concatenate(s_re + s_im, axis=0)),
             *lead_tables(lanes, pr_head, pr_tail, pi_head, pi_tail), 1,
         )
-        local, k = (local0, j) if j < EARLY else (local1, j - EARLY)
-        f_re = full[0:40, 0:128] - full[40:80, 128:256] + local[k, 0]
-        f_im = full[0:40, 128:256] + full[40:80, 0:128] + local[k, 1]
+        f_re = full[0:40, 0:128] - full[40:80, 128:256] + local[j, 0]
+        f_im = full[0:40, 128:256] + full[40:80, 0:128] + local[j, 1]
         for c, f in enumerate((f_re, f_im)):
             after = f[32:40] * keep
             for d in range(4):
@@ -385,14 +381,12 @@
             )
 
 
-def call(kernel, n_scalar, n_vector, shapes, scratch, n_unread=0):
-    scalar, vector, unread = (
-        pl.BlockSpec(memory_space=m) for m in (pltpu.SMEM, pltpu.VMEM, pl.ANY)
-    )
+def call(kernel, n_scalar, n_vector, shapes, scratch):
+    scalar, vector = (pl.BlockSpec(memory_space=m) for m in (pltpu.SMEM, pltpu.VMEM))
     return pl.pallas_call(
         kernel,
         out_shape=[jax.ShapeDtypeStruct(*s) for s in shapes],
-        in_specs=[scalar] * n_scalar + [vector] * n_vector + [unread] * n_unread,
+        in_specs=[scalar] * n_scalar + [vector] * n_vector,
         out_specs=[vector] * len(shapes),
         scratch_shapes=[pltpu.VMEM(*s) for s in scratch],
         compiler_params=pltpu.CompilerParams(vmem_limit_bytes=VMEM_LIMIT),
@@ -411,21 +405,16 @@
 
 def of_column(*args):
     scratch = [((512, 128), F32), ((256, 384), BF16)]
-    return call(column_kernel, 1, 10, [((2, 8, WIDE + 128), F32)], scratch)(*args)[0]
-
-
-def of_chip(*args):
-    return call(chip_kernel, 1, 4, [STATE] * 4, [], 1)(*args)
-
-
-def of_device(first, count, *args):
-    kernel = functools.partial(local_kernel, first=first)
-    return call(kernel, 1, 11, [((count, 2, 40, 128), F32)], [])(*args)[0]
+    return call(column_kernel, 1, 12, [STATE] * 5, scratch)(*args)
+
+
+def of_device(*args):
+    return call(local_kernel, 1, 11, [((8, 2, 40, 128), F32)], [])(*args)[0]
 
 
 def to_peak(*args):
     scratch = [((2, 4, 128, 128), F32), ((2, 4, 192, 128), F32)]
-    return call(peak_kernel, 3, 15, [((8, 1024), F32)], scratch)(*args)[0]
+    return call(peak_kernel, 3, 14, [((8, 1024), F32)], scratch)(*args)[0]
 
 
 def shards(strain, decay_rate, frequency, gain, member, sky_delay, antenna):
@@ -438,17 +427,20 @@
         place, decay_rate.reshape(64, 128), frequency.reshape(64, 128), gain, member.reshape(64, 128),
         jnp.transpose(antenna, (1, 2, 0)).reshape(8, SKY), sky_delay.T,
     )
-    mine = of_column(place, column, flip, *tables, rr, ri, wr, wi)
-    other = lax.ppermute(mine, "core", [(0, 1), (1, 0)])
-    of = (place, column, flip, *tables, rr, ri, br, bi, response)
-    local0 = of_device(0, EARLY, *of)
-    first, *rest = of_chip(place, mine, other, vr, vi, local0)
+    own_core, other_core, *following = of_column(
+        place, column, flip, *tables, rr, ri, wr, wi, vr, vi
+    )
     got = [
-        lax.ppermute(v, "x", [(x, (x + k) % 4) for x in range(4)]) for k, v in enumerate(rest, 1)
+        lax.ppermute(v, "x", [(x, (x + k) % 4) for x in range(4)])
+        for k, v in enumerate(following, 1)
     ]
-    local1 = of_device(EARLY, 8 - EARLY, *of)
+    local = of_device(place, column, flip, *tables, rr, ri, br, bi, response)
+    *got, local = lax.optimization_barrier((*got, local))
+    own_sum = got[0] + got[1] + got[2]
+    swap = [(0, 1), (1, 0)]
     return to_peak(
-        place, delay, weight, first, *got, local0, local1, response, *tables, rr, ri, br, bi
+        place, delay, weight, own_core, lax.ppermute(other_core, "core", swap),
+        own_sum, lax.ppermute(own_sum, "core", swap), local, response, *tables, rr, ri, br, bi,
     )
 
 

time: 42.2 us -> 42 us (level)
  Pallas kernels: 15.6 us -> 13.9 us
  starting transfers between devices: 19.2 us -> 20.6 us
    pallas_call x5 -> x3, Pallas kernels: 11.1 us -> 9.4 us  [the longest x1 5.07 us: to_peak(): return call(peak_kernel, 3, 14, [((8, 1024), F32)], scratch)(*args)[0]]
    ppermute x1 -> x2, starting transfers between devices: 2.15 us -> 3.56 us  [the longest x1 2.9 us: shards(): lax.ppermute(other_core, 'core', swap)]
    ppermute x1 -> x2, waiting for transfers between devices: 0.01 us -> 0.91 us  [the longest x1 0.9 us: shards(): lax.ppermute(own_sum, 'core', swap)]
    ppermute x3, waiting for transfers between devices: 0.82 us -> 0.01 us  [shards(): lax.ppermute(v, 'x', [(x, (x + k) % 4) for x in range(4)])]
  transfers between devices with their start and end apart: 5 -> 6, of which waited for: 2 -> 2; matrix products, arithmetic and copies ran while one was open for 0% -> 0% of each run, Pallas kernels for 19% -> 16%
where the time goes in v5:
time: 42 us; the launch traced here: 41.7 us
  starting transfers between devices  20.6 us (49%)
  Pallas kernels  13.9 us (33%)
  waiting for transfers between devices  5 us (12%)
  local copies, waits for them, and re-layouts  2.05 us (5%)
    all_to_all x1, starting transfers between devices, shards(): lax.all_to_all(sent, ('z', 'det'), 0, 0, tiled=True).reshape(256, 128)  12.2 us
    pallas_call x1, Pallas kernels, to_peak(): return call(peak_kernel, 3, 14, [((8, 1024), F32)], scratch)(*args)[0]  5.07 us
    ppermute x3, starting transfers between devices, shards(): lax.ppermute(v, 'x', [(x, (x + k) % 4) for x in range(4)])  4.89 us
    pallas_call x1, Pallas kernels, prepare(): return call(prepare_kernel, 1, 6, PREPARED, [((4, 16, 128), F32)])(*args)  4.46 us
    all_to_all x1, waiting for transfers between devices, shards(): lax.all_to_all(sent, ('z', 'det'), 0, 0, tiled=True).reshape(256, 128)  4.09 us
    ppermute x1, starting transfers between devices, shards(): lax.ppermute(other_core, 'core', swap)  2.9 us
    pallas_call x1, Pallas kernels, of_device(): return call(local_kernel, 1, 11, [((8, 2, 40, 128), F32)], [])(*args)[0]  2.26 us
    pallas_call x1, Pallas kernels, of_column(): return call(column_kernel, 1, 12, [STATE] * 5, scratch)(*args)  2.07 us
  transfers between devices with their start and end apart: 6, of which 2 were waited for; matrix products, arithmetic and copies ran while one was open for 0% of the time, Pallas kernels for 16%

profile of v5, /device:TPU:1, one launch (start us, length us, event | category | flops | bytes accessed | tf_op | source)
XLA Modules:
  0.0 41.7 jit_solution(2415751075041605710)
XLA Ops:
  0.0 1.4 %broadcast_in_dim.8 = f32[32,8,128]{2,1,0:T(8,128)} broadcast(f32[8,128]{1,0:T(8,128)} %bitcast.19), dimensions={1,2} | broadcast | bytes 135168 | tf_op jit(solution)/shard_map/broadcast_in_dim | solution.py:421
  1.4 0.0 copy-start.1
  1.4 0.0 copy-start.3
  1.4 0.0 copy-start.4
  1.4 12.2 %all-to-all-start = ((f32[32,8,128]{2,1,0:T(8,128)}), f32[32,8,128]{2,1,0:T(8,128)S(1)}, u32[]{:S(2)}, u32[]{:S(2)}) async-start(f32[32,8,128]{2,1,0:T(8,128)} %broadcast_in_dim.8), calls=%async_computation | async-start | bytes 262144 | tf_op jit(solution)/shard_map/all_to_all | solution.py:422
  13.5 0.0 copy-start.2
  13.6 0.1 pad_add_fusion.place
  13.6 0.0 copy-start.5
  13.6 0.0 copy-start.6
  13.6 0.0 copy-done.1
  13.6 0.0 copy-done.3
  13.6 0.0 copy-done.4
  13.7 0.6 %copy-done.2 = f32[8192]{0:T(1024)S(1)} copy-done((f32[8192]{0:T(1024)S(1)}, f32[8192]{0:T(1024)}, u32[]{:S(2)}) %copy-start.2) | copy-done | bytes 32792
  14.3 0.0 copy-done.5
  14.3 0.0 copy-done.6
  14.3 0.0 copy-start
  14.3 4.5 %shard_map.82 = (bf16[128,2048]{1,0:T(8,128)(2,1)S(1)}, bf16[128,2048]{1,0:T(8,128)(2,1)S(1)}, bf16[128,2048]{1,0:T(8,128)(2,1)S(1)}, bf16[128,2048]{1,0:T(8,128...) custom-call(s32[3]{0:T(128)S(1)} %pad_add_fusion.place, ...), custom_call_target="tpu_custom_call" | custom-call | tf_op jit(solution)/shard_map/pallas_call | solution.py:403
  18.8 4.1 %all-to-all-done = f32[32,8,128]{2,1,0:T(8,128)S(1)} async-done(((f32[32,8,128]{2,1,0:T(8,128)}), f32[32,8,128]{2,1,0:T(8,128)S(1)}, u32[]{:S(2)}, u32[]{:S(2)}) %all-to-all-start) | async-done | bytes 131104 | tf_op jit(solution)/shard_map/all_to_all | solution.py:422
  22.9 0.0 copy-done
  22.9 2.1 %shard_map.83 = (f32[8,2176]{1,0:T(8,128)S(1)}, f32[8,2176]{1,0:T(8,128)S(1)}, f32[8,2176]{1,0:T(8,128)S(1)}, f32[8,2176]{1,0:T(8,128)S(1)}, f32[8,2176]{1,0:T(8,128)S(1)}) custom-call(s32[3]{0:T(128)S(1)} %pad_add_fusion.place, f32[256,128]{1,0:T(8,128)S(1)} %bitcast.12, bf16[128,128]{1,0:T(8,128)(2,1)S(1)} %copy-done, ...), custom_call_target="tpu_custom_call" | custom-call | tf_op jit(solution)/shard_map/pallas_call | solution.py:408
  25.0 1.3 %collective-permute-start.1 = (f32[8,2176]{1,0:T(8,128)S(1)}, f32[8,2176]{1,0:T(8,128)S(1)}, u32[]{:S(2)}, u32[]{:S(2)}) collective-permute-start(f32[8,2176]{1,0:T(8,128)S(1)} %get-tuple-element.43), channel_id=1, source_target_pairs={{0,8},{8,16},{16,24},{24,0},{1,9},{9,17},{17,25},{25,1},{2,10},{10... | collective-permute-start | bytes 208904 | tf_op jit(solution)/shard_map/ppermute | solution.py:434
  26.2 2.4 %collective-permute-start.2 = (f32[8,2176]{1,0:T(8,128)S(1)}, f32[8,2176]{1,0:T(8,128)S(1)}, u32[]{:S(2)}, u32[]{:S(2)}) collective-permute-start(f32[8,2176]{1,0:T(8,128)S(1)} %get-tuple-element.44), channel_id=1, source_target_pairs={{0,16},{8,24},{16,0},{24,8},{1,17},{9,25},{17,1},{25,9},{2,18},{10... | collective-permute-start | bytes 208904 | tf_op jit(solution)/shard_map/ppermute | solution.py:434
  28.7 1.2 %collective-permute-start.3 = (f32[8,2176]{1,0:T(8,128)S(1)}, f32[8,2176]{1,0:T(8,128)S(1)}, u32[]{:S(2)}, u32[]{:S(2)}) collective-permute-start(f32[8,2176]{1,0:T(8,128)S(1)} %get-tuple-element.45), channel_id=1, source_target_pairs={{0,24},{8,0},{16,8},{24,16},{1,25},{9,1},{17,9},{25,17},{2,26},{10... | collective-permute-start | bytes 208904 | tf_op jit(solution)/shard_map/ppermute | solution.py:434
  29.9 2.9 %collective-permute-start = (f32[8,2176]{1,0:T(8,128)S(1)}, f32[8,2176]{1,0:T(8,128)S(1)}, u32[]{:S(2)}, u32[]{:S(2)}) collective-permute-start(f32[8,2176]{1,0:T(8,128)S(1)} %get-tuple-element.42), channel_id=1, source_target_pairs={{0,4},{4,0},{1,5},{5,1},{2,6},{6,2},{3,7},{7,3},{8,12},{12,8},{9,1... | collective-permute-start | bytes 208904 | tf_op jit(solution)/shard_map/ppermute | solution.py:442
  32.8 2.3 %shard_map.84.local = f32[8,2,40,128]{3,2,1,0:T(8,128)S(1)} custom-call(s32[3]{0:T(128)S(1)} %pad_add_fusion.place, f32[256,128]{1,0:T(8,128)S(1)} %bitcast.13, bf16[128,128]{1,0:T(8,128)(2,1)S(1)} %copy-done, bf16[128,2048]{1,0:T(8,128)(2,1)S(1)} %get-tuple-element.31.pr_head, bf16[128,2048]{1,0:T(8,128)(2,1)S(1)} %get-tuple-element.32.pr_tail, ...), custom_call_target="tpu_custom_call" | custom-call | tf_op jit(solution)/shard_map/pallas_call | solution.py:412
  35.0 0.0 collective-permute-done.1
  35.0 0.0 collective-permute-done.2
  35.0 0.0 collective-permute-done.3
  35.1 0.7 %collective-permute-start.4 = (f32[8,2176]{1,0:T(8,128)S(1)}, f32[8,2176]{1,0:T(8,128)S(1)}, u32[]{:S(2)}, u32[]{:S(2)}) collective-permute-start(f32[8,2176]{1,0:T(8,128)S(1)} %add_add_fusion.own_sum), channel_id=1, source_target_pairs={{0,4},{4,0},{1,5},{5,1},{2,6},{6,2},{3,7},{7,3},{8,12},{12,8},{9,1... | collective-permute-start | bytes 208904 | tf_op jit(solution)/shard_map/ppermute | solution.py:443
  35.7 0.0 collective-permute-done.other_core
  35.7 0.9 %collective-permute-done.4.other_sum = f32[8,2176]{1,0:T(8,128)S(1)} collective-permute-done((f32[8,2176]{1,0:T(8,128)S(1)}, f32[8,2176]{1,0:T(8,128)S(1)}, u32[]{:S(2)}, u32[]{:S(2)}) %collective-permute-start.4) | collective-permute-done | bytes 69664 | tf_op jit(solution)/shard_map/ppermute | solution.py:443
  36.6 5.1 %shard_map.85 = f32[8,1024]{1,0:T(8,128)} custom-call(s32[3]{0:T(128)S(1)} %pad_add_fusion.place, s32[4,64]{1,0:T(4,128)S(1)} %get-tuple-element.29.delay, f32[8,64]{1,0:T(8,128)S(1)} %get-tuple-element.30.antenna, f32[8,2176]{1,0:T(8,128)S(1)} %get-tuple-element.41.own_core, f32[8,2176]{1,0:T(8,128)S(1)} %collective-permute-done.other_core, ...), custom_call_target="tpu_custom_call" | custom-call | tf_op jit(solution)/shard_map/pallas_call | solution.py:417
  (1 shorter events, 0.0 us)
Async XLA Ops:
  1.4 12.3 %copy-start.1 = (f32[2,8192]{1,0:T(2,128)S(1)}, f32[2,8192]{1,0:T(2,128)}, u32[]{:S(2)}) copy-start(f32[2,8192]{1,0:T(2,128)} %gain.1) | copy-start | bytes 196612
  1.4 12.3 %copy-start.3 = (f32[8192]{0:T(1024)S(1)}, f32[8192]{0:T(1024)}, u32[]{:S(2)}) copy-start(f32[8192]{0:T(1024)} %param.10) | copy-start | bytes 98308
  1.4 12.3 %copy-start.4 = (s32[8192]{0:T(1024)S(1)}, s32[8192]{0:T(1024)}, u32[]{:S(2)}) copy-start(s32[8192]{0:T(1024)} %param.12) | copy-start | bytes 98308
  1.4 21.5 %all-to-all-start = ((f32[32,8,128]{2,1,0:T(8,128)}), f32[32,8,128]{2,1,0:T(8,128)S(1)}, u32[]{:S(2)}, u32[]{:S(2)}) async-start(f32[32,8,128]{2,1,0:T(8,128)} %broadcast_in_dim.8), calls=%async_computation | async-start | bytes 262144 | tf_op jit(solution)/shard_map/all_to_all | solution.py:422
  13.5 0.8 %copy-start.2 = (f32[8192]{0:T(1024)S(1)}, f32[8192]{0:T(1024)}, u32[]{:S(2)}) copy-start(f32[8192]{0:T(1024)} %param.9) | copy-start | bytes 98308
  13.6 0.7 %copy-start.5 = (f32[64,2,4]{0,2,1:T(4,128)S(1)}, f32[64,2,4]{0,2,1:T(4,128)}, u32[]{:S(2)}) copy-start(f32[64,2,4]{0,2,1:T(4,128)} %param.14) | copy-start | bytes 6148
  13.6 0.7 %copy-start.6 = (s32[64,4]{0,1:T(4,128)S(1)}, s32[64,4]{0,1:T(4,128)}, u32[]{:S(2)}) copy-start(s32[64,4]{0,1:T(4,128)} %param.13) | copy-start | bytes 3076
  14.3 8.5 %copy-start = (bf16[128,128]{1,0:T(8,128)(2,1)S(1)}, bf16[128,128]{1,0:T(8,128)(2,1)}, u32[]{:S(2)}) copy-start(bf16[128,128]{1,0:T(8,128)(2,1)} %constant.21.clone.flip) | copy-start | bytes 98308
  25.0 10.1 %collective-permute-start.1 = (f32[8,2176]{1,0:T(8,128)S(1)}, f32[8,2176]{1,0:T(8,128)S(1)}, u32[]{:S(2)}, u32[]{:S(2)}) collective-permute-start(f32[8,2176]{1,0:T(8,128)S(1)} %get-tuple-element.43), channel_id=1, source_target_pairs={{0,8},{8,16},{16,24},{24,0},{1,9},{9,17},{17,25},{25,1},{2,10},{10... | collective-permute-start | bytes 208904 | tf_op jit(solution)/shard_map/ppermute | solution.py:434
  26.2 8.8 %collective-permute-start.2 = (f32[8,2176]{1,0:T(8,128)S(1)}, f32[8,2176]{1,0:T(8,128)S(1)}, u32[]{:S(2)}, u32[]{:S(2)}) collective-permute-start(f32[8,2176]{1,0:T(8,128)S(1)} %get-tuple-element.44), channel_id=1, source_target_pairs={{0,16},{8,24},{16,0},{24,8},{1,17},{9,25},{17,1},{25,9},{2,18},{10... | collective-permute-start | bytes 208904 | tf_op jit(solution)/shard_map/ppermute | solution.py:434
  28.7 6.3 %collective-permute-start.3 = (f32[8,2176]{1,0:T(8,128)S(1)}, f32[8,2176]{1,0:T(8,128)S(1)}, u32[]{:S(2)}, u32[]{:S(2)}) collective-permute-start(f32[8,2176]{1,0:T(8,128)S(1)} %get-tuple-element.45), channel_id=1, source_target_pairs={{0,24},{8,0},{16,8},{24,16},{1,25},{9,1},{17,9},{25,17},{2,26},{10... | collective-permute-start | bytes 208904 | tf_op jit(solution)/shard_map/ppermute | solution.py:434
  29.9 5.9 %collective-permute-start = (f32[8,2176]{1,0:T(8,128)S(1)}, f32[8,2176]{1,0:T(8,128)S(1)}, u32[]{:S(2)}, u32[]{:S(2)}) collective-permute-start(f32[8,2176]{1,0:T(8,128)S(1)} %get-tuple-element.42), channel_id=1, source_target_pairs={{0,4},{4,0},{1,5},{5,1},{2,6},{6,2},{3,7},{7,3},{8,12},{12,8},{9,1... | collective-permute-start | bytes 208904 | tf_op jit(solution)/shard_map/ppermute | solution.py:442
  35.1 1.6 %collective-permute-start.4 = (f32[8,2176]{1,0:T(8,128)S(1)}, f32[8,2176]{1,0:T(8,128)S(1)}, u32[]{:S(2)}, u32[]{:S(2)}) collective-permute-start(f32[8,2176]{1,0:T(8,128)S(1)} %add_add_fusion.own_sum), channel_id=1, source_target_pairs={{0,4},{4,0},{1,5},{5,1},{2,6},{6,2},{3,7},{7,3},{8,12},{12,8},{9,1... | collective-permute-start | bytes 208904 | tf_op jit(solution)/shard_map/ppermute | solution.py:443

commit v6 on v5

--- a/solution.py
+++ b/solution.py
@@ -20,7 +20,6 @@
 ROW_128, ROW_1024, ROW_8192, ROW_GAIN, ROW_LEAD = 0, 1, 2, 3, 4
 
 VMEM_LIMIT = 16 * 2**20
-UNROLL = True
 
 
 def taylor(first, start, count):
@@ -166,7 +165,7 @@
         pi_head[:, lanes], pi_tail[:, lanes] = halves(t_im)
         return 0
 
-    lax.fori_loop(0, WIDE // 128, one_chunk, 0)
+    lax.fori_loop(0, WIDE // 128, one_chunk, 0, unroll=4)
 
     for j in range(WIDE // FILT):
         lanes = slice(FILT * j, FILT * j + FILT)
@@ -188,42 +187,65 @@
 
 def column_kernel(
     place, x, flip, pr_head, pr_tail, pi_head, pi_tail, row_re, row_im, wr, wi, vr, vi,
-    own_core, other_core, next1, next2, next3, turned, lhs,
+    own_core, other_core, next1, next2, next3, turned, lhs, total,
 ):
     zi, xc = place[0], place[1]
-    turned[...] = dot(jnp.concatenate(halves(x[...]), axis=0), flip[...])
-    for q in range(8):
-        rows = [turned[pl.ds(256 * h + 7 - q, 32, stride=8), :].astype(BF16) for h in (0, 1, 0)]
-        lhs[32 * q : 32 * q + 32, :] = jnp.concatenate(rows, axis=1)
-    own = (lax.broadcasted_iota(jnp.int32, (32, 256), 0) >> 2) == zi
+    turned[0:512, :] = dot(jnp.concatenate(halves(x[...]), axis=0), flip[...])
+    for half in range(2):
+        for q in range(8):
+            rows = [
+                turned[pl.ds(256 * h + 128 * half + 7 - q, 16, stride=8), :].astype(BF16)
+                for h in (0, 1, 0)
+            ]
+            at = 128 * half + 16 * q
+            lhs[at : at + 16, :] = jnp.concatenate(rows, axis=1)
+    shard_of = lax.broadcasted_iota(jnp.int32, (16, 256), 0) >> 2
     upper = lax.broadcasted_iota(jnp.int32, (8, 256), 0) < 4
+    x_at, core = xc >> 1, xc & 1
 
     def over_shards(v):
-        total = (v[0:8] + v[8:16]) + (v[16:24] + v[24:32])
+        total = v[0:8] + v[8:16]
         return total + pltpu.roll(total, 4, 0)
 
-    def one_part(part, _):
-        lanes = pl.ds(pl.multiple_of(part * 256, 256), 256)
+    def of_half(half, lanes):
         e_re, e_im = (
-            dot(lhs[...], jnp.concatenate([head[:, lanes], head[:, lanes], tail[:, lanes]], axis=0))
+            dot(
+                lhs[128 * half : 128 * half + 128, :],
+                jnp.concatenate([head[:, lanes], head[:, lanes], tail[:, lanes]], axis=0),
+            )
             for head, tail in ((pr_head, pr_tail), (pi_head, pi_tail))
         )
         step_re = row_re[ROW_128 : ROW_128 + 1, lanes]
         step_im = row_im[ROW_128 : ROW_128 + 1, lanes]
-        s_re, s_im = e_re[224:256], e_im[224:256]
+        s_re, s_im = e_re[112:128], e_im[112:128]
         for q in range(6, -1, -1):
             s_re, s_im = cmul(s_re, s_im, step_re, step_im)
-            s_re = s_re + e_re[32 * q : 32 * q + 32]
-            s_im = s_im + e_im[32 * q : 32 * q + 32]
-        b_re, b_im = (over_shards(v) for v in cmul(s_re, s_im, wr[:, lanes], wi[:, lanes]))
-        o_re, o_im = (over_shards(jnp.where(own, v, 0.0)) for v in (s_re, s_im))
+            s_re = s_re + e_re[16 * q : 16 * q + 16]
+            s_im = s_im + e_im[16 * q : 16 * q + 16]
+        rows = slice(16 * half, 16 * half + 16)
+        weighted = cmul(s_re, s_im, wr[rows, lanes], wi[rows, lanes])
+        own = [jnp.where(shard_of == zi - 4 * half, v, 0.0) for v in (s_re, s_im)]
+        return [over_shards(v) for v in (*weighted, *own)]
+
+    parts = [slice(256 * part, 256 * part + 256) for part in range(WIDE // 256)]
+    for lanes in parts:
+        for k, v in enumerate(of_half(0, lanes)):
+            total[k, :, lanes] = v
+
+    @pl.when(zi >= 4)
+    def _():
+        for lanes in parts:
+            for k, v in enumerate(of_half(1, lanes)):
+                total[k, :, lanes] = total[k, :, lanes] + v
+
+    for lanes in parts:
+        b_re, b_im, o_re, o_im = (total[k, :, lanes] for k in range(4))
         i_re, i_im = cmul(
             b_re, b_im,
             row_re[ROW_8192 : ROW_8192 + 1, lanes], row_im[ROW_8192 : ROW_8192 + 1, lanes],
         )
         before = jnp.where(upper, b_re, b_im)
         through = jnp.where(upper, i_re + o_re, i_im + o_im)
-        x_at, core = xc >> 1, xc & 1
         for row, sent in enumerate((own_core, next1, next2, next3, other_core)):
             if row == 0:
                 state = before
@@ -235,9 +257,6 @@
             sent[:, lanes] = state * vr[row : row + 1, lanes] + pltpu.roll(
                 state, 4, 0
             ) * jnp.where(upper, -turn, turn)
-        return 0
-
-    lax.fori_loop(0, WIDE // 256, one_part, 0, unroll=UNROLL)
 
     shard = jnp.where(xc == 0, zi + 1, zi)
     inside = shard < 8
@@ -350,7 +369,7 @@
     early = lax.broadcasted_iota(jnp.int32, (64, 128), 1) < 64
     for c in range(2):
         for d in range(4):
-            t = grouped[c, d].T
+            t = grouped[c, d, 0:128, :].T
             top, low = t[0:64], t[64:128]
             shifted[c, d, 0:64, :] = jnp.where(early, top, pltpu.roll(low, 64, 1))
             shifted[c, d, 64:128, :] = jnp.where(early, low, top)
@@ -404,7 +423,7 @@
 
 
 def of_column(*args):
-    scratch = [((512, 128), F32), ((256, 384), BF16)]
+    scratch = [((520, 128), F32), ((256, 384), BF16), ((4, 8, WIDE), F32)]
     return call(column_kernel, 1, 12, [STATE] * 5, scratch)(*args)
 
 
@@ -413,7 +432,7 @@
 
 
 def to_peak(*args):
-    scratch = [((2, 4, 128, 128), F32), ((2, 4, 192, 128), F32)]
+    scratch = [((2, 4, 136, 128), F32), ((2, 4, 192, 128), F32)]
     return call(peak_kernel, 3, 14, [((8, 1024), F32)], scratch)(*args)[0]
 
 

time: 42 us -> 41.5 us (0.988)
  Pallas kernels: 13.9 us -> 13.2 us
    pallas_call x1, Pallas kernels: 2.07 us -> 1.57 us  [of_column(): return call(column_kernel, 1, 12, [STATE] * 5, scratch)(*args)]
where the time goes in v6:
time: 41.5 us; the launch traced here: 41.2 us
  starting transfers between devices  20.6 us (50%)
  Pallas kernels  13.2 us (32%)
  waiting for transfers between devices  5.21 us (13%)
  local copies, waits for them, and re-layouts  2.05 us (5%)
    all_to_all x1, starting transfers between devices, shards(): lax.all_to_all(sent, ('z', 'det'), 0, 0, tiled=True).reshape(256, 128)  12.2 us
    pallas_call x1, Pallas kernels, to_peak(): return call(peak_kernel, 3, 14, [((8, 1024), F32)], scratch)(*args)[0]  5.06 us
    ppermute x3, starting transfers between devices, shards(): lax.ppermute(v, 'x', [(x, (x + k) % 4) for x in range(4)])  4.9 us
    all_to_all x1, waiting for transfers between devices, shards(): lax.all_to_all(sent, ('z', 'det'), 0, 0, tiled=True).reshape(256, 128)  4.29 us
    pallas_call x1, Pallas kernels, prepare(): return call(prepare_kernel, 1, 6, PREPARED, [((4, 16, 128), F32)])(*args)  4.25 us
    ppermute x1, starting transfers between devices, shards(): lax.ppermute(other_core, 'core', swap)  2.9 us
    pallas_call x1, Pallas kernels, of_device(): return call(local_kernel, 1, 11, [((8, 2, 40, 128), F32)], [])(*args)[0]  2.26 us
    pallas_call x1, Pallas kernels, of_column(): return call(column_kernel, 1, 12, [STATE] * 5, scratch)(*args)  1.57 us
  transfers between devices with their start and end apart: 6, of which 2 were waited for; matrix products, arithmetic and copies ran while one was open for 0% of the time, Pallas kernels for 16%

profile of v6, /device:TPU:1, one launch (start us, length us, event | category | flops | bytes accessed | tf_op | source)
XLA Modules:
  0.0 41.2 jit_solution(18121664287371167400)
XLA Ops:
  0.0 1.4 %broadcast_in_dim.8 = f32[32,8,128]{2,1,0:T(8,128)} broadcast(f32[8,128]{1,0:T(8,128)} %bitcast.19), dimensions={1,2} | broadcast | bytes 135168 | tf_op jit(solution)/shard_map/broadcast_in_dim | solution.py:440
  1.4 0.0 copy-start.1
  1.4 0.0 copy-start.3
  1.4 0.0 copy-start.4
  1.4 12.2 %all-to-all-start = ((f32[32,8,128]{2,1,0:T(8,128)}), f32[32,8,128]{2,1,0:T(8,128)S(1)}, u32[]{:S(2)}, u32[]{:S(2)}) async-start(f32[32,8,128]{2,1,0:T(8,128)} %broadcast_in_dim.8), calls=%async_computation | async-start | bytes 262144 | tf_op jit(solution)/shard_map/all_to_all | solution.py:441
  13.5 0.0 copy-start.2
  13.6 0.1 pad_add_fusion.place
  13.6 0.0 copy-start.5
  13.6 0.0 copy-start.6
  13.6 0.0 copy-done.1
  13.6 0.0 copy-done.3
  13.6 0.0 copy-done.4
  13.7 0.6 %copy-done.2 = f32[8192]{0:T(1024)S(1)} copy-done((f32[8192]{0:T(1024)S(1)}, f32[8192]{0:T(1024)}, u32[]{:S(2)}) %copy-start.2) | copy-done | bytes 32792
  14.3 0.0 copy-done.5
  14.3 0.0 copy-done.6
  14.3 0.0 copy-start
  14.3 4.3 %shard_map.82 = (bf16[128,2048]{1,0:T(8,128)(2,1)S(1)}, bf16[128,2048]{1,0:T(8,128)(2,1)S(1)}, bf16[128,2048]{1,0:T(8,128)(2,1)S(1)}, bf16[128,2048]{1,0:T(8,128...) custom-call(s32[3]{0:T(128)S(1)} %pad_add_fusion.place, ...), custom_call_target="tpu_custom_call" | custom-call | tf_op jit(solution)/shard_map/pallas_call | solution.py:422
  18.6 4.3 %all-to-all-done = f32[32,8,128]{2,1,0:T(8,128)S(1)} async-done(((f32[32,8,128]{2,1,0:T(8,128)}), f32[32,8,128]{2,1,0:T(8,128)S(1)}, u32[]{:S(2)}, u32[]{:S(2)}) %all-to-all-start) | async-done | bytes 131104 | tf_op jit(solution)/shard_map/all_to_all | solution.py:441
  22.9 0.0 copy-done
  22.9 1.6 %shard_map.83 = (f32[8,2176]{1,0:T(8,128)S(1)}, f32[8,2176]{1,0:T(8,128)S(1)}, f32[8,2176]{1,0:T(8,128)S(1)}, f32[8,2176]{1,0:T(8,128)S(1)}, f32[8,2176]{1,0:T(8,128)S(1)}) custom-call(s32[3]{0:T(128)S(1)} %pad_add_fusion.place, f32[256,128]{1,0:T(8,128)S(1)} %bitcast.12, bf16[128,128]{1,0:T(8,128)(2,1)S(1)} %copy-done, ...), custom_call_target="tpu_custom_call" | custom-call | tf_op jit(solution)/shard_map/pallas_call | solution.py:427
  24.5 1.3 %collective-permute-start.1 = (f32[8,2176]{1,0:T(8,128)S(1)}, f32[8,2176]{1,0:T(8,128)S(1)}, u32[]{:S(2)}, u32[]{:S(2)}) collective-permute-start(f32[8,2176]{1,0:T(8,128)S(1)} %get-tuple-element.43), channel_id=1, source_target_pairs={{0,8},{8,16},{16,24},{24,0},{1,9},{9,17},{17,25},{25,1},{2,10},{10... | collective-permute-start | bytes 208904 | tf_op jit(solution)/shard_map/ppermute | solution.py:453
  25.8 2.4 %collective-permute-start.2 = (f32[8,2176]{1,0:T(8,128)S(1)}, f32[8,2176]{1,0:T(8,128)S(1)}, u32[]{:S(2)}, u32[]{:S(2)}) collective-permute-start(f32[8,2176]{1,0:T(8,128)S(1)} %get-tuple-element.44), channel_id=1, source_target_pairs={{0,16},{8,24},{16,0},{24,8},{1,17},{9,25},{17,1},{25,9},{2,18},{10... | collective-permute-start | bytes 208904 | tf_op jit(solution)/shard_map/ppermute | solution.py:453
  28.2 1.2 %collective-permute-start.3 = (f32[8,2176]{1,0:T(8,128)S(1)}, f32[8,2176]{1,0:T(8,128)S(1)}, u32[]{:S(2)}, u32[]{:S(2)}) collective-permute-start(f32[8,2176]{1,0:T(8,128)S(1)} %get-tuple-element.45), channel_id=1, source_target_pairs={{0,24},{8,0},{16,8},{24,16},{1,25},{9,1},{17,9},{25,17},{2,26},{10... | collective-permute-start | bytes 208904 | tf_op jit(solution)/shard_map/ppermute | solution.py:453
  29.4 2.9 %collective-permute-start = (f32[8,2176]{1,0:T(8,128)S(1)}, f32[8,2176]{1,0:T(8,128)S(1)}, u32[]{:S(2)}, u32[]{:S(2)}) collective-permute-start(f32[8,2176]{1,0:T(8,128)S(1)} %get-tuple-element.42), channel_id=1, source_target_pairs={{0,4},{4,0},{1,5},{5,1},{2,6},{6,2},{3,7},{7,3},{8,12},{12,8},{9,1... | collective-permute-start | bytes 208904 | tf_op jit(solution)/shard_map/ppermute | solution.py:461
  32.3 2.3 %shard_map.84.local = f32[8,2,40,128]{3,2,1,0:T(8,128)S(1)} custom-call(s32[3]{0:T(128)S(1)} %pad_add_fusion.place, f32[256,128]{1,0:T(8,128)S(1)} %bitcast.13, bf16[128,128]{1,0:T(8,128)(2,1)S(1)} %copy-done, bf16[128,2048]{1,0:T(8,128)(2,1)S(1)} %get-tuple-element.31.pr_head, bf16[128,2048]{1,0:T(8,128)(2,1)S(1)} %get-tuple-element.32.pr_tail, ...), custom_call_target="tpu_custom_call" | custom-call | tf_op jit(solution)/shard_map/pallas_call | solution.py:431
  34.5 0.0 collective-permute-done.1
  34.5 0.0 collective-permute-done.2
  34.6 0.0 collective-permute-done.3
  34.6 0.7 %collective-permute-start.4 = (f32[8,2176]{1,0:T(8,128)S(1)}, f32[8,2176]{1,0:T(8,128)S(1)}, u32[]{:S(2)}, u32[]{:S(2)}) collective-permute-start(f32[8,2176]{1,0:T(8,128)S(1)} %add_add_fusion.own_sum), channel_id=1, source_target_pairs={{0,4},{4,0},{1,5},{5,1},{2,6},{6,2},{3,7},{7,3},{8,12},{12,8},{9,1... | collective-permute-start | bytes 208904 | tf_op jit(solution)/shard_map/ppermute | solution.py:462
  35.2 0.0 collective-permute-done.other_core
  35.2 0.9 %collective-permute-done.4.other_sum = f32[8,2176]{1,0:T(8,128)S(1)} collective-permute-done((f32[8,2176]{1,0:T(8,128)S(1)}, f32[8,2176]{1,0:T(8,128)S(1)}, u32[]{:S(2)}, u32[]{:S(2)}) %collective-permute-start.4) | collective-permute-done | bytes 69664 | tf_op jit(solution)/shard_map/ppermute | solution.py:462
  36.1 5.1 %shard_map.85 = f32[8,1024]{1,0:T(8,128)} custom-call(s32[3]{0:T(128)S(1)} %pad_add_fusion.place, s32[4,64]{1,0:T(4,128)S(1)} %get-tuple-element.29.delay, f32[8,64]{1,0:T(8,128)S(1)} %get-tuple-element.30.antenna, f32[8,2176]{1,0:T(8,128)S(1)} %get-tuple-element.41.own_core, f32[8,2176]{1,0:T(8,128)S(1)} %collective-permute-done.other_core, ...), custom_call_target="tpu_custom_call" | custom-call | tf_op jit(solution)/shard_map/pallas_call | solution.py:436
  (1 shorter events, 0.0 us)
Async XLA Ops:
  1.4 12.3 %copy-start.1 = (f32[2,8192]{1,0:T(2,128)S(1)}, f32[2,8192]{1,0:T(2,128)}, u32[]{:S(2)}) copy-start(f32[2,8192]{1,0:T(2,128)} %gain.1) | copy-start | bytes 196612
  1.4 12.3 %copy-start.3 = (f32[8192]{0:T(1024)S(1)}, f32[8192]{0:T(1024)}, u32[]{:S(2)}) copy-start(f32[8192]{0:T(1024)} %param.10) | copy-start | bytes 98308
  1.4 12.3 %copy-start.4 = (s32[8192]{0:T(1024)S(1)}, s32[8192]{0:T(1024)}, u32[]{:S(2)}) copy-start(s32[8192]{0:T(1024)} %param.12) | copy-start | bytes 98308
  1.4 21.5 %all-to-all-start = ((f32[32,8,128]{2,1,0:T(8,128)}), f32[32,8,128]{2,1,0:T(8,128)S(1)}, u32[]{:S(2)}, u32[]{:S(2)}) async-start(f32[32,8,128]{2,1,0:T(8,128)} %broadcast_in_dim.8), calls=%async_computation | async-start | bytes 262144 | tf_op jit(solution)/shard_map/all_to_all | solution.py:441
  13.5 0.8 %copy-start.2 = (f32[8192]{0:T(1024)S(1)}, f32[8192]{0:T(1024)}, u32[]{:S(2)}) copy-start(f32[8192]{0:T(1024)} %param.9) | copy-start | bytes 98308
  13.6 0.7 %copy-start.5 = (f32[64,2,4]{0,2,1:T(4,128)S(1)}, f32[64,2,4]{0,2,1:T(4,128)}, u32[]{:S(2)}) copy-start(f32[64,2,4]{0,2,1:T(4,128)} %param.14) | copy-start | bytes 6148
  13.6 0.7 %copy-start.6 = (s32[64,4]{0,1:T(4,128)S(1)}, s32[64,4]{0,1:T(4,128)}, u32[]{:S(2)}) copy-start(s32[64,4]{0,1:T(4,128)} %param.13) | copy-start | bytes 3076
  14.3 8.5 %copy-start = (bf16[128,128]{1,0:T(8,128)(2,1)S(1)}, bf16[128,128]{1,0:T(8,128)(2,1)}, u32[]{:S(2)}) copy-start(bf16[128,128]{1,0:T(8,128)(2,1)} %constant.21.clone.flip) | copy-start | bytes 98308
  24.5 10.1 %collective-permute-start.1 = (f32[8,2176]{1,0:T(8,128)S(1)}, f32[8,2176]{1,0:T(8,128)S(1)}, u32[]{:S(2)}, u32[]{:S(2)}) collective-permute-start(f32[8,2176]{1,0:T(8,128)S(1)} %get-tuple-element.43), channel_id=1, source_target_pairs={{0,8},{8,16},{16,24},{24,0},{1,9},{9,17},{17,25},{25,1},{2,10},{10... | collective-permute-start | bytes 208904 | tf_op jit(solution)/shard_map/ppermute | solution.py:453
  25.8 8.8 %collective-permute-start.2 = (f32[8,2176]{1,0:T(8,128)S(1)}, f32[8,2176]{1,0:T(8,128)S(1)}, u32[]{:S(2)}, u32[]{:S(2)}) collective-permute-start(f32[8,2176]{1,0:T(8,128)S(1)} %get-tuple-element.44), channel_id=1, source_target_pairs={{0,16},{8,24},{16,0},{24,8},{1,17},{9,25},{17,1},{25,9},{2,18},{10... | collective-permute-start | bytes 208904 | tf_op jit(solution)/shard_map/ppermute | solution.py:453
  28.2 6.4 %collective-permute-start.3 = (f32[8,2176]{1,0:T(8,128)S(1)}, f32[8,2176]{1,0:T(8,128)S(1)}, u32[]{:S(2)}, u32[]{:S(2)}) collective-permute-start(f32[8,2176]{1,0:T(8,128)S(1)} %get-tuple-element.45), channel_id=1, source_target_pairs={{0,24},{8,0},{16,8},{24,16},{1,25},{9,1},{17,9},{25,17},{2,26},{10... | collective-permute-start | bytes 208904 | tf_op jit(solution)/shard_map/ppermute | solution.py:453
  29.4 5.9 %collective-permute-start = (f32[8,2176]{1,0:T(8,128)S(1)}, f32[8,2176]{1,0:T(8,128)S(1)}, u32[]{:S(2)}, u32[]{:S(2)}) collective-permute-start(f32[8,2176]{1,0:T(8,128)S(1)} %get-tuple-element.42), channel_id=1, source_target_pairs={{0,4},{4,0},{1,5},{5,1},{2,6},{6,2},{3,7},{7,3},{8,12},{12,8},{9,1... | collective-permute-start | bytes 208904 | tf_op jit(solution)/shard_map/ppermute | solution.py:461
  34.6 1.6 %collective-permute-start.4 = (f32[8,2176]{1,0:T(8,128)S(1)}, f32[8,2176]{1,0:T(8,128)S(1)}, u32[]{:S(2)}, u32[]{:S(2)}) collective-permute-start(f32[8,2176]{1,0:T(8,128)S(1)} %add_add_fusion.own_sum), channel_id=1, source_target_pairs={{0,4},{4,0},{1,5},{5,1},{2,6},{6,2},{3,7},{7,3},{8,12},{12,8},{9,1... | collective-permute-start | bytes 208904 | tf_op jit(solution)/shard_map/ppermute | solution.py:462

commit v7 on v6

--- a/solution.py
+++ b/solution.py
@@ -190,53 +190,65 @@
     own_core, other_core, next1, next2, next3, turned, lhs, total,
 ):
     zi, xc = place[0], place[1]
-    turned[0:512, :] = dot(jnp.concatenate(halves(x[...]), axis=0), flip[...])
-    for half in range(2):
-        for q in range(8):
-            rows = [
-                turned[pl.ds(256 * h + 128 * half + 7 - q, 16, stride=8), :].astype(BF16)
+    shard_of = lax.broadcasted_iota(jnp.int32, (8, 256), 0) >> 2
+    upper = lax.broadcasted_iota(jnp.int32, (8, 256), 0) < 4
+    x_at, core = xc >> 1, xc & 1
+
+    def over_shards(v):
+        return v + pltpu.roll(v, 4, 0)
+
+    def arrange(group):
+        base = 128 * group
+        rows = x[64 * group : 64 * group + 64, :]
+        turned[base : base + 128, :] = dot(jnp.concatenate(halves(rows), axis=0), flip[...])
+        for pair in range(4):
+            columns = [
+                jnp.concatenate(
+                    [
+                        turned[pl.ds(base + 64 * h + 7 - q, 8, stride=8), :]
+                        for q in (2 * pair, 2 * pair + 1)
+                    ],
+                    axis=0,
+                ).astype(BF16)
                 for h in (0, 1, 0)
             ]
-            at = 128 * half + 16 * q
-            lhs[at : at + 16, :] = jnp.concatenate(rows, axis=1)
-    shard_of = lax.broadcasted_iota(jnp.int32, (16, 256), 0) >> 2
-    upper = lax.broadcasted_iota(jnp.int32, (8, 256), 0) < 4
-    x_at, core = xc >> 1, xc & 1
-
-    def over_shards(v):
-        total = v[0:8] + v[8:16]
-        return total + pltpu.roll(total, 4, 0)
-
-    def of_half(half, lanes):
+            at = 64 * group + 16 * pair
+            lhs[at : at + 16, :] = jnp.concatenate(columns, axis=1)
+
+    def of_group(group, lanes):
         e_re, e_im = (
             dot(
-                lhs[128 * half : 128 * half + 128, :],
+                lhs[64 * group : 64 * group + 64, :],
                 jnp.concatenate([head[:, lanes], head[:, lanes], tail[:, lanes]], axis=0),
             )
             for head, tail in ((pr_head, pr_tail), (pi_head, pi_tail))
         )
         step_re = row_re[ROW_128 : ROW_128 + 1, lanes]
         step_im = row_im[ROW_128 : ROW_128 + 1, lanes]
-        s_re, s_im = e_re[112:128], e_im[112:128]
+        s_re, s_im = e_re[56:64], e_im[56:64]
         for q in range(6, -1, -1):
             s_re, s_im = cmul(s_re, s_im, step_re, step_im)
-            s_re = s_re + e_re[16 * q : 16 * q + 16]
-            s_im = s_im + e_im[16 * q : 16 * q + 16]
-        rows = slice(16 * half, 16 * half + 16)
+            s_re = s_re + e_re[8 * q : 8 * q + 8]
+            s_im = s_im + e_im[8 * q : 8 * q + 8]
+        rows = slice(8 * group, 8 * group + 8)
         weighted = cmul(s_re, s_im, wr[rows, lanes], wi[rows, lanes])
-        own = [jnp.where(shard_of == zi - 4 * half, v, 0.0) for v in (s_re, s_im)]
+        own = [jnp.where(shard_of == zi - 2 * group, v, 0.0) for v in (s_re, s_im)]
         return [over_shards(v) for v in (*weighted, *own)]
 
     parts = [slice(256 * part, 256 * part + 256) for part in range(WIDE // 256)]
+    arrange(0)
     for lanes in parts:
-        for k, v in enumerate(of_half(0, lanes)):
+        for k, v in enumerate(of_group(0, lanes)):
             total[k, :, lanes] = v
 
-    @pl.when(zi >= 4)
-    def _():
-        for lanes in parts:
-            for k, v in enumerate(of_half(1, lanes)):
-                total[k, :, lanes] = total[k, :, lanes] + v
+    for group in range(1, 4):
+
+        @pl.when(zi >= 2 * group)
+        def _(group=group):
+            arrange(group)
+            for lanes in parts:
+                for k, v in enumerate(of_group(group, lanes)):
+                    total[k, :, lanes] = total[k, :, lanes] + v
 
     for lanes in parts:
         b_re, b_im, o_re, o_im = (total[k, :, lanes] for k in range(4))

time: 41.5 us -> 41.4 us (level)
  no operation moved by 1% of the time
where the time goes in v7:
time: 41.4 us; the launch traced here: 41.1 us
  starting transfers between devices  20.6 us (50%)
  Pallas kernels  13.1 us (32%)
  waiting for transfers between devices  5.21 us (13%)
  local copies, waits for them, and re-layouts  2.05 us (5%)
    all_to_all x1, starting transfers between devices, shards(): lax.all_to_all(sent, ('z', 'det'), 0, 0, tiled=True).reshape(256, 128)  12.2 us
    pallas_call x1, Pallas kernels, to_peak(): return call(peak_kernel, 3, 14, [((8, 1024), F32)], scratch)(*args)[0]  5.06 us
    ppermute x3, starting transfers between devices, shards(): lax.ppermute(v, 'x', [(x, (x + k) % 4) for x in range(4)])  4.89 us
    all_to_all x1, waiting for transfers between devices, shards(): lax.all_to_all(sent, ('z', 'det'), 0, 0, tiled=True).reshape(256, 128)  4.29 us
    pallas_call x1, Pallas kernels, prepare(): return call(prepare_kernel, 1, 6, PREPARED, [((4, 16, 128), F32)])(*args)  4.25 us
    ppermute x1, starting transfers between devices, shards(): lax.ppermute(other_core, 'core', swap)  2.9 us
    pallas_call x1, Pallas kernels, of_device(): return call(local_kernel, 1, 11, [((8, 2, 40, 128), F32)], [])(*args)[0]  2.26 us
    pallas_call x1, Pallas kernels, of_column(): return call(column_kernel, 1, 12, [STATE] * 5, scratch)(*args)  1.5 us
  transfers between devices with their start and end apart: 6, of which 2 were waited for; matrix products, arithmetic and copies ran while one was open for 0% of the time, Pallas kernels for 16%

profile of v7, /device:TPU:1, one launch (start us, length us, event | category | flops | bytes accessed | tf_op | source)
XLA Modules:
  0.0 41.1 jit_solution(3322466868007664417)
XLA Ops:
  0.0 1.4 %broadcast_in_dim.8 = f32[32,8,128]{2,1,0:T(8,128)} broadcast(f32[8,128]{1,0:T(8,128)} %bitcast.19), dimensions={1,2} | broadcast | bytes 135168 | tf_op jit(solution)/shard_map/broadcast_in_dim | solution.py:452
  1.4 0.0 copy-start.1
  1.4 0.0 copy-start.3
  1.4 0.0 copy-start.4
  1.4 12.2 %all-to-all-start = ((f32[32,8,128]{2,1,0:T(8,128)}), f32[32,8,128]{2,1,0:T(8,128)S(1)}, u32[]{:S(2)}, u32[]{:S(2)}) async-start(f32[32,8,128]{2,1,0:T(8,128)} %broadcast_in_dim.8), calls=%async_computation | async-start | bytes 262144 | tf_op jit(solution)/shard_map/all_to_all | solution.py:453
  13.5 0.0 copy-start.2
  13.6 0.1 pad_add_fusion.place
  13.6 0.0 copy-start.5
  13.6 0.0 copy-start.6
  13.6 0.0 copy-done.1
  13.6 0.0 copy-done.3
  13.6 0.0 copy-done.4
  13.7 0.6 %copy-done.2 = f32[8192]{0:T(1024)S(1)} copy-done((f32[8192]{0:T(1024)S(1)}, f32[8192]{0:T(1024)}, u32[]{:S(2)}) %copy-start.2) | copy-done | bytes 32792
  14.3 0.0 copy-done.5
  14.3 0.0 copy-done.6
  14.3 0.0 copy-start
  14.3 4.3 %shard_map.82 = (bf16[128,2048]{1,0:T(8,128)(2,1)S(1)}, bf16[128,2048]{1,0:T(8,128)(2,1)S(1)}, bf16[128,2048]{1,0:T(8,128)(2,1)S(1)}, bf16[128,2048]{1,0:T(8,128...) custom-call(s32[3]{0:T(128)S(1)} %pad_add_fusion.place, ...), custom_call_target="tpu_custom_call" | custom-call | tf_op jit(solution)/shard_map/pallas_call | solution.py:434
  18.6 4.3 %all-to-all-done = f32[32,8,128]{2,1,0:T(8,128)S(1)} async-done(((f32[32,8,128]{2,1,0:T(8,128)}), f32[32,8,128]{2,1,0:T(8,128)S(1)}, u32[]{:S(2)}, u32[]{:S(2)}) %all-to-all-start) | async-done | bytes 131104 | tf_op jit(solution)/shard_map/all_to_all | solution.py:453
  22.9 0.0 copy-done
  22.9 1.5 %shard_map.83 = (f32[8,2176]{1,0:T(8,128)S(1)}, f32[8,2176]{1,0:T(8,128)S(1)}, f32[8,2176]{1,0:T(8,128)S(1)}, f32[8,2176]{1,0:T(8,128)S(1)}, f32[8,2176]{1,0:T(8,128)S(1)}) custom-call(s32[3]{0:T(128)S(1)} %pad_add_fusion.place, f32[256,128]{1,0:T(8,128)S(1)} %bitcast.12, bf16[128,128]{1,0:T(8,128)(2,1)S(1)} %copy-done, ...), custom_call_target="tpu_custom_call" | custom-call | tf_op jit(solution)/shard_map/pallas_call | solution.py:439
  24.4 1.3 %collective-permute-start.1 = (f32[8,2176]{1,0:T(8,128)S(1)}, f32[8,2176]{1,0:T(8,128)S(1)}, u32[]{:S(2)}, u32[]{:S(2)}) collective-permute-start(f32[8,2176]{1,0:T(8,128)S(1)} %get-tuple-element.43), channel_id=1, source_target_pairs={{0,8},{8,16},{16,24},{24,0},{1,9},{9,17},{17,25},{25,1},{2,10},{10... | collective-permute-start | bytes 208904 | tf_op jit(solution)/shard_map/ppermute | solution.py:465
  25.7 2.5 %collective-permute-start.2 = (f32[8,2176]{1,0:T(8,128)S(1)}, f32[8,2176]{1,0:T(8,128)S(1)}, u32[]{:S(2)}, u32[]{:S(2)}) collective-permute-start(f32[8,2176]{1,0:T(8,128)S(1)} %get-tuple-element.44), channel_id=1, source_target_pairs={{0,16},{8,24},{16,0},{24,8},{1,17},{9,25},{17,1},{25,9},{2,18},{10... | collective-permute-start | bytes 208904 | tf_op jit(solution)/shard_map/ppermute | solution.py:465
  28.1 1.1 %collective-permute-start.3 = (f32[8,2176]{1,0:T(8,128)S(1)}, f32[8,2176]{1,0:T(8,128)S(1)}, u32[]{:S(2)}, u32[]{:S(2)}) collective-permute-start(f32[8,2176]{1,0:T(8,128)S(1)} %get-tuple-element.45), channel_id=1, source_target_pairs={{0,24},{8,0},{16,8},{24,16},{1,25},{9,1},{17,9},{25,17},{2,26},{10... | collective-permute-start | bytes 208904 | tf_op jit(solution)/shard_map/ppermute | solution.py:465
  29.3 2.9 %collective-permute-start = (f32[8,2176]{1,0:T(8,128)S(1)}, f32[8,2176]{1,0:T(8,128)S(1)}, u32[]{:S(2)}, u32[]{:S(2)}) collective-permute-start(f32[8,2176]{1,0:T(8,128)S(1)} %get-tuple-element.42), channel_id=1, source_target_pairs={{0,4},{4,0},{1,5},{5,1},{2,6},{6,2},{3,7},{7,3},{8,12},{12,8},{9,1... | collective-permute-start | bytes 208904 | tf_op jit(solution)/shard_map/ppermute | solution.py:473
  32.2 2.3 %shard_map.84.local = f32[8,2,40,128]{3,2,1,0:T(8,128)S(1)} custom-call(s32[3]{0:T(128)S(1)} %pad_add_fusion.place, f32[256,128]{1,0:T(8,128)S(1)} %bitcast.13, bf16[128,128]{1,0:T(8,128)(2,1)S(1)} %copy-done, bf16[128,2048]{1,0:T(8,128)(2,1)S(1)} %get-tuple-element.31.pr_head, bf16[128,2048]{1,0:T(8,128)(2,1)S(1)} %get-tuple-element.32.pr_tail, ...), custom_call_target="tpu_custom_call" | custom-call | tf_op jit(solution)/shard_map/pallas_call | solution.py:443
  34.5 0.0 collective-permute-done.1
  34.5 0.0 collective-permute-done.2
  34.5 0.0 collective-permute-done.3
  34.5 0.7 %collective-permute-start.4 = (f32[8,2176]{1,0:T(8,128)S(1)}, f32[8,2176]{1,0:T(8,128)S(1)}, u32[]{:S(2)}, u32[]{:S(2)}) collective-permute-start(f32[8,2176]{1,0:T(8,128)S(1)} %add_add_fusion.own_sum), channel_id=1, source_target_pairs={{0,4},{4,0},{1,5},{5,1},{2,6},{6,2},{3,7},{7,3},{8,12},{12,8},{9,1... | collective-permute-start | bytes 208904 | tf_op jit(solution)/shard_map/ppermute | solution.py:474
  35.2 0.0 collective-permute-done.other_core
  35.2 0.9 %collective-permute-done.4.other_sum = f32[8,2176]{1,0:T(8,128)S(1)} collective-permute-done((f32[8,2176]{1,0:T(8,128)S(1)}, f32[8,2176]{1,0:T(8,128)S(1)}, u32[]{:S(2)}, u32[]{:S(2)}) %collective-permute-start.4) | collective-permute-done | bytes 69664 | tf_op jit(solution)/shard_map/ppermute | solution.py:474
  36.1 5.1 %shard_map.85 = f32[8,1024]{1,0:T(8,128)} custom-call(s32[3]{0:T(128)S(1)} %pad_add_fusion.place, s32[4,64]{1,0:T(4,128)S(1)} %get-tuple-element.29.delay, f32[8,64]{1,0:T(8,128)S(1)} %get-tuple-element.30.antenna, f32[8,2176]{1,0:T(8,128)S(1)} %get-tuple-element.41.own_core, f32[8,2176]{1,0:T(8,128)S(1)} %collective-permute-done.other_core, ...), custom_call_target="tpu_custom_call" | custom-call | tf_op jit(solution)/shard_map/pallas_call | solution.py:448
  (1 shorter events, 0.0 us)
Async XLA Ops:
  1.4 12.3 %copy-start.1 = (f32[2,8192]{1,0:T(2,128)S(1)}, f32[2,8192]{1,0:T(2,128)}, u32[]{:S(2)}) copy-start(f32[2,8192]{1,0:T(2,128)} %gain.1) | copy-start | bytes 196612
  1.4 12.3 %copy-start.3 = (f32[8192]{0:T(1024)S(1)}, f32[8192]{0:T(1024)}, u32[]{:S(2)}) copy-start(f32[8192]{0:T(1024)} %param.10) | copy-start | bytes 98308
  1.4 12.3 %copy-start.4 = (s32[8192]{0:T(1024)S(1)}, s32[8192]{0:T(1024)}, u32[]{:S(2)}) copy-start(s32[8192]{0:T(1024)} %param.12) | copy-start | bytes 98308
  1.4 21.5 %all-to-all-start = ((f32[32,8,128]{2,1,0:T(8,128)}), f32[32,8,128]{2,1,0:T(8,128)S(1)}, u32[]{:S(2)}, u32[]{:S(2)}) async-start(f32[32,8,128]{2,1,0:T(8,128)} %broadcast_in_dim.8), calls=%async_computation | async-start | bytes 262144 | tf_op jit(solution)/shard_map/all_to_all | solution.py:453
  13.5 0.8 %copy-start.2 = (f32[8192]{0:T(1024)S(1)}, f32[8192]{0:T(1024)}, u32[]{:S(2)}) copy-start(f32[8192]{0:T(1024)} %param.9) | copy-start | bytes 98308
  13.6 0.7 %copy-start.5 = (f32[64,2,4]{0,2,1:T(4,128)S(1)}, f32[64,2,4]{0,2,1:T(4,128)}, u32[]{:S(2)}) copy-start(f32[64,2,4]{0,2,1:T(4,128)} %param.14) | copy-start | bytes 6148
  13.6 0.7 %copy-start.6 = (s32[64,4]{0,1:T(4,128)S(1)}, s32[64,4]{0,1:T(4,128)}, u32[]{:S(2)}) copy-start(s32[64,4]{0,1:T(4,128)} %param.13) | copy-start | bytes 3076
  14.3 8.5 %copy-start = (bf16[128,128]{1,0:T(8,128)(2,1)S(1)}, bf16[128,128]{1,0:T(8,128)(2,1)}, u32[]{:S(2)}) copy-start(bf16[128,128]{1,0:T(8,128)(2,1)} %constant.21.clone.flip) | copy-start | bytes 98308
  24.4 10.1 %collective-permute-start.1 = (f32[8,2176]{1,0:T(8,128)S(1)}, f32[8,2176]{1,0:T(8,128)S(1)}, u32[]{:S(2)}, u32[]{:S(2)}) collective-permute-start(f32[8,2176]{1,0:T(8,128)S(1)} %get-tuple-element.43), channel_id=1, source_target_pairs={{0,8},{8,16},{16,24},{24,0},{1,9},{9,17},{17,25},{25,1},{2,10},{10... | collective-permute-start | bytes 208904 | tf_op jit(solution)/shard_map/ppermute | solution.py:465
  25.7 8.8 %collective-permute-start.2 = (f32[8,2176]{1,0:T(8,128)S(1)}, f32[8,2176]{1,0:T(8,128)S(1)}, u32[]{:S(2)}, u32[]{:S(2)}) collective-permute-start(f32[8,2176]{1,0:T(8,128)S(1)} %get-tuple-element.44), channel_id=1, source_target_pairs={{0,16},{8,24},{16,0},{24,8},{1,17},{9,25},{17,1},{25,9},{2,18},{10... | collective-permute-start | bytes 208904 | tf_op jit(solution)/shard_map/ppermute | solution.py:465
  28.1 6.3 %collective-permute-start.3 = (f32[8,2176]{1,0:T(8,128)S(1)}, f32[8,2176]{1,0:T(8,128)S(1)}, u32[]{:S(2)}, u32[]{:S(2)}) collective-permute-start(f32[8,2176]{1,0:T(8,128)S(1)} %get-tuple-element.45), channel_id=1, source_target_pairs={{0,24},{8,0},{16,8},{24,16},{1,25},{9,1},{17,9},{25,17},{2,26},{10... | collective-permute-start | bytes 208904 | tf_op jit(solution)/shard_map/ppermute | solution.py:465
  29.3 5.9 %collective-permute-start = (f32[8,2176]{1,0:T(8,128)S(1)}, f32[8,2176]{1,0:T(8,128)S(1)}, u32[]{:S(2)}, u32[]{:S(2)}) collective-permute-start(f32[8,2176]{1,0:T(8,128)S(1)} %get-tuple-element.42), channel_id=1, source_target_pairs={{0,4},{4,0},{1,5},{5,1},{2,6},{6,2},{3,7},{7,3},{8,12},{12,8},{9,1... | collective-permute-start | bytes 208904 | tf_op jit(solution)/shard_map/ppermute | solution.py:473
  34.5 1.6 %collective-permute-start.4 = (f32[8,2176]{1,0:T(8,128)S(1)}, f32[8,2176]{1,0:T(8,128)S(1)}, u32[]{:S(2)}, u32[]{:S(2)}) collective-permute-start(f32[8,2176]{1,0:T(8,128)S(1)} %add_add_fusion.own_sum), channel_id=1, source_target_pairs={{0,4},{4,0},{1,5},{5,1},{2,6},{6,2},{3,7},{7,3},{8,12},{12,8},{9,1... | collective-permute-start | bytes 208904 | tf_op jit(solution)/shard_map/ppermute | solution.py:474

commit v8 on v7

--- a/solution.py
+++ b/solution.py
@@ -190,49 +190,55 @@
     own_core, other_core, next1, next2, next3, turned, lhs, total,
 ):
     zi, xc = place[0], place[1]
-    shard_of = lax.broadcasted_iota(jnp.int32, (8, 256), 0) >> 2
+    sizes, starts = (8, 24), (0, 8)
     upper = lax.broadcasted_iota(jnp.int32, (8, 256), 0) < 4
     x_at, core = xc >> 1, xc & 1
 
+    def shard_of(size):
+        return lax.broadcasted_iota(jnp.int32, (size, 256), 0) >> 2
+
     def over_shards(v):
+        v = sum(v[at : at + 8] for at in range(0, v.shape[0], 8))
         return v + pltpu.roll(v, 4, 0)
 
     def arrange(group):
-        base = 128 * group
-        rows = x[64 * group : 64 * group + 64, :]
-        turned[base : base + 128, :] = dot(jnp.concatenate(halves(rows), axis=0), flip[...])
+        size, start = sizes[group], starts[group]
+        base = 16 * start
+        rows = x[8 * start : 8 * (start + size), :]
+        turned[base : base + 16 * size, :] = dot(jnp.concatenate(halves(rows), axis=0), flip[...])
         for pair in range(4):
             columns = [
                 jnp.concatenate(
                     [
-                        turned[pl.ds(base + 64 * h + 7 - q, 8, stride=8), :]
+                        turned[pl.ds(base + 8 * size * h + 7 - q, size, stride=8), :]
                         for q in (2 * pair, 2 * pair + 1)
                     ],
                     axis=0,
                 ).astype(BF16)
                 for h in (0, 1, 0)
             ]
-            at = 64 * group + 16 * pair
-            lhs[at : at + 16, :] = jnp.concatenate(columns, axis=1)
+            at = 8 * start + 2 * size * pair
+            lhs[at : at + 2 * size, :] = jnp.concatenate(columns, axis=1)
 
     def of_group(group, lanes):
+        size, start = sizes[group], starts[group]
         e_re, e_im = (
             dot(
-                lhs[64 * group : 64 * group + 64, :],
+                lhs[8 * start : 8 * (start + size), :],
                 jnp.concatenate([head[:, lanes], head[:, lanes], tail[:, lanes]], axis=0),
             )
             for head, tail in ((pr_head, pr_tail), (pi_head, pi_tail))
         )
         step_re = row_re[ROW_128 : ROW_128 + 1, lanes]
         step_im = row_im[ROW_128 : ROW_128 + 1, lanes]
-        s_re, s_im = e_re[56:64], e_im[56:64]
+        s_re, s_im = e_re[7 * size :], e_im[7 * size :]
         for q in range(6, -1, -1):
             s_re, s_im = cmul(s_re, s_im, step_re, step_im)
-            s_re = s_re + e_re[8 * q : 8 * q + 8]
-            s_im = s_im + e_im[8 * q : 8 * q + 8]
-        rows = slice(8 * group, 8 * group + 8)
+            s_re = s_re + e_re[size * q : size * q + size]
+            s_im = s_im + e_im[size * q : size * q + size]
+        rows = slice(start, start + size)
         weighted = cmul(s_re, s_im, wr[rows, lanes], wi[rows, lanes])
-        own = [jnp.where(shard_of == zi - 2 * group, v, 0.0) for v in (s_re, s_im)]
+        own = [jnp.where(shard_of(size) == zi - start // 4, v, 0.0) for v in (s_re, s_im)]
         return [over_shards(v) for v in (*weighted, *own)]
 
     parts = [slice(256 * part, 256 * part + 256) for part in range(WIDE // 256)]
@@ -241,14 +247,12 @@
         for k, v in enumerate(of_group(0, lanes)):
             total[k, :, lanes] = v
 
-    for group in range(1, 4):
-
-        @pl.when(zi >= 2 * group)
-        def _(group=group):
-            arrange(group)
-            for lanes in parts:
-                for k, v in enumerate(of_group(group, lanes)):
-                    total[k, :, lanes] = total[k, :, lanes] + v
+    @pl.when(zi >= 2)
+    def _():
+        arrange(1)
+        for lanes in parts:
+            for k, v in enumerate(of_group(1, lanes)):
+                total[k, :, lanes] = total[k, :, lanes] + v
 
     for lanes in parts:
         b_re, b_im, o_re, o_im = (total[k, :, lanes] for k in range(4))

time: 41.4 us -> 41.4 us (level)
  no operation moved by 1% of the time
where the time goes in v8:
time: 41.4 us; the launch traced here: 41.1 us
  starting transfers between devices  20.6 us (50%)
  Pallas kernels  13.1 us (32%)
  waiting for transfers between devices  5.21 us (13%)
  local copies, waits for them, and re-layouts  2.05 us (5%)
    all_to_all x1, starting transfers between devices, shards(): lax.all_to_all(sent, ('z', 'det'), 0, 0, tiled=True).reshape(256, 128)  12.2 us
    pallas_call x1, Pallas kernels, to_peak(): return call(peak_kernel, 3, 14, [((8, 1024), F32)], scratch)(*args)[0]  5.07 us
    ppermute x3, starting transfers between devices, shards(): lax.ppermute(v, 'x', [(x, (x + k) % 4) for x in range(4)])  4.89 us
    all_to_all x1, waiting for transfers between devices, shards(): lax.all_to_all(sent, ('z', 'det'), 0, 0, tiled=True).reshape(256, 128)  4.29 us
    pallas_call x1, Pallas kernels, prepare(): return call(prepare_kernel, 1, 6, PREPARED, [((4, 16, 128), F32)])(*args)  4.25 us
    ppermute x1, starting transfers between devices, shards(): lax.ppermute(other_core, 'core', swap)  2.9 us
    pallas_call x1, Pallas kernels, of_device(): return call(local_kernel, 1, 11, [((8, 2, 40, 128), F32)], [])(*args)[0]  2.26 us
    pallas_call x1, Pallas kernels, of_column(): return call(column_kernel, 1, 12, [STATE] * 5, scratch)(*args)  1.49 us
  transfers between devices with their start and end apart: 6, of which 2 were waited for; matrix products, arithmetic and copies ran while one was open for 0% of the time, Pallas kernels for 16%

profile of v8, /device:TPU:1, one launch (start us, length us, event | category | flops | bytes accessed | tf_op | source)
XLA Modules:
  0.0 41.1 jit_solution(15538723356508021755)
XLA Ops:
  0.0 1.4 %broadcast_in_dim.8 = f32[32,8,128]{2,1,0:T(8,128)} broadcast(f32[8,128]{1,0:T(8,128)} %bitcast.19), dimensions={1,2} | broadcast | bytes 135168 | tf_op jit(solution)/shard_map/broadcast_in_dim | solution.py:456
  1.4 0.0 copy-start.1
  1.4 0.0 copy-start.3
  1.4 0.0 copy-start.4
  1.4 12.2 %all-to-all-start = ((f32[32,8,128]{2,1,0:T(8,128)}), f32[32,8,128]{2,1,0:T(8,128)S(1)}, u32[]{:S(2)}, u32[]{:S(2)}) async-start(f32[32,8,128]{2,1,0:T(8,128)} %broadcast_in_dim.8), calls=%async_computation | async-start | bytes 262144 | tf_op jit(solution)/shard_map/all_to_all | solution.py:457
  13.5 0.0 copy-start.2
  13.6 0.1 pad_add_fusion.place
  13.6 0.0 copy-start.5
  13.6 0.0 copy-start.6
  13.6 0.0 copy-done.1
  13.6 0.0 copy-done.3
  13.6 0.0 copy-done.4
  13.7 0.6 %copy-done.2 = f32[8192]{0:T(1024)S(1)} copy-done((f32[8192]{0:T(1024)S(1)}, f32[8192]{0:T(1024)}, u32[]{:S(2)}) %copy-start.2) | copy-done | bytes 32792
  14.3 0.0 copy-done.5
  14.3 0.0 copy-done.6
  14.3 0.0 copy-start
  14.3 4.3 %shard_map.82 = (bf16[128,2048]{1,0:T(8,128)(2,1)S(1)}, bf16[128,2048]{1,0:T(8,128)(2,1)S(1)}, bf16[128,2048]{1,0:T(8,128)(2,1)S(1)}, bf16[128,2048]{1,0:T(8,128...) custom-call(s32[3]{0:T(128)S(1)} %pad_add_fusion.place, ...), custom_call_target="tpu_custom_call" | custom-call | tf_op jit(solution)/shard_map/pallas_call | solution.py:438
  18.6 4.3 %all-to-all-done = f32[32,8,128]{2,1,0:T(8,128)S(1)} async-done(((f32[32,8,128]{2,1,0:T(8,128)}), f32[32,8,128]{2,1,0:T(8,128)S(1)}, u32[]{:S(2)}, u32[]{:S(2)}) %all-to-all-start) | async-done | bytes 131104 | tf_op jit(solution)/shard_map/all_to_all | solution.py:457
  22.9 0.0 copy-done
  22.9 1.5 %shard_map.83 = (f32[8,2176]{1,0:T(8,128)S(1)}, f32[8,2176]{1,0:T(8,128)S(1)}, f32[8,2176]{1,0:T(8,128)S(1)}, f32[8,2176]{1,0:T(8,128)S(1)}, f32[8,2176]{1,0:T(8,128)S(1)}) custom-call(s32[3]{0:T(128)S(1)} %pad_add_fusion.place, f32[256,128]{1,0:T(8,128)S(1)} %bitcast.12, bf16[128,128]{1,0:T(8,128)(2,1)S(1)} %copy-done, ...), custom_call_target="tpu_custom_call" | custom-call | tf_op jit(solution)/shard_map/pallas_call | solution.py:443
  24.4 1.3 %collective-permute-start.1 = (f32[8,2176]{1,0:T(8,128)S(1)}, f32[8,2176]{1,0:T(8,128)S(1)}, u32[]{:S(2)}, u32[]{:S(2)}) collective-permute-start(f32[8,2176]{1,0:T(8,128)S(1)} %get-tuple-element.43), channel_id=1, source_target_pairs={{0,8},{8,16},{16,24},{24,0},{1,9},{9,17},{17,25},{25,1},{2,10},{10... | collective-permute-start | bytes 208904 | tf_op jit(solution)/shard_map/ppermute | solution.py:469
  25.7 2.5 %collective-permute-start.2 = (f32[8,2176]{1,0:T(8,128)S(1)}, f32[8,2176]{1,0:T(8,128)S(1)}, u32[]{:S(2)}, u32[]{:S(2)}) collective-permute-start(f32[8,2176]{1,0:T(8,128)S(1)} %get-tuple-element.44), channel_id=1, source_target_pairs={{0,16},{8,24},{16,0},{24,8},{1,17},{9,25},{17,1},{25,9},{2,18},{10... | collective-permute-start | bytes 208904 | tf_op jit(solution)/shard_map/ppermute | solution.py:469
  28.1 1.1 %collective-permute-start.3 = (f32[8,2176]{1,0:T(8,128)S(1)}, f32[8,2176]{1,0:T(8,128)S(1)}, u32[]{:S(2)}, u32[]{:S(2)}) collective-permute-start(f32[8,2176]{1,0:T(8,128)S(1)} %get-tuple-element.45), channel_id=1, source_target_pairs={{0,24},{8,0},{16,8},{24,16},{1,25},{9,1},{17,9},{25,17},{2,26},{10... | collective-permute-start | bytes 208904 | tf_op jit(solution)/shard_map/ppermute | solution.py:469
  29.3 2.9 %collective-permute-start = (f32[8,2176]{1,0:T(8,128)S(1)}, f32[8,2176]{1,0:T(8,128)S(1)}, u32[]{:S(2)}, u32[]{:S(2)}) collective-permute-start(f32[8,2176]{1,0:T(8,128)S(1)} %get-tuple-element.42), channel_id=1, source_target_pairs={{0,4},{4,0},{1,5},{5,1},{2,6},{6,2},{3,7},{7,3},{8,12},{12,8},{9,1... | collective-permute-start | bytes 208904 | tf_op jit(solution)/shard_map/ppermute | solution.py:477
  32.2 2.3 %shard_map.84.local = f32[8,2,40,128]{3,2,1,0:T(8,128)S(1)} custom-call(s32[3]{0:T(128)S(1)} %pad_add_fusion.place, f32[256,128]{1,0:T(8,128)S(1)} %bitcast.13, bf16[128,128]{1,0:T(8,128)(2,1)S(1)} %copy-done, bf16[128,2048]{1,0:T(8,128)(2,1)S(1)} %get-tuple-element.31.pr_head, bf16[128,2048]{1,0:T(8,128)(2,1)S(1)} %get-tuple-element.32.pr_tail, ...), custom_call_target="tpu_custom_call" | custom-call | tf_op jit(solution)/shard_map/pallas_call | solution.py:447
  34.4 0.0 collective-permute-done.1
  34.5 0.0 collective-permute-done.2
  34.5 0.0 collective-permute-done.3
  34.5 0.7 %collective-permute-start.4 = (f32[8,2176]{1,0:T(8,128)S(1)}, f32[8,2176]{1,0:T(8,128)S(1)}, u32[]{:S(2)}, u32[]{:S(2)}) collective-permute-start(f32[8,2176]{1,0:T(8,128)S(1)} %add_add_fusion.own_sum), channel_id=1, source_target_pairs={{0,4},{4,0},{1,5},{5,1},{2,6},{6,2},{3,7},{7,3},{8,12},{12,8},{9,1... | collective-permute-start | bytes 208904 | tf_op jit(solution)/shard_map/ppermute | solution.py:478
  35.2 0.0 collective-permute-done.other_core
  35.2 0.9 %collective-permute-done.4.other_sum = f32[8,2176]{1,0:T(8,128)S(1)} collective-permute-done((f32[8,2176]{1,0:T(8,128)S(1)}, f32[8,2176]{1,0:T(8,128)S(1)}, u32[]{:S(2)}, u32[]{:S(2)}) %collective-permute-start.4) | collective-permute-done | bytes 69664 | tf_op jit(solution)/shard_map/ppermute | solution.py:478
  36.1 5.1 %shard_map.85 = f32[8,1024]{1,0:T(8,128)} custom-call(s32[3]{0:T(128)S(1)} %pad_add_fusion.place, s32[4,64]{1,0:T(4,128)S(1)} %get-tuple-element.29.delay, f32[8,64]{1,0:T(8,128)S(1)} %get-tuple-element.30.antenna, f32[8,2176]{1,0:T(8,128)S(1)} %get-tuple-element.41.own_core, f32[8,2176]{1,0:T(8,128)S(1)} %collective-permute-done.other_core, ...), custom_call_target="tpu_custom_call" | custom-call | tf_op jit(solution)/shard_map/pallas_call | solution.py:452
  (1 shorter events, 0.0 us)
Async XLA Ops:
  1.4 12.3 %copy-start.1 = (f32[2,8192]{1,0:T(2,128)S(1)}, f32[2,8192]{1,0:T(2,128)}, u32[]{:S(2)}) copy-start(f32[2,8192]{1,0:T(2,128)} %gain.1) | copy-start | bytes 196612
  1.4 12.3 %copy-start.3 = (f32[8192]{0:T(1024)S(1)}, f32[8192]{0:T(1024)}, u32[]{:S(2)}) copy-start(f32[8192]{0:T(1024)} %param.10) | copy-start | bytes 98308
  1.4 12.3 %copy-start.4 = (s32[8192]{0:T(1024)S(1)}, s32[8192]{0:T(1024)}, u32[]{:S(2)}) copy-start(s32[8192]{0:T(1024)} %param.12) | copy-start | bytes 98308
  1.4 21.5 %all-to-all-start = ((f32[32,8,128]{2,1,0:T(8,128)}), f32[32,8,128]{2,1,0:T(8,128)S(1)}, u32[]{:S(2)}, u32[]{:S(2)}) async-start(f32[32,8,128]{2,1,0:T(8,128)} %broadcast_in_dim.8), calls=%async_computation | async-start | bytes 262144 | tf_op jit(solution)/shard_map/all_to_all | solution.py:457
  13.5 0.8 %copy-start.2 = (f32[8192]{0:T(1024)S(1)}, f32[8192]{0:T(1024)}, u32[]{:S(2)}) copy-start(f32[8192]{0:T(1024)} %param.9) | copy-start | bytes 98308
  13.6 0.7 %copy-start.5 = (f32[64,2,4]{0,2,1:T(4,128)S(1)}, f32[64,2,4]{0,2,1:T(4,128)}, u32[]{:S(2)}) copy-start(f32[64,2,4]{0,2,1:T(4,128)} %param.14) | copy-start | bytes 6148
  13.6 0.7 %copy-start.6 = (s32[64,4]{0,1:T(4,128)S(1)}, s32[64,4]{0,1:T(4,128)}, u32[]{:S(2)}) copy-start(s32[64,4]{0,1:T(4,128)} %param.13) | copy-start | bytes 3076
  14.3 8.5 %copy-start = (bf16[128,128]{1,0:T(8,128)(2,1)S(1)}, bf16[128,128]{1,0:T(8,128)(2,1)}, u32[]{:S(2)}) copy-start(bf16[128,128]{1,0:T(8,128)(2,1)} %constant.21.clone.flip) | copy-start | bytes 98308
  24.4 10.1 %collective-permute-start.1 = (f32[8,2176]{1,0:T(8,128)S(1)}, f32[8,2176]{1,0:T(8,128)S(1)}, u32[]{:S(2)}, u32[]{:S(2)}) collective-permute-start(f32[8,2176]{1,0:T(8,128)S(1)} %get-tuple-element.43), channel_id=1, source_target_pairs={{0,8},{8,16},{16,24},{24,0},{1,9},{9,17},{17,25},{25,1},{2,10},{10... | collective-permute-start | bytes 208904 | tf_op jit(solution)/shard_map/ppermute | solution.py:469
  25.7 8.8 %collective-permute-start.2 = (f32[8,2176]{1,0:T(8,128)S(1)}, f32[8,2176]{1,0:T(8,128)S(1)}, u32[]{:S(2)}, u32[]{:S(2)}) collective-permute-start(f32[8,2176]{1,0:T(8,128)S(1)} %get-tuple-element.44), channel_id=1, source_target_pairs={{0,16},{8,24},{16,0},{24,8},{1,17},{9,25},{17,1},{25,9},{2,18},{10... | collective-permute-start | bytes 208904 | tf_op jit(solution)/shard_map/ppermute | solution.py:469
  28.1 6.3 %collective-permute-start.3 = (f32[8,2176]{1,0:T(8,128)S(1)}, f32[8,2176]{1,0:T(8,128)S(1)}, u32[]{:S(2)}, u32[]{:S(2)}) collective-permute-start(f32[8,2176]{1,0:T(8,128)S(1)} %get-tuple-element.45), channel_id=1, source_target_pairs={{0,24},{8,0},{16,8},{24,16},{1,25},{9,1},{17,9},{25,17},{2,26},{10... | collective-permute-start | bytes 208904 | tf_op jit(solution)/shard_map/ppermute | solution.py:469
  29.3 5.9 %collective-permute-start = (f32[8,2176]{1,0:T(8,128)S(1)}, f32[8,2176]{1,0:T(8,128)S(1)}, u32[]{:S(2)}, u32[]{:S(2)}) collective-permute-start(f32[8,2176]{1,0:T(8,128)S(1)} %get-tuple-element.42), channel_id=1, source_target_pairs={{0,4},{4,0},{1,5},{5,1},{2,6},{6,2},{3,7},{7,3},{8,12},{12,8},{9,1... | collective-permute-start | bytes 208904 | tf_op jit(solution)/shard_map/ppermute | solution.py:477
  34.5 1.6 %collective-permute-start.4 = (f32[8,2176]{1,0:T(8,128)S(1)}, f32[8,2176]{1,0:T(8,128)S(1)}, u32[]{:S(2)}, u32[]{:S(2)}) collective-permute-start(f32[8,2176]{1,0:T(8,128)S(1)} %add_add_fusion.own_sum), channel_id=1, source_target_pairs={{0,4},{4,0},{1,5},{5,1},{2,6},{6,2},{3,7},{7,3},{8,12},{12,8},{9,1... | collective-permute-start | bytes 208904 | tf_op jit(solution)/shard_map/ppermute | solution.py:478
